TPU v7x, 32 devices: a whole 2x2x4 slice. The times are simulated.
32 devices in a mesh: seq: 2 (over x), ctx: 16 (over z, y, core).
Axes of the slice: x: 2, y: 2, z: 4, core: 2. Of those that a mesh axis runs over, the one named last changes fastest.
Arguments:
- tokens: bfloat16 [4096, 4, 768], P('ctx', 'seq'), may hold values from -6 to 6
- segment: int32 [4096, 4], P('ctx', 'seq'), may hold values from 0 to 4095, as said below
- ln1_gain: bfloat16 [768], P(('seq', 'ctx')), may hold values from 0.099609375 to 1.8984375
- ln1_bias: bfloat16 [768], P(('seq', 'ctx')), may hold values from -3 to 3
- ln2_gain: bfloat16 [768], P(('seq', 'ctx')), may hold values from 0.099609375 to 1.8984375
- ln2_bias: bfloat16 [768], P(('seq', 'ctx')), may hold values from -3 to 3
- qkv_weight: bfloat16 [768, 2304], P(('seq', 'ctx')), may hold values from -0.21875 to 0.21875
- qkv_bias: bfloat16 [2304], P(('seq', 'ctx')), may hold values from -3 to 3
- dense_weight: bfloat16 [768, 768], P(('seq', 'ctx')), may hold values from -1.75 to 1.75
- dense_bias: bfloat16 [768], P(('seq', 'ctx')), may hold values from -3 to 3
- fc1_weight: bfloat16 [768, 3072], P(('seq', 'ctx')), may hold values from -0.21875 to 0.21875
- fc1_bias: bfloat16 [3072], P(('seq', 'ctx')), may hold values from -3 to 3
- output_feed_weight: bfloat16 [3072, 768], P(('seq', 'ctx')), may hold values from -0.109375 to 0.109375
- output_feed_bias: bfloat16 [768], P(('seq', 'ctx')), may hold values from -3 to 3
- cotangent: bfloat16 [4096, 4, 768], P('ctx', 'seq'), may hold values from -6 to 6
Outputs:
- output: bfloat16 [4096, 4, 768], P('ctx', 'seq')
- tokens_grad: bfloat16 [4096, 4, 768], P('ctx', 'seq')
- ln1_gain_grad: float32 [768], P(('seq', 'ctx'))
- ln1_bias_grad: float32 [768], P(('seq', 'ctx'))
- ln2_gain_grad: float32 [768], P(('seq', 'ctx'))
- ln2_bias_grad: float32 [768], P(('seq', 'ctx'))
- qkv_weight_grad: float32 [768, 2304], P(('seq', 'ctx'))
- qkv_bias_grad: float32 [2304], P(('seq', 'ctx'))
- dense_weight_grad: float32 [768, 768], P(('seq', 'ctx'))
- dense_bias_grad: float32 [768], P(('seq', 'ctx'))
- fc1_weight_grad: float32 [768, 3072], P(('seq', 'ctx'))
- fc1_bias_grad: float32 [3072], P(('seq', 'ctx'))
- fc2_weight_grad: float32 [3072, 768], P(('seq', 'ctx'))
- fc2_bias_grad: float32 [768], P(('seq', 'ctx'))
Inputs may be any that keep to these rules, and one draw needn't show every extreme that they name: segment[t, s] is the first position of the document holding token t of sequence s, so segment[t, s] <= t; it is the same for all tokens of one document and documents are contiguous; a sequence's last document may be cut short by the sequence's end.
All inputs are finite; a program needn't handle non-finite values.
Results may differ from a plain program's by a relative error of at most 0.013.
Values may be sent and summed in bfloat16 or wider, within the bound.
No kernel may reach another device: no remote copies, remote signals or barrier semaphores. Data moves between devices by JAX's collectives and lax.ppermute only.
A program may use at most 192 MiB of HBM per device.

v0:
```python
import math

import jax
import jax.numpy as jnp
from jax import lax
from jax.sharding import PartitionSpec as P

HEADS = 12
HEAD_DIM = 64
ROT = 16


EPSILON = 1e-05
NEG_BIG = -1e30


def layer_norm(values, gain, offset):
    centre = values - jnp.mean(values, -1, keepdims=True)
    spread = jnp.mean(centre * centre, -1, keepdims=True)
    return centre * lax.rsqrt(spread + EPSILON) * gain + offset


def gelu_exact(pre_act):
    return jax.nn.gelu(pre_act, approximate=False)


def rotary_tables(positions):
    freq_index = jnp.arange(ROT // 2, dtype=jnp.float32)
    inverse = jnp.exp(freq_index * (-2.0 * math.log(10000.0) / ROT))
    angles = positions.astype(jnp.float32)[..., None] * inverse
    return (jnp.cos(angles), jnp.sin(angles))


def rotate(values, cos_table, sin_table):
    half_rot = ROT // 2
    first_half = values[..., :half_rot]
    second_half = values[..., half_rot:ROT]
    return jnp.concatenate(
        [
            first_half * cos_table - second_half * sin_table,
            second_half * cos_table + first_half * sin_table,
            values[..., ROT:],
        ],
        -1,
    )


def outer_sum(left_rows, right_rows):
    return lax.dot_general(
        left_rows, right_rows, (((0,), (0,)), ((), ())), preferred_element_type=jnp.float32
    )


def inner_back(grad_rows, weight):
    return lax.dot_general(
        grad_rows, weight, (((1,), (1,)), ((), ())), preferred_element_type=jnp.float32
    )


def over_blocks(step_fn, state, pieces):
    total_rows = pieces[0].shape[0]
    block_len = math.gcd(total_rows, 512)
    block_count = total_rows // block_len
    stacked = tuple((piece.reshape((block_count, block_len) + piece.shape[1:]) for piece in pieces))

    def inner_step(carried, block_item):
        block_index, parts = block_item
        return (step_fn(carried, parts, block_index * block_len), None)

    state, unused = lax.scan(inner_step, state, (jnp.arange(block_count, dtype=jnp.int32), stacked))
    return state


def on_device(
    tokens,
    segment,
    ln1_gain,
    ln1_bias,
    ln2_gain,
    ln2_bias,
    qkv_weight,
    qkv_bias,
    dense_weight,
    dense_bias,
    fc1_weight,
    fc1_bias,
    output_feed_weight,
    output_feed_bias,
    cotangent,
):
    local_len, groups, model_width = tokens.shape
    rows_all = local_len * groups
    seq_len = local_len * lax.axis_size("ctx")
    softmax_scale = HEAD_DIM ** (-0.5)
    shape_four = (local_len, groups, HEADS, HEAD_DIM)
    query_pos = lax.axis_index("ctx") * local_len + jnp.arange(local_len, dtype=jnp.int32)
    seg_cols = segment.T
    (
        gain_one,
        bias_one,
        gain_two,
        bias_two,
        qkv_full,
        qkv_shift,
        dense_full,
        dense_shift,
        up_full,
        up_shift,
        down_full,
        down_projection_offset,
    ) = (
        lax.all_gather(ln1_gain, ("seq", "ctx"), axis=0, tiled=True),
        lax.all_gather(ln1_bias, ("seq", "ctx"), axis=0, tiled=True),
        lax.all_gather(ln2_gain, ("seq", "ctx"), axis=0, tiled=True),
        lax.all_gather(ln2_bias, ("seq", "ctx"), axis=0, tiled=True),
        lax.all_gather(qkv_weight, ("seq", "ctx"), axis=0, tiled=True),
        lax.all_gather(qkv_bias, ("seq", "ctx"), axis=0, tiled=True),
        lax.all_gather(dense_weight, ("seq", "ctx"), axis=0, tiled=True),
        lax.all_gather(dense_bias, ("seq", "ctx"), axis=0, tiled=True),
        lax.all_gather(fc1_weight, ("seq", "ctx"), axis=0, tiled=True),
        lax.all_gather(fc1_bias, ("seq", "ctx"), axis=0, tiled=True),
        lax.all_gather(output_feed_weight, ("seq", "ctx"), axis=0, tiled=True),
        lax.all_gather(output_feed_bias, ("seq", "ctx"), axis=0, tiled=True),
    )
    float_tok = tokens.reshape(rows_all, model_width).astype(jnp.float32)
    normed_one = layer_norm(
        float_tok, gain_one.astype(jnp.float32), bias_one.astype(jnp.float32)
    ).astype(jnp.bfloat16)
    normed_two = layer_norm(
        float_tok, gain_two.astype(jnp.float32), bias_two.astype(jnp.float32)
    ).astype(jnp.bfloat16)
    projected = jnp.dot(
        normed_one, qkv_full, preferred_element_type=jnp.float32
    ) + qkv_shift.astype(jnp.float32)
    positions = query_pos[:, None] - segment
    cos_table, sin_table = rotary_tables(positions)
    cos_table = cos_table[:, :, None, :]
    sin_table = sin_table[:, :, None, :]
    queries = rotate(projected[:, :model_width].reshape(shape_four), cos_table, sin_table).astype(
        jnp.bfloat16
    )
    keys_rot = rotate(
        projected[:, model_width : 2 * model_width].reshape(shape_four), cos_table, sin_table
    ).astype(jnp.bfloat16)
    values_loc = projected[:, 2 * model_width :].reshape(shape_four).astype(jnp.bfloat16)
    key_value = jnp.concatenate(
        [
            keys_rot.reshape(local_len, groups, model_width),
            values_loc.reshape(local_len, groups, model_width),
        ],
        -1,
    )

    def live_mask(key_start, key_rows):
        key_pos = key_start + jnp.arange(key_rows, dtype=jnp.int32)
        allowed = (key_pos[None, None, :] <= query_pos[None, :, None]) & (
            key_pos[None, None, :] >= seg_cols[:, :, None]
        )
        return allowed[:, None]

    def split_pair(piece):
        key_rows = piece.shape[0]
        return (
            piece[:, :, :model_width].reshape((key_rows, groups, HEADS, HEAD_DIM)),
            piece[:, :, model_width:].reshape((key_rows, groups, HEADS, HEAD_DIM)),
        )

    def attend_step(state, pieces, key_start):
        part_keys, part_vals = split_pair(pieces[0])
        key_rows = part_keys.shape[0]
        run_max, run_total, run_acc = state
        scores = (
            jnp.einsum("lsha,ksha->shlk", queries, part_keys, preferred_element_type=jnp.float32)
            * softmax_scale
        )
        allowed = live_mask(key_start, key_rows)
        scores = jnp.where(allowed, scores, NEG_BIG)
        new_max = jnp.maximum(run_max, jnp.max(scores, -1))
        weights = jnp.where(allowed, jnp.exp(scores - new_max[..., None]), 0.0)
        factor = jnp.exp(run_max - new_max)
        run_total = run_total * factor + jnp.sum(weights, -1)
        run_acc = run_acc * factor[..., None] + jnp.einsum(
            "shlk,ksha->shla",
            weights.astype(jnp.bfloat16),
            part_vals,
            preferred_element_type=jnp.float32,
        )
        return (new_max, run_total, run_acc)

    head_zero = jnp.zeros((groups, HEADS, local_len), jnp.float32)
    query_zero = jnp.zeros((groups, HEADS, local_len, HEAD_DIM), jnp.float32)
    run_max, run_total, run_acc = over_blocks(
        attend_step,
        (head_zero + NEG_BIG, head_zero, query_zero),
        (lax.all_gather(key_value, "ctx", axis=0, tiled=True),),
    )
    attended_f = run_acc / run_total[..., None]
    log_total = run_max + jnp.log(run_total)
    attended_low = (
        attended_f.transpose(2, 0, 1, 3).reshape(rows_all, model_width).astype(jnp.bfloat16)
    )
    branch_one = jnp.dot(
        attended_low, dense_full, preferred_element_type=jnp.float32
    ) + dense_shift.astype(jnp.float32)
    hidden_pre = jnp.dot(normed_two, up_full, preferred_element_type=jnp.float32) + up_shift.astype(
        jnp.float32
    )
    hidden_reduced = gelu_exact(hidden_pre).astype(jnp.bfloat16)
    second_branch = jnp.dot(
        hidden_reduced, down_full, preferred_element_type=jnp.float32
    ) + down_projection_offset.astype(jnp.float32)
    output = (
        (float_tok + branch_one + second_branch)
        .astype(jnp.bfloat16)
        .reshape(local_len, groups, model_width)
    )
    gain_back_one, gain_back_two, qkv_back, dense_back, up_back, down_back = (
        lax.all_gather(ln1_gain, ("seq", "ctx"), axis=0, tiled=True),
        lax.all_gather(ln2_gain, ("seq", "ctx"), axis=0, tiled=True),
        lax.all_gather(qkv_weight, ("seq", "ctx"), axis=0, tiled=True),
        lax.all_gather(dense_weight, ("seq", "ctx"), axis=0, tiled=True),
        lax.all_gather(fc1_weight, ("seq", "ctx"), axis=0, tiled=True),
        lax.all_gather(output_feed_weight, ("seq", "ctx"), axis=0, tiled=True),
    )
    cot_rows = cotangent.reshape(rows_all, model_width)
    cot_float = cot_rows.astype(jnp.float32)
    shift_grad = jnp.sum(cot_float, 0)
    down_grad = outer_sum(hidden_reduced, cot_rows)
    hidden_grad = inner_back(cot_rows, down_back)
    unused_value, gelu_back = jax.vjp(gelu_exact, hidden_pre)
    pre_grad = gelu_back(hidden_grad)[0].astype(jnp.bfloat16)
    up_grad = outer_sum(normed_two, pre_grad)
    up_shift_grad = jnp.sum(pre_grad.astype(jnp.float32), 0)
    normed_two_grad = inner_back(pre_grad, up_back)
    dense_grad = outer_sum(attended_low, cot_rows)
    attended_grad = inner_back(cot_rows, dense_back).astype(jnp.bfloat16).reshape(shape_four)
    delta_rows = jnp.einsum("lsha,shla->shl", attended_grad.astype(jnp.float32), attended_f)

    def query_grad_step(state, pieces, key_start):
        part_keys, part_vals = split_pair(pieces[0])
        key_rows = part_keys.shape[0]
        scores = (
            jnp.einsum("lsha,ksha->shlk", queries, part_keys, preferred_element_type=jnp.float32)
            * softmax_scale
        )
        allowed = live_mask(key_start, key_rows)
        probs = jnp.where(
            allowed, jnp.exp(jnp.where(allowed, scores, NEG_BIG) - log_total[..., None]), 0.0
        )
        prob_grad = jnp.einsum(
            "lsha,ksha->shlk", attended_grad, part_vals, preferred_element_type=jnp.float32
        )
        score_grad = (probs * (prob_grad - delta_rows[..., None])).astype(jnp.bfloat16)
        query_acc = (
            state[0]
            + jnp.einsum(
                "shlk,ksha->shla", score_grad, part_keys, preferred_element_type=jnp.float32
            )
            * softmax_scale
        )
        key_part = (
            jnp.einsum("shlk,lsha->ksha", score_grad, queries, preferred_element_type=jnp.float32)
            * softmax_scale
        )
        value_part = jnp.einsum(
            "shlk,lsha->ksha",
            probs.astype(jnp.bfloat16),
            attended_grad,
            preferred_element_type=jnp.float32,
        )
        block_term = jnp.concatenate(
            [
                key_part.reshape(key_rows, groups, model_width),
                value_part.reshape(key_rows, groups, model_width),
            ],
            -1,
        )
        return (query_acc, lax.dynamic_update_slice_in_dim(state[1], block_term, key_start, 0))

    back_init = (query_zero, jnp.zeros((seq_len, groups, 2 * model_width), jnp.float32))
    back_state = over_blocks(
        query_grad_step, back_init, (lax.all_gather(key_value, "ctx", axis=0, tiled=True),)
    )
    key_terms = lax.psum_scatter(
        back_state[1].astype(jnp.bfloat16), "ctx", scatter_dimension=0, tiled=True
    ).astype(jnp.float32)
    key_grad = key_terms[:, :, :model_width].reshape(shape_four)
    value_grad = key_terms[:, :, model_width:].reshape(shape_four)
    query_grad = back_state[0].transpose(2, 0, 1, 3)
    qkv_grad = jnp.concatenate(
        [
            rotate(query_grad, cos_table, -sin_table).reshape(rows_all, model_width),
            rotate(key_grad, cos_table, -sin_table).reshape(rows_all, model_width),
            value_grad.reshape(rows_all, model_width),
        ],
        -1,
    ).astype(jnp.bfloat16)
    qkv_grad_w = outer_sum(normed_one, qkv_grad)
    qkv_shift_grad = jnp.sum(qkv_grad.astype(jnp.float32), 0)
    normed_one_grad = inner_back(qkv_grad, qkv_back)
    zero_shift = jnp.zeros((model_width,), jnp.float32)
    unused_one, norm_back_one = jax.vjp(
        layer_norm, float_tok, gain_back_one.astype(jnp.float32), zero_shift
    )
    tok_grad_one, gain_one_grad, bias_one_grad = norm_back_one(normed_one_grad)
    unused_two, norm_back_two = jax.vjp(
        layer_norm, float_tok, gain_back_two.astype(jnp.float32), zero_shift
    )
    tok_grad_two, gain_two_grad, bias_two_grad = norm_back_two(normed_two_grad)
    tokens_grad = (
        (cot_float + tok_grad_one + tok_grad_two)
        .astype(jnp.bfloat16)
        .reshape(local_len, groups, model_width)
    )
    summed = (
        lax.psum_scatter(gain_one_grad, ("seq", "ctx"), scatter_dimension=0, tiled=True),
        lax.psum_scatter(bias_one_grad, ("seq", "ctx"), scatter_dimension=0, tiled=True),
        lax.psum_scatter(gain_two_grad, ("seq", "ctx"), scatter_dimension=0, tiled=True),
        lax.psum_scatter(bias_two_grad, ("seq", "ctx"), scatter_dimension=0, tiled=True),
        lax.psum_scatter(qkv_grad_w, ("seq", "ctx"), scatter_dimension=0, tiled=True),
        lax.psum_scatter(qkv_shift_grad, ("seq", "ctx"), scatter_dimension=0, tiled=True),
        lax.psum_scatter(dense_grad, ("seq", "ctx"), scatter_dimension=0, tiled=True),
        lax.psum_scatter(shift_grad, ("seq", "ctx"), scatter_dimension=0, tiled=True),
        lax.psum_scatter(up_grad, ("seq", "ctx"), scatter_dimension=0, tiled=True),
        lax.psum_scatter(up_shift_grad, ("seq", "ctx"), scatter_dimension=0, tiled=True),
        lax.psum_scatter(down_grad, ("seq", "ctx"), scatter_dimension=0, tiled=True),
        lax.psum_scatter(shift_grad, ("seq", "ctx"), scatter_dimension=0, tiled=True),
    )
    return (
        output,
        tokens_grad,
        summed[0],
        summed[1],
        summed[2],
        summed[3],
        summed[4],
        summed[5],
        summed[6],
        summed[7],
        summed[8],
        summed[9],
        summed[10],
        summed[11],
    )


def solution(mesh):
    placed = (
        P("ctx", "seq", None),
        P("ctx", "seq"),
        P(("seq", "ctx")),
        P(("seq", "ctx")),
        P(("seq", "ctx")),
        P(("seq", "ctx")),
        P(("seq", "ctx"), None),
        P(("seq", "ctx")),
        P(("seq", "ctx"), None),
        P(("seq", "ctx")),
        P(("seq", "ctx"), None),
        P(("seq", "ctx")),
        P(("seq", "ctx"), None),
        P(("seq", "ctx")),
        P("ctx", "seq", None),
    )
    return jax.shard_map(
        on_device,
        mesh=mesh,
        in_specs=placed,
        out_specs=(
            P("ctx", "seq", None),
            P("ctx", "seq", None),
            P(("seq", "ctx")),
            P(("seq", "ctx")),
            P(("seq", "ctx")),
            P(("seq", "ctx")),
            P(("seq", "ctx"), None),
            P(("seq", "ctx")),
            P(("seq", "ctx"), None),
            P(("seq", "ctx")),
            P(("seq", "ctx"), None),
            P(("seq", "ctx")),
            P(("seq", "ctx"), None),
            P(("seq", "ctx")),
        ),
        check_vma=False,
    )
```

profile of v0, /device:TPU:0, one launch (start us, length us, event | category | flops | bytes accessed | tf_op | source)
XLA Modules:
  0.0 1495.4 jit_solution(5138301103193831858)
XLA Ops:
  17.6 43.0 %all-reduce.16 = (bf16[768]{0:T(1024)(128)(2,1)}, bf16[768]{0:T(1024)(128)(2,1)}, bf16[3072]{0:T(1024)(128)(2,1)}, bf16[2304]{0:T(1024)(128)(2,1)S(1)}, bf16[768...) all-reduce(bf16[768]{0:T(1024)(128)(2,1)S(1)} %dynamic-update-slice, ...), channel_id=1, replica_groups=mesh['seq'=2,'ctx'=16] {'seq','ctx'}, use_global_device_ids=true, to_apply=%add.5 | all-reduce | flops 9984 | bytes 39936
  61.0 5.2 fusion.34
  66.2 7.8 all-gather.6.cloned.1.call-done
  74.0 4.1 convolution_add_fusion
  94.6 18.5 %slice_multiply_fusion.9 = (f32[256,2,12,8]{3,2,1,0:T(8,128)}, f32[256,2,12,8]{3,2,1,0:T(8,128)}, f32[256,2,12,8]{3,2,1,0:T(8,128)}, f32[256,2,12,8]{3,2,1,0:T(8...) fusion(f32[256,2,12,64]{3,2,1,0:T(8,128)} %reshape.262, ...), kind=kLoop, calls=%fused_computation.77 | loop fusion | flops 393216 | bytes 2392064 | tf_op jit(solution)/shard_map/mul | solution.py:40
  137.5 4.2 bitcast_convert_fusion
  141.8 4.1 copy.152
  145.8 4.1 slice.133
  165.4 101.9 %all-gather.8.cloned.1.call-done = bf16[4096,2,1536]{0,2,1:T(8,128)(2,1)} async-done(((bf16[256,2,1536]{0,2,1:T(8,128)(2,1)}), bf16[4096,2,1536]{0,2,1:T(8,128)(2,1)}) %all-gather.8.cloned.1.call-update) | async-done | bytes 25165840 | tf_op jit(solution)/shard_map/all_gather | solution.py:195
  267.3 32.6 %copy.126 = bf16[4096,2,1536]{2,0,1:T(8,128)(2,1)} copy(bf16[4096,2,1536]{0,2,1:T(8,128)(2,1)} %all-gather.8.cloned.1.call-done) | data formatting | bytes 50331648 | tf_op jit(solution)/shard_map/all_gather | solution.py:195
  299.9 30.9 %copy.132 = bf16[8,512,2,1536]{1,3,2,0:T(8,128)(2,1)} copy(bf16[8,512,2,1536]{3,1,0,2:T(8,128)(2,1)} %bitcast.147) | data formatting | bytes 50331648
  330.8 113.2 %while.28 = (s32[]{:T(128)}, f32[2,12,256]{2,1,0:T(8,128)S(1)}, f32[2,12,256]{2,1,0:T(8,128)S(1)}, f32[2,12,256,64]{2,3,1,0:T(8,128)}, s32[8]{0:T(128)S(1)}, /*i...) while((s32[]{:T(128)}, f32[2,12,256]{2,1,0:T(8,128)S(1)}, ...), condition=%wide.region_5.6_spmd.clone, body=%wide.region_2.5_spmd.clone.sunk | while | flops 848067328 | bytes 71706848 | solution.py:70
  354.3 3.6 fusion.113
  382.6 3.6 fusion.113
  396.8 3.6 fusion.113
  411.0 3.6 fusion.113
  439.3 3.6 fusion.113
  447.2 8.5 broadcast_in_dim.62
  455.7 274.1 %while.29 = (s32[]{:T(128)}, f32[2,12,256,64]{2,3,1,0:T(8,128)S(1)}, bf16[4096,2,1536]{0,2,1:T(8,128)(2,1)}, s32[8]{0:T(128)S(1)}, s32[2,256]{1,0:T(2,128)S(1)},...) while((s32[]{:T(128)}, ...), condition=%wide.region_7.8_spmd.clone, body=%wide.region_6.7_spmd.clone.sunk | while | flops 2060714752 | bytes 97077504 | solution.py:70
  461.0 6.3 fusion.125
  467.3 9.1 fusion.127
  476.4 8.5 fusion.126
  495.2 6.3 fusion.125
  501.6 9.1 fusion.127
  510.6 8.5 fusion.126
  529.5 6.3 fusion.125
  535.8 9.1 fusion.127
  544.8 8.5 fusion.126
  563.7 6.3 fusion.125
  570.0 9.1 fusion.127
  579.0 8.5 fusion.126
  597.9 6.3 fusion.125
  604.2 9.1 fusion.127
  613.2 8.5 fusion.126
  632.2 6.3 fusion.125
  638.5 9.1 fusion.127
  647.5 8.5 fusion.126
  666.4 6.3 fusion.125
  672.7 9.1 fusion.127
  681.8 8.5 fusion.126
  700.7 6.3 fusion.125
  707.0 9.1 fusion.127
  716.0 8.5 fusion.126
  730.6 8.2 fusion.37
  738.8 20.4 %convert_reduce_fusion = (f32[3072]{0:T(1024)S(1)}, bf16[512,3072]{1,0:T(8,128)(2,1)}, f32[512,3072]{1,0:T(8,128)S(1)}) fusion(f32[512,3072]{1,0:T(8,128)} %fusion.37, f32[3072]{0:T(1024)S(1)} %convert_element_type.126, bf16[512,768]{1,0:T(8,128)(2,1)S(1)} %copy-done.4, bf16[3072,768]{1,0:T(8,128)(2,1)} %all-gather.14.cloned.1.call-done), kind=kOutput, calls=%fused_computation.45 | convolution fusion | flops 2533880832 | bytes 21258240 | tf_op jit(solution)/shard_map/dot_general | solution.py:55
  762.6 5.1 fusion.49
  767.7 9.5 fusion.36
  778.3 3.8 copy.133
  787.8 4.5 copy.136
  792.3 4.1 slice.132
  796.4 178.4 %reduce-scatter.6.cloned.1.call-done = bf16[256,2,1536]{0,2,1:T(8,128)(2,1)} async-done(((bf16[4096,2,1536]{0,2,1:T(8,128)(2,1)}), bf16[256,2,1536]{0,2,1:T(8,128)(2,1)}) %reduce-scatter.6.cloned.1.call-update) | async-done | bytes 1572880 | tf_op jit(solution)/shard_map/reduce_scatter | solution.py:284
  978.9 3.9 copy.137
  991.3 7.4 slice_multiply_fusion.1
  1002.2 4.0 reshape.268
  1020.2 3.9 copy.142
  1030.2 5.3 fusion.35
  1037.3 6.1 fusion.46
  1048.2 5.0 fusion.47
  1053.2 5.6 multiply_reduce_fusion.1
  1064.4 41.2 %all-reduce.15 = (f32[768]{0:T(1024)S(1)}, f32[768]{0:T(1024)S(1)}, f32[768]{0:T(1024)S(1)}, f32[768]{0:T(1024)S(1)}, f32[2304]{0:T(1024)S(1)}, /*index=5*/f32[768]{0:T(1024)S(1)}, f32[3072]{0:T(1024)S(1)}) all-reduce(f32[768]{0:T(1024)S(1)} %get-tuple-element.294, ...), channel_id=3, replica_groups=mesh['seq'=2,'ctx'=16] {'seq','ctx'}, use_global_device_ids=true, to_apply=%region_14.15.clone | all-reduce | flops 9216 | bytes 73728
  1109.2 7.2 reduce-scatter.14.cloned.1.call-done
  1116.3 142.2 %reduce-scatter.12.cloned.1.call-done = f32[24,3072]{1,0:T(8,128)} async-done(((f32[768,3072]{1,0:T(8,128)}), f32[24,3072]{1,0:T(8,128)}) %reduce-scatter.12.cloned.1.call-update) | async-done | bytes 294928 | tf_op jit(solution)/shard_map/reduce_scatter | solution.py:324
  1258.5 104.0 %reduce-scatter.10.cloned.1.call-done = f32[24,768]{1,0:T(8,128)} async-done(((f32[768,768]{1,0:T(8,128)}), f32[24,768]{1,0:T(8,128)}) %reduce-scatter.10.cloned.1.call-update) | async-done | bytes 73744 | tf_op jit(solution)/shard_map/reduce_scatter | solution.py:322
  1362.5 125.2 %reduce-scatter.8.cloned.1.call-done = f32[24,2304]{1,0:T(8,128)} async-done(((f32[768,2304]{1,0:T(8,128)}), f32[24,2304]{1,0:T(8,128)}) %reduce-scatter.8.cloned.1.call-update) | async-done | bytes 221200 | tf_op jit(solution)/shard_map/reduce_scatter | solution.py:320
  (464 shorter events, 299.5 us)
Async XLA Ops:
  7.2 8.5 copy-start.46
  7.2 8.8 copy-start.47
  7.2 9.0 copy-start.48
  7.2 9.2 copy-start.49
  7.2 9.4 copy-start.50
  7.2 9.7 copy-start.51
  7.2 9.9 copy-start.52
  7.3 10.1 copy-start.53
  7.3 53.4 %copy-start.29 = (s32[256,2]{0,1:T(2,128)S(1)}, s32[256,2]{0,1:T(2,128)}, u32[]{:S(2)}) copy-start(s32[256,2]{0,1:T(2,128)} %param.20) | copy-start | bytes 6148
  7.3 66.7 %all-gather.6.cloned.1.call-start = ((), (), s32[]{:S(2)}) async-start(), calls=%async_computation.5 | async-start | bytes 3649536 | tf_op jit(solution)/shard_map/all_gather | solution.py:116
  8.0 122.0 %all-gather.10.cloned.1.call-start = ((), (), s32[]{:S(2)}) async-start(), calls=%async_computation.7 | async-start | bytes 1216512 | tf_op jit(solution)/shard_map/all_gather | solution.py:118
  8.8 258.6 %all-gather.8.cloned.1.call-start = ((), (), s32[]{:S(2)}) async-start(), calls=%async_computation.6 | async-start | bytes 26738688 | tf_op jit(solution)/shard_map/all_gather | solution.py:195
  10.8 63.2 %copy-start.34 = (f32[512]{0:T(512)}, f32[512]{0:T(512)S(1)}, u32[]{:S(2)}) copy-start(f32[512]{0:T(512)S(1)} %div.44) | copy-start | bytes 6148
  15.7 62.5 %copy-start.5 = (f32[512,768]{1,0:T(8,128)}, f32[512,768]{1,0:T(8,128)S(1)}, u32[]{:S(2)}) copy-start(f32[512,768]{1,0:T(8,128)S(1)} %reshape.273) | copy-start | bytes 4718596
  60.6 13.4 copy-start.32
  60.6 13.4 copy-start.39
  60.9 13.0 copy-start.30
  61.0 13.0 copy-start.36
  66.2 28.4 %copy-start.20 = (f32[256,2,8]{2,1,0:T(2,128)}, f32[256,2,8]{2,1,0:T(2,128)S(1)}, u32[]{:S(2)}) copy-start(f32[256,2,8]{2,1,0:T(2,128)S(1)} %get-tuple-element.403) | copy-start | bytes 49156
  78.1 2.1 copy-start.13
  89.7 5.0 copy-start.27
  122.3 3.3 copy-start.23
  122.3 3.4 copy-start.17
  125.6 3.0 copy-start.14
  127.0 603.6 %all-gather.12.cloned.1.call-start = ((), (), s32[]{:S(2)}) async-start(), calls=%async_computation.8 | async-start | bytes 4866048 | tf_op jit(solution)/shard_map/all_gather | solution.py:120
  127.6 611.2 %all-gather.14.cloned.1.call-start = ((), (), s32[]{:S(2)}) async-start(), calls=%async_computation.9 | async-start | bytes 4866048 | tf_op jit(solution)/shard_map/all_gather | solution.py:122
  128.1 846.6 %reduce-scatter.6.cloned.1.call-start = ((), (), s32[]{:S(2)}) async-start(), calls=%async_computation.10 | async-start | bytes 26738688 | tf_op jit(solution)/shard_map/reduce_scatter | solution.py:284
  128.9 8.6 copy-start.3
  337.0 3.2 copy-start.24
  351.1 3.2 copy-start.24
  365.3 3.2 copy-start.24
  379.4 3.2 copy-start.24
  393.6 3.2 copy-start.24
  407.8 3.2 copy-start.24
  421.9 3.2 copy-start.24
  436.1 3.2 copy-start.24
  447.2 8.5 copy-start.28
  486.1 2.0 copy-start.1
  520.3 2.0 copy-start.1
  554.6 2.0 copy-start.1
  588.8 2.0 copy-start.1
  691.5 2.0 copy-start.1
  729.8 386.5 %reduce-scatter.14.cloned.1.call-start = ((), (), s32[]{:S(2)}) async-start(), calls=%async_computation.14 | async-start | bytes 9732096 | tf_op jit(solution)/shard_map/reduce_scatter | solution.py:326
  730.5 8.3 copy-start.4
  738.8 20.4 %copy-start.7 = (f32[512,3072]{1,0:T(8,128)S(1)}, f32[512,3072]{1,0:T(8,128)}, u32[]{:S(2)}) copy-start(f32[512,3072]{1,0:T(8,128)} %fusion.37) | copy-start | bytes 18874372
  767.7 490.8 %reduce-scatter.12.cloned.1.call-start = ((), (), s32[]{:S(2)}) async-start(), calls=%async_computation.13 | async-start | bytes 9732096 | tf_op jit(solution)/shard_map/reduce_scatter | solution.py:324
  777.2 585.3 %reduce-scatter.10.cloned.1.call-start = ((), (), s32[]{:S(2)}) async-start(), calls=%async_computation.12 | async-start | bytes 2433024 | tf_op jit(solution)/shard_map/reduce_scatter | solution.py:322
  785.3 2.3 copy-start.9
  787.6 700.2 %reduce-scatter.8.cloned.1.call-start = ((), (), s32[]{:S(2)}) async-start(), calls=%async_computation.11 | async-start | bytes 7299072 | tf_op jit(solution)/shard_map/reduce_scatter | solution.py:320
  988.8 2.4 copy-start
  988.8 2.4 copy-start.21
  988.8 2.5 copy-start.26
  991.3 7.4 copy-start.2
  1015.7 3.5 copy-start.22
  1024.1 6.1 copy-start.33
  1024.1 6.1 copy-start.40
  1026.1 2.5 copy-start.16
  1026.1 4.0 copy-start.6
  1037.3 6.1 copy-start.10
  1037.3 6.1 copy-start.45
  1048.2 5.0 copy-start.55
  1053.2 5.6 copy-start.31
  1059.8 4.1 copy-start.12
  1106.2 382.0 %copy-start.54 = (f32[24]{0:T(128)}, f32[24]{0:T(128)S(1)}, u32[]{:S(2)}) copy-start(f32[24]{0:T(128)S(1)} %dynamic-slice.5) | copy-start | bytes 292
  (23 other events, 26.8 us)
Sparse Core Ops, SparseCore 0:
  11.0 62.9 all-gather.5
  76.9 53.0 all-gather.9
  131.5 135.7 all-gather.7
  270.1 62.3 all-gather.11
  335.3 62.4 all-gather.13
  730.0 244.7 reduce-scatter.5
  981.3 134.9 reduce-scatter.13
  1123.8 134.7 reduce-scatter.11
  1264.4 98.0 reduce-scatter.9
  1369.6 118.1 reduce-scatter.7
where the time goes:
time: 1500 us
  waiting for transfers between devices  670 us (45%)
  matrix products  338 us (23%)
  local copies, waits for them, and re-layouts  272 us (18%)
  other arithmetic  102 us (7%)
  blocking collectives  84.2 us (6%)
  between operations  15.2 us (1%)
    reduce_scatter x1, waiting for transfers between devices, on_device(): lax.psum_scatter(back_state[1].astype(jnp.bfloat16), 'ctx', scatter_dimen...  178 us
    reduce_scatter x1, waiting for transfers between devices, on_device(): lax.psum_scatter(up_grad, ('seq', 'ctx'), scatter_dimension=0, tiled=True)  142 us
    reduce_scatter x1, waiting for transfers between devices, on_device(): lax.psum_scatter(qkv_grad_w, ('seq', 'ctx'), scatter_dimension=0, tiled=T...  125 us
    reduce_scatter x1, waiting for transfers between devices, on_device(): lax.psum_scatter(dense_grad, ('seq', 'ctx'), scatter_dimension=0, tiled=T...  104 us
    all_gather x1, waiting for transfers between devices, on_device(): lax.all_gather(key_value, 'ctx', axis=0, tiled=True)  102 us
    unnamed x2, blocking collectives  84.2 us
    dot_general x8, matrix products, query_grad_step(): jnp.einsum('shlk,lsha->ksha', probs.astype(jnp.bfloat16), attended_grad,...  72.4 us
    dot_general x8, matrix products, query_grad_step(): jnp.einsum('lsha,ksha->shlk', attended_grad, part_vals, preferred_element...  68.1 us
  transfers between devices with their start and end apart: 10, of which 8 were waited for; matrix products, arithmetic and copies ran while one was open for 46% of the time, Pallas kernels for 0%

commit v1 on v0

v1 whole, which is shorter than its diff:
```python
import functools
import math

import jax
import jax.numpy as jnp
from jax import lax
from jax.experimental import pallas as pl
from jax.experimental.pallas import tpu as pltpu
from jax.sharding import Mesh, PartitionSpec as P

HEADS = 12
HEAD_DIM = 64
ROT = 16
TRIO = 3
TILE = 128
PACK = 5 * TILE
OPACK = 2 * TILE

EPSILON = 1e-05
NEG_BIG = -1e30
BF = jnp.bfloat16
F32 = jnp.float32
ALL_AXES = ("seq", "unit", "part")
VMEM_BYTES = 56 * 1024 * 1024


def params_of(*semantics):
    return pltpu.CompilerParams(
        dimension_semantics=semantics, vmem_limit_bytes=VMEM_BYTES
    )


def mm(a, b):
    return jnp.dot(a, b, preferred_element_type=F32)


def outer_sum(left_rows, right_rows):
    return lax.dot_general(
        left_rows, right_rows, (((0,), (0,)), ((), ())), preferred_element_type=F32
    )


def inner_back(grad_rows, weight):
    return lax.dot_general(
        grad_rows, weight, (((1,), (1,)), ((), ())), preferred_element_type=F32
    )


def lane_of(shape):
    return lax.broadcasted_iota(jnp.int32, shape, len(shape) - 1)


def turn(tile, cos, sin):
    partner = jnp.where(
        lane_of(tile.shape) % HEAD_DIM < ROT // 2,
        pltpu.roll(tile, TILE - ROT // 2, 1),
        pltpu.roll(tile, ROT // 2, 1),
    )
    return tile * cos + partner * sin


def project_kernel(x_ref, w_ref, b_ref, cos_ref, sin_ref, aux_ref, out_ref):
    y = mm(x_ref[...], w_ref[...]) + b_ref[...]
    cos = cos_ref[...]
    sin = sin_ref[...]
    for t in range(5):
        tile = y[:, t * TILE : (t + 1) * TILE]
        if t in (0, 1, 3):
            tile = turn(tile, cos, sin)
        if t == 4:
            tile = tile + aux_ref[...]
        out_ref[0, :, t * TILE : (t + 1) * TILE] = tile.astype(BF)


def project(xn, weight, bias, cos, sin, aux, rows, trios, groups):
    d = xn.shape[1]
    row_spec = pl.BlockSpec((rows, TILE), lambda g, s: (s, 0))
    return pl.pallas_call(
        project_kernel,
        grid=(trios, groups),
        in_specs=[
            pl.BlockSpec((rows, d), lambda g, s: (s, 0)),
            pl.BlockSpec((d, PACK), lambda g, s: (0, g)),
            pl.BlockSpec((1, PACK), lambda g, s: (0, g)),
            row_spec,
            row_spec,
            row_spec,
        ],
        out_specs=pl.BlockSpec((1, rows, PACK), lambda g, s: (g * groups + s, 0, 0)),
        out_shape=jax.ShapeDtypeStruct((trios * groups, rows, PACK), BF),
        compiler_params=params_of("arbitrary", "arbitrary"),
        name="project",
    )(xn, weight, bias, cos, sin, aux)


def unturn_kernel(in_ref, cos_ref, sin_ref, out_ref):
    cos = cos_ref[...]
    sin = sin_ref[...]
    for t in range(5):
        tile = in_ref[0, :, t * TILE : (t + 1) * TILE].astype(F32)
        if t in (0, 1, 3):
            tile = turn(tile, cos, -sin)
        out_ref[:, t * TILE : (t + 1) * TILE] = tile.astype(BF)


def unturn(packed, cos, sin, rows, trios, groups):
    row_spec = pl.BlockSpec((rows, TILE), lambda g, s: (s, 0))
    return pl.pallas_call(
        unturn_kernel,
        grid=(trios, groups),
        in_specs=[
            pl.BlockSpec((1, rows, PACK), lambda g, s: (g * groups + s, 0, 0)),
            row_spec,
            row_spec,
        ],
        out_specs=pl.BlockSpec((rows, PACK), lambda g, s: (s, g)),
        out_shape=jax.ShapeDtypeStruct((rows * groups, trios * PACK), BF),
        compiler_params=params_of("arbitrary", "arbitrary"),
        name="unturn",
    )(packed, cos, sin)


def flip(tile):
    return tile.astype(F32).T


def head_rows(flipped, low):
    row = lax.broadcasted_iota(jnp.int32, flipped.shape, 0)
    keep = row < HEAD_DIM if low else row >= HEAD_DIM
    return jnp.where(keep, flipped, 0.0)


def head_lanes(tile, low):
    lane = lane_of(tile.shape)
    keep = lane < HEAD_DIM if low else lane >= HEAD_DIM
    return jnp.where(keep, tile, 0.0)


def query_sides(q_ref, qb):
    scale = HEAD_DIM ** (-0.5)
    a = flip(q_ref[0, :, 0:TILE]) * scale
    d = flip(q_ref[0, :, 3 * TILE : 4 * TILE]) * scale
    qb[0] = head_rows(a, True).astype(BF)
    qb[1] = head_rows(a, False).astype(BF)
    qb[2] = jnp.concatenate(
        [jnp.zeros((HEAD_DIM, d.shape[1]), F32), d[:HEAD_DIM]], 0
    ).astype(BF)


def live_of(seg_row, key_start, query_start, rows):
    shape = (rows, rows)
    key_pos = key_start + lax.broadcasted_iota(jnp.int32, shape, 0)
    query_pos = query_start + lax.broadcasted_iota(jnp.int32, shape, 1)
    return (key_pos <= query_pos) & (key_pos >= seg_row)


def block_loop(meta, part, units, rows, step):
    j = pl.program_id(0)
    c = meta[2 * units]
    diag = j * part + c
    first = meta[j] // rows
    top_seg = meta[units + j]

    def one(kb, unused):
        where = (lax.rem(c - lax.rem(kb, part) + part, part), kb // part)
        masked = (kb == diag) | (top_seg > kb * rows)

        @pl.when(masked)
        def _():
            step(where, kb, diag, True)

        @pl.when(jnp.logical_not(masked))
        def _():
            step(where, kb, diag, False)

        return unused

    lax.fori_loop(first, diag + 1, one, 0)
    return diag


def forward_kernel(
    part, units, meta, q_ref, kv_ref, seg_ref, o_ref, ot_ref, lse_ref, qb, vt, top, total, acc
):
    rows = q_ref.shape[1]
    c = meta[2 * units]

    @pl.when(pl.program_id(0) == 0)
    def _():
        for i in range(part):
            p = lax.rem(c - i + part, part)
            for unit in range(units):
                kb = unit * part + p
                vt[kb, :TILE] = flip(kv_ref[i, unit, :, TILE : 2 * TILE]).astype(BF)
                vt[kb, TILE:] = flip(kv_ref[i, unit, :, 3 * TILE :])[:HEAD_DIM].astype(BF)

    query_sides(q_ref, qb)
    top[...] = jnp.full(top.shape, NEG_BIG, F32)
    total[...] = jnp.zeros(total.shape, F32)
    acc[...] = jnp.zeros(acc.shape, F32)
    seg_row = seg_ref[0]

    def step(where, kb, diag, masked):
        k01 = kv_ref[where[0], where[1], :, 0:TILE]
        k2 = kv_ref[where[0], where[1], :, 2 * TILE : 3 * TILE]
        if masked:
            live = live_of(seg_row, kb * rows, diag * rows, rows)
        for h in range(TRIO):
            score = mm(k2 if h == 2 else k01, qb[h])
            if masked:
                score = jnp.where(live, score, NEG_BIG)
            old = top[h : h + 1]
            new = jnp.maximum(old, jnp.max(score, 0, keepdims=True))
            weight = jnp.exp(score - new)
            if masked:
                weight = jnp.where(live, weight, 0.0)
            factor = jnp.exp(old - new)
            top[h : h + 1] = new
            total[h : h + 1] = total[h : h + 1] * factor + jnp.sum(weight, 0, keepdims=True)
            vth = vt[kb, h * HEAD_DIM : (h + 1) * HEAD_DIM]
            acc[h] = acc[h] * factor + mm(vth, weight.astype(BF))

    block_loop(meta, part, units, rows, step)
    out = [acc[h] / total[h : h + 1] for h in range(TRIO)]
    for h in range(TRIO):
        ot_ref[0, h * HEAD_DIM : (h + 1) * HEAD_DIM] = out[h]
    lse_ref[0, 0:TRIO] = top[0:TRIO] + jnp.log(total[0:TRIO])
    o_ref[0, :, :TILE] = jnp.concatenate(out[:2], 0).T.astype(BF)
    o_ref[0, :, TILE:] = jnp.concatenate([out[2], jnp.zeros_like(out[2])], 0).T.astype(BF)


def backward_kernel(
    part,
    units,
    meta,
    q_ref,
    do_ref,
    ot_ref,
    lse_ref,
    kv_ref,
    seg_ref,
    own_ref,
    oth_ref,
    qb,
    db,
    qn,
    dn,
    kt,
    delta,
    dqt,
    dk01,
    dv01,
    dk2,
    dv2,
):
    rows = q_ref.shape[1]
    c = meta[2 * units]
    j = pl.program_id(0)

    @pl.when(j == 0)
    def _():
        for i in range(part):
            p = lax.rem(c - i + part, part)
            for unit in range(units):
                kb = unit * part + p
                kt[kb, :TILE] = flip(kv_ref[i, unit, :, 0:TILE]).astype(BF)
                kt[kb, TILE:] = flip(kv_ref[i, unit, :, 2 * TILE : 3 * TILE])[HEAD_DIM:].astype(BF)
        for ref in (dk01, dv01, dk2, dv2):
            ref[...] = jnp.zeros(ref.shape, F32)

    query_sides(q_ref, qb)
    scale = HEAD_DIM ** (-0.5)
    q01 = q_ref[0, :, 0:TILE].astype(F32) * scale
    q2 = pltpu.roll(q_ref[0, :, 3 * TILE : 4 * TILE].astype(F32), HEAD_DIM, 1) * scale
    qn[0:rows] = head_lanes(q01, True).astype(BF)
    qn[rows : 2 * rows] = head_lanes(q01, False).astype(BF)
    qn[2 * rows :] = head_lanes(q2, False).astype(BF)
    do01 = do_ref[0, :, :TILE].astype(F32)
    do2 = do_ref[0, :, TILE:].astype(F32)
    dn[0:rows] = head_lanes(do01, True).astype(BF)
    dn[rows : 2 * rows] = head_lanes(do01, False).astype(BF)
    dn[2 * rows :] = do2.astype(BF)
    do01t = do01.T
    do2t = do2.T
    db[0] = head_rows(do01t, True).astype(BF)
    db[1] = head_rows(do01t, False).astype(BF)
    db[2] = do2t.astype(BF)
    for h in range(TRIO):
        dot = do2t[:HEAD_DIM] if h == 2 else do01t[h * HEAD_DIM : (h + 1) * HEAD_DIM]
        delta[h : h + 1] = jnp.sum(
            dot * ot_ref[0, h * HEAD_DIM : (h + 1) * HEAD_DIM], 0, keepdims=True
        )
    dqt[...] = jnp.zeros(dqt.shape, F32)
    seg_row = seg_ref[0]

    def step(where, kb, diag, masked):
        k01 = kv_ref[where[0], where[1], :, 0:TILE]
        v01 = kv_ref[where[0], where[1], :, TILE : 2 * TILE]
        k2 = kv_ref[where[0], where[1], :, 2 * TILE : 3 * TILE]
        v2 = kv_ref[where[0], where[1], :, 3 * TILE :]
        if masked:
            live = live_of(seg_row, kb * rows, diag * rows, rows)
        probs = []
        grads = []
        for h in range(TRIO):
            score = mm(k2 if h == 2 else k01, qb[h])
            if masked:
                score = jnp.where(live, score, NEG_BIG)
            prob = jnp.exp(score - lse_ref[0, h : h + 1])
            if masked:
                prob = jnp.where(live, prob, 0.0)
            dprob = mm(v2 if h == 2 else v01, db[h])
            ds = (prob * (dprob - delta[h : h + 1])).astype(BF)
            probs.append(prob.astype(BF))
            grads.append(ds)
            kth = kt[kb, h * HEAD_DIM : (h + 1) * HEAD_DIM]
            dqt[h * HEAD_DIM : (h + 1) * HEAD_DIM] += mm(kth, ds)
        dv01[kb] += mm(jnp.concatenate(probs[:2], 1), dn[: 2 * rows])
        dk01[kb] += mm(jnp.concatenate(grads[:2], 1), qn[: 2 * rows])
        dv2[kb] += mm(probs[2], dn[2 * rows :])
        dk2[kb] += mm(grads[2], qn[2 * rows :])

    diag = block_loop(meta, part, units, rows, step)
    own_ref[j, :, 0:TILE] = (dqt[:TILE] * scale).T.astype(BF)
    dq2 = dqt[TILE:] * scale
    dk2[diag] += jnp.concatenate([dq2, jnp.zeros_like(dq2)], 0).T

    @pl.when(j == units - 1)
    def _():
        for unit in range(units):
            for i in range(part):
                kb = unit * part + lax.rem(c + i, part)
                for t, ref in enumerate((dk01, dv01, dk2, dv2)):
                    tile = ref[kb].astype(BF)
                    if i == 0:
                        own_ref[unit, :, (t + 1) * TILE : (t + 2) * TILE] = tile
                    else:
                        oth_ref[i - 1, unit, :, t * TILE : (t + 1) * TILE] = tile


def attention_cost(products, units, rows, part):
    pairs = TRIO * rows * rows * units * units * part // 2
    return pl.CostEstimate(
        flops=2 * 64 * products * pairs, bytes_accessed=20_000_000, transcendentals=pairs
    )


def whole_spec(shape):
    zeros = (0,) * len(shape)
    return pl.BlockSpec(shape, lambda j, meta: zeros)


def attend_forward(meta, packed, kv, seg):
    units, rows, unused = packed.shape
    part = kv.shape[0]
    return pl.pallas_call(
        functools.partial(forward_kernel, part, units),
        grid_spec=pltpu.PrefetchScalarGridSpec(
            num_scalar_prefetch=1,
            grid=(units,),
            in_specs=[
                pl.BlockSpec((1, rows, PACK), lambda j, meta: (j, 0, 0)),
                whole_spec(kv.shape),
                pl.BlockSpec((1, 1, rows), lambda j, meta: (j, 0, 0)),
            ],
            out_specs=[
                pl.BlockSpec((1, rows, OPACK), lambda j, meta: (j, 0, 0)),
                pl.BlockSpec((1, TRIO * HEAD_DIM, rows), lambda j, meta: (j, 0, 0)),
                pl.BlockSpec((1, 8, rows), lambda j, meta: (j, 0, 0)),
            ],
            scratch_shapes=[
                pltpu.VMEM((TRIO, TILE, rows), BF),
                pltpu.VMEM((units * part, TRIO * HEAD_DIM, rows), BF),
                pltpu.VMEM((8, rows), F32),
                pltpu.VMEM((8, rows), F32),
                pltpu.VMEM((TRIO, HEAD_DIM, rows), F32),
            ],
        ),
        out_shape=[
            jax.ShapeDtypeStruct((units, rows, OPACK), BF),
            jax.ShapeDtypeStruct((units, TRIO * HEAD_DIM, rows), F32),
            jax.ShapeDtypeStruct((units, 8, rows), F32),
        ],
        compiler_params=params_of("arbitrary"),
        cost_estimate=attention_cost(8, units, rows, part),
        name="attend_forward",
    )(meta, packed, kv, seg)


def attend_backward(meta, packed, dout, out_t, lse, kv, seg):
    units, rows, unused = packed.shape
    part = kv.shape[0]
    others = (max(part - 1, 1), units, rows, 4 * TILE)
    grads = pltpu.VMEM((units * part, rows, TILE), F32)
    return pl.pallas_call(
        functools.partial(backward_kernel, part, units),
        grid_spec=pltpu.PrefetchScalarGridSpec(
            num_scalar_prefetch=1,
            grid=(units,),
            in_specs=[
                pl.BlockSpec((1, rows, PACK), lambda j, meta: (j, 0, 0)),
                pl.BlockSpec((1, rows, OPACK), lambda j, meta: (j, 0, 0)),
                pl.BlockSpec((1, TRIO * HEAD_DIM, rows), lambda j, meta: (j, 0, 0)),
                pl.BlockSpec((1, 8, rows), lambda j, meta: (j, 0, 0)),
                whole_spec(kv.shape),
                pl.BlockSpec((1, 1, rows), lambda j, meta: (j, 0, 0)),
            ],
            out_specs=[whole_spec(packed.shape), whole_spec(others)],
            scratch_shapes=[
                pltpu.VMEM((TRIO, TILE, rows), BF),
                pltpu.VMEM((TRIO, TILE, rows), BF),
                pltpu.VMEM((TRIO * rows, TILE), BF),
                pltpu.VMEM((TRIO * rows, TILE), BF),
                pltpu.VMEM((units * part, TRIO * HEAD_DIM, rows), BF),
                pltpu.VMEM((8, rows), F32),
                pltpu.VMEM((TRIO * HEAD_DIM, rows), F32),
                grads,
                grads,
                grads,
                grads,
            ],
        ),
        out_shape=[
            jax.ShapeDtypeStruct(packed.shape, BF),
            jax.ShapeDtypeStruct(others, BF),
        ],
        compiler_params=params_of("arbitrary"),
        cost_estimate=attention_cost(20, units, rows, part),
        name="attend_backward",
    )(meta, packed, dout, out_t, lse, kv, seg)


def pack_columns(matrix, trios):
    r = matrix.shape[0]
    q, k, v = (
        part.reshape(r, trios, TRIO * HEAD_DIM) for part in jnp.split(matrix, 3, axis=1)
    )
    zeros = jnp.zeros((r, trios, HEAD_DIM), matrix.dtype)
    pieces = [q[..., :TILE], k[..., :TILE], v[..., :TILE], q[..., TILE:], k[..., TILE:]]
    return jnp.concatenate(pieces + [v[..., TILE:], zeros], -1).reshape(r, trios * PACK)


def unpack_columns(matrix, trios):
    r = matrix.shape[0]
    m = matrix.reshape(r, trios, PACK)
    halves = [
        m[..., 3 * TILE : 3 * TILE + HEAD_DIM],
        m[..., 3 * TILE + HEAD_DIM : 4 * TILE],
        m[..., 4 * TILE : 4 * TILE + HEAD_DIM],
    ]
    return jnp.concatenate(
        [
            jnp.concatenate([m[..., i * TILE : (i + 1) * TILE], halves[i]], -1).reshape(r, -1)
            for i in range(3)
        ],
        -1,
    )


def split_hidden(matrix, count, r):
    lead = matrix.shape[0]
    return matrix.reshape(lead, count, -1, r).transpose(0, 2, 1, 3).reshape(lead, -1)


def join_hidden(matrix, count, r):
    lead = matrix.shape[0]
    return matrix.reshape(lead, -1, count, r).transpose(0, 2, 1, 3).reshape(lead, -1)


def on_device(
    tokens,
    segment,
    ln1_gain,
    ln1_bias,
    ln2_gain,
    ln2_bias,
    qkv_weight,
    qkv_bias,
    dense_weight,
    dense_bias,
    fc1_weight,
    fc1_bias,
    output_feed_weight,
    output_feed_bias,
    cotangent,
):
    rows, groups, d = tokens.shape
    units = lax.axis_size("unit")
    part = lax.axis_size("part")
    count = units * part * lax.axis_size("seq")
    trios = units // groups
    all_rows = rows * groups
    r = qkv_weight.shape[0]
    ff = fc1_weight.shape[1]
    blocks = ff // d
    c = lax.axis_index("part")
    unit = lax.axis_index("unit")

    vectors = (
        ln1_gain,
        ln1_bias,
        ln2_gain,
        ln2_bias,
        qkv_bias,
        dense_bias,
        fc1_bias,
        output_feed_bias,
    )
    widths = [v.shape[0] // r for v in vectors]
    held = sum(widths)
    vec = jnp.pad(jnp.concatenate(vectors), (0, r * (16 - held))).reshape(r, 16)
    vec = jnp.pad(vec, ((0, 0), (0, TILE - 16)))
    first_pack = jnp.concatenate([pack_columns(qkv_weight, trios), dense_weight, vec], 1)
    first = lax.all_gather(first_pack, ALL_AXES, axis=0, tiled=True)
    feed_blocks = output_feed_weight.reshape(blocks, r, d)
    second_pack = jnp.concatenate(
        [split_hidden(fc1_weight, count, r)] + [feed_blocks[b] for b in range(blocks)], 1
    )
    second = lax.all_gather(second_pack, ALL_AXES, axis=0, tiled=True)

    qkv_cols = trios * PACK
    qkv_full = first[:, :qkv_cols]
    dense_pad = jnp.pad(
        first[:, qkv_cols : qkv_cols + d].reshape(trios, d // trios, d),
        ((0, 0), (0, OPACK - d // trios), (0, 0)),
    )
    vec_full = first[:, qkv_cols + d : qkv_cols + d + 16].reshape(count, r * 16).astype(F32)
    vecs = []
    at = 0
    for w in widths:
        vecs.append(vec_full[:, at * r : (at + w) * r].reshape(1, count * w * r))
        at += w
    gain_one, bias_one, gain_two, bias_two, qkv_shift, dense_shift, up_shift, down_shift = vecs
    qkv_shift = pack_columns(qkv_shift, trios)
    up_shift = split_hidden(up_shift, count, r)

    x = tokens.transpose(1, 0, 2).reshape(all_rows, d).astype(F32)
    cot = cotangent.transpose(1, 0, 2).reshape(all_rows, d)
    cot_float = cot.astype(F32)
    centre = x - jnp.mean(x, -1, keepdims=True)
    spread = lax.rsqrt(jnp.mean(centre * centre, -1, keepdims=True) + EPSILON)
    xhat = centre * spread
    normed_one = (xhat * gain_one + bias_one).astype(BF)
    normed_two = (xhat * gain_two + bias_two).astype(BF)

    seg_rows = segment.T.reshape(all_rows, 1)
    token_pos = (unit * part + c) * rows + jnp.arange(rows, dtype=jnp.int32)
    token_pos = jnp.tile(token_pos, groups)[:, None]
    lane = jnp.arange(TILE, dtype=jnp.int32)[None, :]
    in_head = lane % HEAD_DIM
    freq = (in_head % (ROT // 2)).astype(F32)
    inverse = jnp.where(in_head < ROT, jnp.exp(freq * (-2.0 * math.log(10000.0) / ROT)), 0.0)
    angles = (token_pos - seg_rows).astype(F32) * inverse
    cos = jnp.cos(angles)
    sin = jnp.sin(angles) * jnp.where(in_head < ROT // 2, -1.0, 1.0)
    aux = jnp.where(lane == HEAD_DIM, seg_rows // 64, 0) + jnp.where(
        lane == HEAD_DIM + 1, seg_rows % 64, 0
    )

    packed = project(
        normed_one, qkv_full, qkv_shift, cos, sin, aux.astype(F32), rows, trios, groups
    )

    def exchange(blocks_out):
        width = blocks_out.shape[-1]
        return lax.all_to_all(
            blocks_out.reshape(units * rows, width), "unit", 0, 0, tiled=True
        ).reshape(units, rows, width)

    mine = exchange(packed)
    seg_mine = mine[:, :, 4 * TILE + HEAD_DIM : 4 * TILE + HEAD_DIM + 2].astype(jnp.int32)
    seg_mine = seg_mine[:, :, 0] * 64 + seg_mine[:, :, 1]
    meta = jnp.concatenate([seg_mine[:, 0], seg_mine[:, -1], c[None]])
    seg_mine = seg_mine[:, None, :]

    def shift_part(value, i):
        return lax.ppermute(value, "part", [(p, (p + i) % part) for p in range(part)])

    kv_own = mine[:, :, TILE:]
    kv = jnp.stack([kv_own] + [shift_part(kv_own, i) for i in range(1, part)])

    attended_grad = jnp.einsum(
        "sld,gkd->gslk", cot.reshape(groups, rows, d), dense_pad, preferred_element_type=F32
    ).astype(BF)
    dout = exchange(attended_grad)

    out_low, out_t, lse = attend_forward(meta, mine, kv, seg_mine)
    attended = exchange(out_low)

    up_full = second[:, :ff]
    down_full = jnp.concatenate(
        [second[:, ff + b * d : ff + (b + 1) * d] for b in range(blocks)], 0
    )
    hidden_pre = mm(normed_two, up_full) + up_shift
    cdf = 0.5 * (1.0 + lax.erf(hidden_pre * math.sqrt(0.5)))
    hidden_low = (hidden_pre * cdf).astype(BF)
    slope = cdf + hidden_pre * (
        jnp.exp(-0.5 * hidden_pre * hidden_pre) * (1.0 / math.sqrt(2.0 * math.pi))
    )
    pre_grad = (inner_back(cot, down_full) * slope).astype(BF)
    second_branch = mm(hidden_low, down_full) + down_shift
    down_grad = outer_sum(hidden_low, cot)
    up_grad = outer_sum(normed_two, pre_grad)
    up_shift_grad = jnp.sum(pre_grad.astype(F32), 0)
    normed_two_grad = inner_back(pre_grad, up_full)
    cot_sum = jnp.sum(cot_float, 0)

    mlp_grads = jnp.concatenate(
        [up_grad.astype(BF)] + [down_grad[b * d : (b + 1) * d].astype(BF) for b in range(blocks)],
        1,
    )
    mlp_sum = lax.psum_scatter(mlp_grads, ALL_AXES, scatter_dimension=0, tiled=True).astype(F32)

    attended = attended.reshape(trios, groups, rows, OPACK).transpose(1, 2, 0, 3)
    attended = attended.reshape(all_rows, trios * OPACK)
    branch_one = mm(attended, dense_pad.reshape(trios * OPACK, d)) + dense_shift
    output = (x + branch_one + second_branch).astype(BF)
    dense_grad = outer_sum(attended, cot).reshape(trios, OPACK, d)[:, : d // trios].reshape(d, d)

    own, others = attend_backward(meta, mine, dout, out_t, lse, kv, seg_mine)
    rest = own[:, :, TILE:].astype(F32)
    for i in range(1, part):
        rest = rest + shift_part(others[i - 1], i).astype(F32)
    back = exchange(jnp.concatenate([own[:, :, :TILE], rest.astype(BF)], -1))
    qkv_grad = unturn(back, cos, sin, rows, trios, groups)
    qkv_grad_w = outer_sum(normed_one, qkv_grad)
    qkv_shift_grad = unpack_columns(jnp.sum(qkv_grad.astype(F32), 0)[None], trios)
    normed_one_grad = inner_back(qkv_grad, qkv_full)

    def norm_back(grad, gain):
        gy = grad * gain
        part_in = spread * (
            gy - jnp.mean(gy, -1, keepdims=True) - xhat * jnp.mean(gy * xhat, -1, keepdims=True)
        )
        return part_in, jnp.sum(grad * xhat, 0), jnp.sum(grad, 0)

    in_one, gain_one_grad, bias_one_grad = norm_back(normed_one_grad, gain_one)
    in_two, gain_two_grad, bias_two_grad = norm_back(normed_two_grad, gain_two)
    tokens_grad = (cot_float + in_one + in_two).astype(BF)

    vec_grads = [
        gain_one_grad,
        bias_one_grad,
        gain_two_grad,
        bias_two_grad,
        qkv_shift_grad,
        cot_sum,
        join_hidden(up_shift_grad[None], count, r),
    ]
    vec_grads = jnp.concatenate([v.reshape(count, -1) for v in vec_grads], 1)
    vec_grads = jnp.pad(vec_grads, ((0, 0), (0, 16 * r - vec_grads.shape[1])))
    vec_grads = jnp.pad(vec_grads.reshape(d, 16), ((0, 0), (0, TILE - 16)))
    last = jnp.concatenate(
        [qkv_grad_w.astype(BF), dense_grad.astype(BF), vec_grads.astype(BF)], 1
    )
    last_sum = lax.psum_scatter(last, ALL_AXES, scatter_dimension=0, tiled=True).astype(F32)

    def natural(value):
        return value.reshape(groups, rows, d).transpose(1, 0, 2)

    vec_sum = last_sum[:, qkv_cols + d : qkv_cols + d + 16].reshape(-1)
    vec_out = []
    at = 0
    for w in widths[:7]:
        vec_out.append(vec_sum[at * r : (at + w) * r])
        at += w
    down_sum = jnp.concatenate(
        [mlp_sum[:, ff + b * d : ff + (b + 1) * d] for b in range(blocks)], 0
    )
    return (
        natural(output),
        natural(tokens_grad),
        vec_out[0],
        vec_out[1],
        vec_out[2],
        vec_out[3],
        unpack_columns(last_sum[:, :qkv_cols], trios),
        vec_out[4],
        last_sum[:, qkv_cols : qkv_cols + d],
        vec_out[5],
        join_hidden(mlp_sum[:, :ff], count, r),
        vec_out[6],
        down_sum,
        vec_out[5],
    )


def solution(mesh):
    devices = mesh.devices
    seq_size, ctx_size = devices.shape
    ctx = ("unit", "part")
    tok = P(ctx, "seq", None)
    vec = P(ALL_AXES)
    mat = P(ALL_AXES, None)
    pairs = (vec, vec, vec, vec, mat, vec, mat, vec, mat, vec, mat, vec)

    def run(tokens, *rest):
        units = HEADS // TRIO * (tokens.shape[1] // seq_size)
        split = Mesh(devices.reshape(seq_size, units, ctx_size // units), ALL_AXES)
        mapped = jax.shard_map(
            on_device,
            mesh=split,
            in_specs=(tok, P(ctx, "seq")) + pairs + (tok,),
            out_specs=(tok, tok) + pairs,
            check_vma=False,
        )
        return mapped(tokens, *rest)

    return run
```

time: 1500 us -> 788 us (0.53)
  waiting for transfers between devices: 670 us -> 308 us
  matrix products: 338 us -> 59.8 us
  local copies, waits for them, and re-layouts: 272 us -> 78.9 us
  Pallas kernels: 0 us -> 153 us
  other arithmetic: 102 us -> 30.9 us
  starting transfers between devices: 1.38 us -> 30.8 us
  blocking collectives: 84.2 us -> 102 us
    reduce_scatter x5 -> x1, waiting for transfers between devices: 557 us -> 134 us  [on_device(): lax.psum_scatter(mlp_grads, ALL_AXES, scatter_dimension=0, tiled=True)]
    dot_general x60 -> x4, matrix products: 283 us -> 17.2 us  [the longest x3 15.3 us: mm(): return jnp.dot(a, b, preferred_element_type=F32)]
    pallas_call x0 -> x4, Pallas kernels: none -> 153 us  [the longest x1 72.4 us: attend_backward(): pl.pallas_call(functools.partial(backward_kernel, part, units), grid_spec...]
    all_to_all x0 -> x1, blocking collectives: none -> 102 us  [exchange(): lax.all_to_all(blocks_out.reshape(units * rows, width), 'unit', 0, 0, til...]
    unnamed x2 -> x0, blocking collectives: 84.2 us -> none
    unnamed x10 -> x5, waiting for transfers between devices: 2.53 us -> 72.7 us
    all_gather x5 -> x2, waiting for transfers between devices: 111 us -> 58 us  [the longest x1 57.9 us: on_device(): first = lax.all_gather(first_pack, ALL_AXES, axis=0, tiled=True)]
    unnamed x135 -> x103, local copies, waits for them, and re-layouts: 57.4 us -> 11.7 us
  transfers between devices with their start and end apart: 10 -> 9, of which waited for: 8 -> 5; matrix products, arithmetic and copies ran while one was open for 46% -> 16% of each run, Pallas kernels for 0% -> 19%
where the time goes in v1:
time: 788 us; the launch traced here: 778 us
  waiting for transfers between devices  308 us (39%)
  Pallas kernels  153 us (19%)
  blocking collectives  102 us (13%)
  local copies, waits for them, and re-layouts  78.9 us (10%)
  matrix products  59.8 us (8%)
  other arithmetic  30.9 us (4%)
  starting transfers between devices  30.8 us (4%)
  between operations  15.1 us (2%)
    reduce_scatter x1, waiting for transfers between devices, on_device(): lax.psum_scatter(mlp_grads, ALL_AXES, scatter_dimension=0, tiled=True)  134 us
    all_to_all x1, blocking collectives, exchange(): lax.all_to_all(blocks_out.reshape(units * rows, width), 'unit', 0, 0, til...  102 us
    unnamed x5, waiting for transfers between devices  72.7 us
    pallas_call x1, Pallas kernels, attend_backward(): pl.pallas_call(functools.partial(backward_kernel, part, units), grid_spec...  72.4 us
    pallas_call x1, Pallas kernels, attend_forward(): pl.pallas_call(functools.partial(forward_kernel, part, units), grid_spec=...  62.8 us
    all_gather x1, waiting for transfers between devices, on_device(): first = lax.all_gather(first_pack, ALL_AXES, axis=0, tiled=True)  57.9 us
    all_to_all x3, waiting for transfers between devices, exchange(): lax.all_to_all(blocks_out.reshape(units * rows, width), 'unit', 0, 0, til...  43.5 us
    dot_general x3, matrix products, inner_back(): lax.dot_general(grad_rows, weight, (((1,), (1,)), ((), ())), preferred_el...  25.9 us
  transfers between devices with their start and end apart: 9, of which 5 were waited for; matrix products, arithmetic and copies ran while one was open for 16% of the time, Pallas kernels for 19%

profile of v1, /device:TPU:0, one launch (start us, length us, event | category | flops | bytes accessed | tf_op | source)
XLA Modules:
  0.0 778.3 jit_solution(11200081745468945962)
XLA Ops:
  8.5 5.4 concatenate.66
  14.3 1.4 fusion.29
  15.9 2.1 reshape.453
  18.2 1.3 reshape.454
  21.0 1.5 multiply_reduce_fusion.4
  23.4 1.1 add_convert_fusion.4.aux_ref
  24.5 1.8 fusion.28
  26.3 57.9 %all-gather.3.cloned.1.call-done = bf16[768,3456]{1,0:T(8,128)(2,1)} async-done(((bf16[24,3456]{1,0:T(8,128)(2,1)}), bf16[768,3456]{1,0:T(8,128)(2,1)}) %all-gather.3.cloned.1.call-update) | async-done | bytes 5308432 | tf_op jit(solution)/shard_map/all_gather | solution.py:514
  87.4 4.3 slice.317.w_ref
  91.7 1.7 add_convert_fusion.3
  93.5 10.1 %project.1 = bf16[8,256,640]{2,1,0:T(8,128)(2,1)} custom-call(bf16[512,768]{1,0:T(8,128)(2,1)} %get-tuple-element.40.x_ref, bf16[768,2560]{1,0:T(8,128)(2,1)} %slice.317.w_ref, f32[1,2560]{1,0:T(1,128)} %bitcast.127, f32[512,128]{1,0:T(8,128)} %get-tuple-element.74.cos_ref, f32[512,128]{1,0:T(8,128)} %get-tuple-element.73.sin_ref, ...), custom_call_target="tpu_custom_call" | custom-call | tf_op jit(solution)/shard_map/project/pallas_call | solution.py:78
  103.6 4.4 copy.85
  108.0 102.1 %all_to_all.27 = bf16[8,256,640]{1,2,0:T(8,128)(2,1)S(1)} all-to-all(bf16[8,256,640]{1,2,0:T(8,128)(2,1)} %copy.85), channel_id=1, replica_groups=mesh['seq'=2,'unit'=8,'part'=2] {'unit'}, dimensions={0} | all-to-all | bytes 5242880 | tf_op jit(solution)/shard_map/all_to_all | solution.py:566
  210.1 2.4 slice_bitcast_fusion
  212.5 1.3 slice.331
  214.9 2.0 fusion.21
  216.9 2.3 copy.94
  219.2 4.5 all-to-all-start.2
  223.7 2.6 copy.86.q_ref
  227.7 4.6 pad_maximum_fusion.1
  232.2 6.3 copy.87.kv_ref
  238.5 62.8 %attend_forward.1 = (bf16[8,256,256]{2,1,0:T(8,128)(2,1)}, f32[8,192,256]{2,1,0:T(8,128)}, f32[8,8,256]{2,1,0:T(8,128)}) custom-call(s32[17]{0:T(128)} %pad_add_fusion.meta, bf16[8,256,640]{2,1,0:T(8,128)(2,1)} %copy.86.q_ref, bf16[2,8,256,512]{3,2,1,0:T(8,128)(2,1)} %copy.87.kv_ref, s32[8,1,256]{2,1,0:T(1,128)} %fusion.67.seg_ref), custom_call_target="tpu_custom_call" | custom-call | flops 12884901888 | bytes 20000000 | tf_op jit(solution)/shard_map/attend_forward/pallas_call | solution.py:356
  301.4 72.4 %attend_backward.1 = (bf16[8,256,640]{2,1,0:T(8,128)(2,1)}, bf16[1,8,256,512]{3,2,1,0:T(8,128)(2,1)}) custom-call(s32[17]{0:T(128)} %pad_add_fusion.meta, bf16[8,256,640]{2,1,0:T(8,128)(2,1)} %copy.86.q_ref, bf16[8,256,256]{2,1,0:T(8,128)(2,1)} %all-to-all-done.2.do_ref, f32[8,192,256]{2,1,0:T(8,128)} %get-tuple-element.20.ot_ref, ...), custom_call_target="tpu_custom_call" | custom-call | flops 32212254720 | bytes 20000000 | tf_op jit(solution)/shard_map/attend_backward/pallas_call | solution.py:395
  373.8 16.6 %collective-permute-start.1 = (bf16[8,256,512]{2,1,0:T(8,128)(2,1)}, bf16[8,256,512]{2,1,0:T(8,128)(2,1)}, u32[]{:S(2)}, u32[]{:S(2)}) collective-permute-start(bf16[8,256,512]{2,1,0:T(8,128)(2,1)} %bitcast.138), channel_id=1, source_target_pairs={{0,1},{1,0},{2,3},{3,2},{4,5},{5,4},{6,7},{7,6},{8,9},{9,8},{10,11... | collective-permute-start | bytes 6291464 | tf_op jit(solution)/shard_map/ppermute | solution.py:577
  390.4 5.7 all-to-all-start.1
  396.1 1.1 slice.273
  397.2 2.9 add_convert_fusion
  400.0 1.8 pad_maximum_fusion.2
  401.8 20.2 %all-to-all-done.1 = bf16[8,256,256]{2,1,0:T(8,128)(2,1)S(1)} async-done(((bf16[8,256,256]{2,1,0:T(8,128)(2,1)}), bf16[8,256,256]{2,1,0:T(8,128)(2,1)S(1)}, u32[]{:S(2)}, u32[]{:S(2)}) %all-to-all-start.1) | async-done | bytes 1048608 | tf_op jit(solution)/shard_map/all_to_all | solution.py:566
  423.0 3.6 all-to-all-start.3
  429.8 2.8 fusion.43
  432.6 7.7 multiply_convert_fusion
  440.4 13.5 %fusion.52 = (bf16[3072]{0:T(1024)(128)(2,1)S(1)}, bf16[512,3072]{1,0:T(8,128)(2,1)}) fusion(f32[512,3072]{1,0:T(8,128)S(1)} %get-tuple-element.84, f32[3072]{0:T(1024)S(1)} %add.196, bf16[512,768]{1,0:T(8,128)(2,1)S(1)} %bitcast.114, bf16[768,768]{1,0:T(8,128)(2,1)S(1)} %get-tuple-element.43, bf16[768,768]{1,0:T(8,128)(2,1)S(1)} %get-tuple-element.44, ...), kind=kOutput, calls=%fused_computation.132 | convolution fusion | flops 2453664768 | bytes 14960640 | tf_op jit(solution)/shard_map/dot_general | solution.py:44
  454.1 2.0 copy.88
  456.1 1.2 copy.111
  457.3 2.3 copy.98
  459.6 2.2 fusion.53
  461.8 1.1 slice.393
  462.9 23.4 %all-to-all-done.3.in_ref = bf16[8,256,640]{2,1,0:T(8,128)(2,1)S(1)} async-done(((bf16[8,256,640]{2,1,0:T(8,128)(2,1)}), bf16[8,256,640]{2,1,0:T(8,128)(2,1)S(1)}, u32[]{:S(2)}, u32[]{:S(2)}) %all-to-all-start.3) | async-done | bytes 2621472 | tf_op jit(solution)/shard_map/all_to_all | solution.py:566
  486.3 1.5 copy-done
  487.7 7.6 unturn.1
  495.3 2.4 reduce.6
  497.8 5.2 convolution_convert_fusion.2
  503.5 4.5 fusion.40
  508.1 7.9 %multiply_reduce_fusion = (bf16[768]{0:T(1024)(128)(2,1)S(1)}, f32[512]{0:T(512)}, f32[512]{0:T(512)}, bf16[768]{0:T(1024)(128)(2,1)S(1)}, f32[512]{0:T(512)}, /...) fusion(f32[512,768]{1,0:T(8,128)S(1)} %copy-done.6, ...), kind=kOutput, calls=%fused_computation.33 | convolution fusion | flops 2421419008 | bytes 12603392 | tf_op jit(solution)/shard_map/dot_general | solution.py:44
  516.7 5.1 fusion.7
  522.0 4.7 convolution_convert_fusion
  526.7 4.5 fusion.8
  531.2 1.2 slice_dynamic-update-slice_fusion.3
  532.4 1.2 slice_dynamic-update-slice_fusion.2
  533.5 1.1 slice_dynamic-update-slice_fusion.1
  534.7 1.1 slice_dynamic-update-slice_fusion
  535.8 1.3 copy-done.9
  537.1 1.3 pad.24
  539.3 6.6 fusion.24
  546.0 1.0 fusion.17
  547.1 1.7 copy.122
  549.7 1.7 copy.121
  551.4 72.7 %reduce-scatter.7.cloned.1.call-done = bf16[24,3456]{1,0:T(8,128)(2,1)} async-done(((bf16[768,3456]{1,0:T(8,128)(2,1)}), bf16[24,3456]{1,0:T(8,128)(2,1)}) %reduce-scatter.7.cloned.1.call-update) | async-done | bytes 165904
  628.8 1.4 slice.357
  630.9 133.5 %reduce-scatter.5.cloned.1.call-done = bf16[24,6144]{1,0:T(8,128)(2,1)} async-done(((bf16[768,6144]{1,0:T(8,128)(2,1)}), bf16[24,6144]{1,0:T(8,128)(2,1)}) %reduce-scatter.5.cloned.1.call-update) | async-done | bytes 294928 | tf_op jit(solution)/shard_map/reduce_scatter | solution.py:612
  765.4 1.1 reshape.473
  766.5 1.2 copy.101
  767.8 2.6 reshape.474
  (216 shorter events, 24.8 us)
Async XLA Ops:
  7.2 77.1 %all-gather.3.cloned.1.call-start = ((), (), s32[]{:S(2)}) async-start(), calls=%async_computation.6 | async-start | bytes 5474304 | tf_op jit(solution)/shard_map/all_gather | solution.py:514
  8.2 11.3 %copy-start.25 = (bf16[96,768]{1,0:T(8,128)(2,1)S(1)}, bf16[96,768]{1,0:T(8,128)(2,1)}, u32[]{:S(2)}) copy-start(bf16[96,768]{1,0:T(8,128)(2,1)} %param.27) | copy-start | bytes 442372
  14.1 6.2 copy-start.2
  15.8 414.0 %all-gather.5.cloned.1.call-start = ((), (), s32[]{:S(2)}) async-start(), calls=%async_computation.7 | async-start | bytes 9732096 | tf_op jit(solution)/shard_map/all_gather | solution.py:519
  18.0 4.6 copy-start.34
  19.5 0.7 copy-start.24
  22.7 69.1 %copy-start.30 = (f32[1,2,2,128]{3,1,2,0:T(2,128)}, f32[1,2,2,128]{3,1,2,0:T(2,128)S(1)}, u32[]{:S(2)}) copy-start(f32[1,2,2,128]{3,1,2,0:T(2,128)S(1)} %copy.106) | copy-start | bytes 6148
  23.4 68.4 %copy-start.3 = (f32[2,256,768]{2,1,0:T(8,128)}, f32[2,256,768]{2,1,0:T(8,128)S(1)}, u32[]{:S(2)}) copy-start(f32[2,256,768]{2,1,0:T(8,128)S(1)} %copy.81) | copy-start | bytes 4718596
  87.3 4.4 copy-start.26
  210.1 4.8 copy-start.13
  212.5 15.1 %collective-permute-start = (bf16[8,256,512]{1,2,0:T(8,128)(2,1)}, bf16[8,256,512]{1,2,0:T(8,128)(2,1)}, u32[]{:S(2)}, u32[]{:S(2)}) collective-permute-start(bf16[8,256,512]{1,2,0:T(8,128)(2,1)} %get-tuple-element.47), channel_id=1, source_target_pairs={{0,1},{1,0},{2,3},{3,2},{4,5},{5,4},{6,7},{7,6},{8,9},{9,8},{10,11... | collective-permute-start | bytes 6291464 | tf_op jit(solution)/shard_map/ppermute | solution.py:577
  213.9 1.0 copy-start.8
  219.2 82.2 %all-to-all-start.2 = ((bf16[8,256,256]{2,1,0:T(8,128)(2,1)}), bf16[8,256,256]{2,1,0:T(8,128)(2,1)}, u32[]{:S(2)}, u32[]{:S(2)}) async-start(bf16[8,256,256]{2,1,0:T(8,128)(2,1)} %bitcast.109), calls=%async_computation.2 | async-start | bytes 2097152 | tf_op jit(solution)/shard_map/all_to_all | solution.py:566
  373.8 23.4 %collective-permute-start.1 = (bf16[8,256,512]{2,1,0:T(8,128)(2,1)}, bf16[8,256,512]{2,1,0:T(8,128)(2,1)}, u32[]{:S(2)}, u32[]{:S(2)}) collective-permute-start(bf16[8,256,512]{2,1,0:T(8,128)(2,1)} %bitcast.138), channel_id=1, source_target_pairs={{0,1},{1,0},{2,3},{3,2},{4,5},{5,4},{6,7},{7,6},{8,9},{9,8},{10,11... | collective-permute-start | bytes 6291464 | tf_op jit(solution)/shard_map/ppermute | solution.py:577
  390.4 31.6 %all-to-all-start.1 = ((bf16[8,256,256]{2,1,0:T(8,128)(2,1)}), bf16[8,256,256]{2,1,0:T(8,128)(2,1)S(1)}, u32[]{:S(2)}, u32[]{:S(2)}) async-start(bf16[8,256,256]{2,1,0:T(8,128)(2,1)} %get-tuple-element.19), calls=%async_computation.1 | async-start | bytes 2097152 | tf_op jit(solution)/shard_map/all_to_all | solution.py:566
  422.0 1.0 copy-start.12
  423.0 63.3 %all-to-all-start.3 = ((bf16[8,256,640]{2,1,0:T(8,128)(2,1)}), bf16[8,256,640]{2,1,0:T(8,128)(2,1)S(1)}, u32[]{:S(2)}, u32[]{:S(2)}) async-start(bf16[8,256,640]{2,1,0:T(8,128)(2,1)} %pad_maximum_fusion.2), calls=%async_computation.3 | async-start | bytes 5242880 | tf_op jit(solution)/shard_map/all_to_all | solution.py:566
  426.6 197.4 %reduce-scatter.7.cloned.1.call-start = ((), (), s32[]{:S(2)}) async-start(), calls=%async_computation.9 | async-start | bytes 5474304
  429.7 97.0 %copy-start.32 = (f32[768]{0:T(1024)}, f32[768]{0:T(1024)S(1)}, u32[]{:S(2)}) copy-start(f32[768]{0:T(1024)S(1)} %mul.190) | copy-start | bytes 9220
  429.8 2.9 copy-start.5
  432.6 7.7 copy-start.19
  432.6 7.7 copy-start.20
  432.6 7.7 copy-start.21
  432.6 7.7 copy-start.22
  432.6 7.7 copy-start.14
  486.3 1.5 copy-start
  495.3 2.5 copy-start.1
  503.5 4.5 copy-start.6
  503.5 4.5 copy-start.27
  503.5 4.5 copy-start.40
  508.0 8.0 %copy-start.16 = (f32[512,768]{1,0:T(8,128)}, f32[512,768]{1,0:T(8,128)S(1)}, u32[]{:S(2)}) copy-start(f32[512,768]{1,0:T(8,128)S(1)} %fusion.40) | copy-start | bytes 4718596
  508.1 8.3 %copy-start.29 = (bf16[32,24]{1,0:T(8,128)(2,1)S(1)}, bf16[32,24]{1,0:T(8,128)(2,1)}, u32[]{:S(2)}) copy-start(bf16[32,24]{1,0:T(8,128)(2,1)} %reshape.466) | copy-start | bytes 4612
  508.1 8.6 %copy-start.10 = (bf16[4,192,768]{2,1,0:T(8,128)(2,1)S(1)}, bf16[4,192,768]{2,1,0:T(8,128)(2,1)}, u32[]{:S(2)}) copy-start(bf16[4,192,768]{2,1,0:T(8,128)(2,1)} %slice.393) | copy-start | bytes 3538948
  521.9 242.6 %reduce-scatter.5.cloned.1.call-start = ((), (), s32[]{:S(2)}) async-start(), calls=%async_computation.8 | async-start | bytes 9732096 | tf_op jit(solution)/shard_map/reduce_scatter | solution.py:612
  521.9 4.7 copy-start.7
  521.9 4.7 copy-start.41
  535.8 1.3 copy-start.9
  539.3 6.6 copy-start.4
  539.3 6.6 copy-start.11
  539.3 6.6 copy-start.15
  545.9 2.8 copy-start.38
  545.9 2.8 copy-start.37
  546.0 2.8 copy-start.36
  546.0 2.8 copy-start.35
  546.0 2.8 copy-start.18
  546.0 2.8 copy-start.28
  546.0 2.8 copy-start.31
  546.0 2.8 copy-start.33
  547.1 1.8 copy-start.17
  627.3 143.8 %copy-start.39 = (f32[24]{0:T(128)}, f32[24]{0:T(128)S(1)}, u32[]{:S(2)}) copy-start(f32[24]{0:T(128)S(1)} %get-tuple-element.119) | copy-start | bytes 292
  766.5 3.8 copy-start.23
Sparse Core Ops, SparseCore 0:
  15.9 68.3 all-gather.2
  87.8 118.8 all-gather.4
  522.0 101.9 reduce-scatter.6
  629.8 134.6 reduce-scatter.4

commit v2 on v1

--- a/solution.py
+++ b/solution.py
@@ -59,65 +59,94 @@
     return tile * cos + partner * sin
 
 
-def project_kernel(x_ref, w_ref, b_ref, cos_ref, sin_ref, aux_ref, out_ref):
-    y = mm(x_ref[...], w_ref[...]) + b_ref[...]
-    cos = cos_ref[...]
-    sin = sin_ref[...]
+def turn_tables(cos_rows, sin_rows):
+    rows = cos_rows.shape[1]
+    rest = HEAD_DIM - ROT
+    cos_head = [cos_rows, cos_rows, jnp.ones((rest, rows), F32)]
+    sin_head = [-sin_rows, sin_rows, jnp.zeros((rest, rows), F32)]
+    return jnp.concatenate(cos_head * 2, 0).T, jnp.concatenate(sin_head * 2, 0).T
+
+
+def project_kernel(
+    tok_ref, w_ref, b_ref, gain_ref, bias_ref, cos_ref, sin_ref, out_ref, norm_ref, hat_ref
+):
+    x = tok_ref[0].astype(F32)
+    centre = x - jnp.mean(x, -1, keepdims=True)
+    spread = jnp.mean(centre * centre, -1, keepdims=True)
+    hat = centre * lax.rsqrt(spread + EPSILON)
+    normed = (hat * gain_ref[...] + bias_ref[...]).astype(BF)
+    hat_ref[0] = hat.astype(BF)
+    norm_ref[0] = normed
+    y = mm(normed, w_ref[...]) + b_ref[...]
+    cos, sin = turn_tables(cos_ref[0], sin_ref[0])
     for t in range(5):
         tile = y[:, t * TILE : (t + 1) * TILE]
         if t in (0, 1, 3):
             tile = turn(tile, cos, sin)
-        if t == 4:
-            tile = tile + aux_ref[...]
         out_ref[0, :, t * TILE : (t + 1) * TILE] = tile.astype(BF)
 
 
-def project(xn, weight, bias, cos, sin, aux, rows, trios, groups):
-    d = xn.shape[1]
-    row_spec = pl.BlockSpec((rows, TILE), lambda g, s: (s, 0))
+def project(toks, weight, bias, gain, offset, cos, sin):
+    units, rows, d = toks.shape
+    tok_spec = pl.BlockSpec((1, rows, d), lambda j: (j, 0, 0))
+    row_spec = pl.BlockSpec((1, d), lambda j: (0, 0))
+    turn_spec = pl.BlockSpec((1, ROT // 2, rows), lambda j: (j, 0, 0))
     return pl.pallas_call(
         project_kernel,
-        grid=(trios, groups),
+        grid=(units,),
         in_specs=[
-            pl.BlockSpec((rows, d), lambda g, s: (s, 0)),
-            pl.BlockSpec((d, PACK), lambda g, s: (0, g)),
-            pl.BlockSpec((1, PACK), lambda g, s: (0, g)),
+            tok_spec,
+            pl.BlockSpec((d, PACK), lambda j: (0, 0)),
+            pl.BlockSpec((1, PACK), lambda j: (0, 0)),
             row_spec,
             row_spec,
-            row_spec,
+            turn_spec,
+            turn_spec,
         ],
-        out_specs=pl.BlockSpec((1, rows, PACK), lambda g, s: (g * groups + s, 0, 0)),
-        out_shape=jax.ShapeDtypeStruct((trios * groups, rows, PACK), BF),
-        compiler_params=params_of("arbitrary", "arbitrary"),
+        out_specs=[pl.BlockSpec((1, rows, PACK), lambda j: (j, 0, 0)), tok_spec, tok_spec],
+        out_shape=[
+            jax.ShapeDtypeStruct((units, rows, PACK), BF),
+            jax.ShapeDtypeStruct((units, rows, d), BF),
+            jax.ShapeDtypeStruct((units, rows, d), BF),
+        ],
+        compiler_params=params_of("arbitrary"),
+        cost_estimate=pl.CostEstimate(
+            flops=2 * units * rows * d * PACK,
+            bytes_accessed=2 * units * rows * (3 * d + PACK),
+            transcendentals=0,
+        ),
         name="project",
-    )(xn, weight, bias, cos, sin, aux)
-
-
-def unturn_kernel(in_ref, cos_ref, sin_ref, out_ref):
-    cos = cos_ref[...]
-    sin = sin_ref[...]
+    )(toks, weight, bias, gain, offset, cos, sin)
+
+
+def unturn_kernel(*refs):
+    own_ref, cos_ref, sin_ref, out_ref = refs[0], refs[-3], refs[-2], refs[-1]
+    others = refs[1:-3]
+    cos, sin = turn_tables(cos_ref[0], sin_ref[0])
     for t in range(5):
-        tile = in_ref[0, :, t * TILE : (t + 1) * TILE].astype(F32)
+        tile = own_ref[0, :, t * TILE : (t + 1) * TILE].astype(F32)
+        if t > 0:
+            for other in others:
+                tile = tile + other[0, :, (t - 1) * TILE : t * TILE].astype(F32)
         if t in (0, 1, 3):
             tile = turn(tile, cos, -sin)
-        out_ref[:, t * TILE : (t + 1) * TILE] = tile.astype(BF)
-
-
-def unturn(packed, cos, sin, rows, trios, groups):
-    row_spec = pl.BlockSpec((rows, TILE), lambda g, s: (s, 0))
+        out_ref[0, :, t * TILE : (t + 1) * TILE] = tile.astype(BF)
+
+
+def unturn(own, others, cos, sin):
+    units, rows, unused = own.shape
+    turn_spec = pl.BlockSpec((1, ROT // 2, rows), lambda j: (j, 0, 0))
+    own_spec = pl.BlockSpec((1, rows, PACK), lambda j: (j, 0, 0))
+    other_spec = pl.BlockSpec((1, rows, PACK - TILE), lambda j: (j, 0, 0))
     return pl.pallas_call(
         unturn_kernel,
-        grid=(trios, groups),
-        in_specs=[
-            pl.BlockSpec((1, rows, PACK), lambda g, s: (g * groups + s, 0, 0)),
-            row_spec,
-            row_spec,
-        ],
-        out_specs=pl.BlockSpec((rows, PACK), lambda g, s: (s, g)),
-        out_shape=jax.ShapeDtypeStruct((rows * groups, trios * PACK), BF),
-        compiler_params=params_of("arbitrary", "arbitrary"),
+        grid=(units,),
+        in_specs=[own_spec] + [other_spec] * len(others) + [turn_spec, turn_spec],
+        out_specs=own_spec,
+        out_shape=jax.ShapeDtypeStruct(own.shape, BF),
+        compiler_params=params_of("arbitrary"),
         name="unturn",
-    )(packed, cos, sin)
+    )(own, *others, cos, sin)
 
 
 def flip(tile):
@@ -205,20 +234,22 @@
         k2 = kv_ref[where[0], where[1], :, 2 * TILE : 3 * TILE]
         if masked:
             live = live_of(seg_row, kb * rows, diag * rows, rows)
+        scores = [mm(k2 if h == 2 else k01, qb[h]) for h in range(TRIO)]
+        if masked:
+            scores = [jnp.where(live, score, NEG_BIG) for score in scores]
+        old = top[0:TRIO]
+        new = jnp.concatenate([jnp.max(score, 0, keepdims=True) for score in scores], 0)
+        new = jnp.maximum(old, new)
+        factor = jnp.exp(old - new)
+        weights = [jnp.exp(scores[h] - new[h : h + 1]) for h in range(TRIO)]
+        if masked:
+            weights = [jnp.where(live, weight, 0.0) for weight in weights]
+        sums = [jnp.sum(weight, 0, keepdims=True) for weight in weights]
+        top[0:TRIO] = new
+        total[0:TRIO] = total[0:TRIO] * factor + jnp.concatenate(sums, 0)
         for h in range(TRIO):
-            score = mm(k2 if h == 2 else k01, qb[h])
-            if masked:
-                score = jnp.where(live, score, NEG_BIG)
-            old = top[h : h + 1]
-            new = jnp.maximum(old, jnp.max(score, 0, keepdims=True))
-            weight = jnp.exp(score - new)
-            if masked:
-                weight = jnp.where(live, weight, 0.0)
-            factor = jnp.exp(old - new)
-            top[h : h + 1] = new
-            total[h : h + 1] = total[h : h + 1] * factor + jnp.sum(weight, 0, keepdims=True)
             vth = vt[kb, h * HEAD_DIM : (h + 1) * HEAD_DIM]
-            acc[h] = acc[h] * factor + mm(vth, weight.astype(BF))
+            acc[h] = acc[h] * factor[h : h + 1] + mm(vth, weights[h].astype(BF))
 
     block_loop(meta, part, units, rows, step)
     out = [acc[h] / total[h : h + 1] for h in range(TRIO)]
@@ -496,96 +527,115 @@
     c = lax.axis_index("part")
     unit = lax.axis_index("unit")
 
-    vectors = (
-        ln1_gain,
-        ln1_bias,
-        ln2_gain,
-        ln2_bias,
-        qkv_bias,
-        dense_bias,
-        fc1_bias,
-        output_feed_bias,
-    )
-    widths = [v.shape[0] // r for v in vectors]
-    held = sum(widths)
-    vec = jnp.pad(jnp.concatenate(vectors), (0, r * (16 - held))).reshape(r, 16)
-    vec = jnp.pad(vec, ((0, 0), (0, TILE - 16)))
-    first_pack = jnp.concatenate([pack_columns(qkv_weight, trios), dense_weight, vec], 1)
-    first = lax.all_gather(first_pack, ALL_AXES, axis=0, tiled=True)
+    seq = lax.axis_index("seq")
+    seqs = lax.axis_size("seq")
+    place = (seq * units + unit) * part + c
+
+    def exchange(blocks_out):
+        width = blocks_out.shape[-1]
+        return lax.all_to_all(
+            blocks_out.reshape(-1, width), "unit", 0, 0, tiled=True
+        ).reshape(blocks_out.shape)
+
+    def shift(value, axis, i):
+        n = lax.axis_size(axis)
+        return lax.ppermute(value, axis, [(p, (p + i) % n) for p in range(n)])
+
+    def gather_small(value, axis):
+        n = lax.axis_size(axis)
+        me = lax.axis_index(axis)
+        got = [value] + [shift(value, axis, i) for i in range(1, n)]
+        if n == 2:
+            return jnp.where(me == 0, jnp.stack(got), jnp.stack(got[::-1]))
+        got = jnp.stack(got)
+        return jnp.stack(
+            [lax.dynamic_index_in_dim(got, (me - k + n) % n, 0, False) for k in range(n)]
+        )
+
+    def scatter_small(value, axis):
+        n = lax.axis_size(axis)
+        me = lax.axis_index(axis)
+        total = lax.dynamic_index_in_dim(value, me, 0, False).astype(F32)
+        for i in range(1, n):
+            piece = lax.dynamic_index_in_dim(value, (me + i) % n, 0, False)
+            total = total + shift(piece, axis, i).astype(F32)
+        return total.astype(BF)
+
+    vectors = (ln1_gain, ln1_bias, ln2_gain, ln2_bias, dense_bias, output_feed_bias)
+    vec = jnp.concatenate(
+        [v.reshape(r, 1) for v in vectors] + [qkv_bias.reshape(r, 3), fc1_bias.reshape(r, blocks)],
+        1,
+    )
+    vec = jnp.pad(vec, ((0, 0), (0, TILE - vec.shape[1])))
+    qkv_local = pack_columns(qkv_weight, trios)
+    seg_rows = segment.T
+    seg_pack = jnp.concatenate([seg_rows // 64, seg_rows % 64], 1).astype(BF)
+    seg_pack = jnp.pad(seg_pack[:, None, :], ((0, 0), (0, 7), (0, PACK + TILE - 2 * rows)))
+    early = []
+    for u in range(units):
+        g = u // groups
+        trio_cols = jnp.concatenate([qkv_local[:, g * PACK : (g + 1) * PACK], vec], 1)
+        early += [trio_cols, seg_pack[u % groups]]
+    early = exchange(jnp.concatenate(early, 0).reshape(units, r + 8, PACK + TILE))
+    token_rows = tokens.transpose(1, 0, 2)
+    toks = exchange(jnp.concatenate([token_rows] * trios, 0))
+
+    seg_mine = early[:, r, : 2 * rows].astype(jnp.int32)
+    seg_mine = seg_mine[:, :rows] * 64 + seg_mine[:, rows:]
+    meta = jnp.concatenate([seg_mine[:, 0], seg_mine[:, -1], c[None]])
+    seg_mine = seg_mine[:, None, :]
+    trio_full = gather_small(gather_small(early[:, :r], "seq"), "part")
+    trio_full = trio_full.transpose(1, 2, 0, 3, 4).reshape(d, PACK + TILE)
+    vec_full = trio_full[:, PACK:].astype(F32)
+    vec_rows = vec_full[:, :8].T
+    gain_one, bias_one, gain_two, bias_two, dense_shift, down_shift = (
+        vec_rows[i : i + 1] for i in range(6)
+    )
+    qkv_shift = pack_columns(vec_full[:, 6:9].reshape(1, 3 * d), trios).reshape(trios, PACK)
+    qkv_shift = lax.dynamic_slice_in_dim(qkv_shift, unit // groups, 1, 0)
+    up_shift = split_hidden(vec_full[:, 9 : 9 + blocks].reshape(1, ff), count, r)
+
     feed_blocks = output_feed_weight.reshape(blocks, r, d)
     second_pack = jnp.concatenate(
-        [split_hidden(fc1_weight, count, r)] + [feed_blocks[b] for b in range(blocks)], 1
+        [split_hidden(fc1_weight, count, r)]
+        + [feed_blocks[b] for b in range(blocks)]
+        + [dense_weight],
+        1,
     )
     second = lax.all_gather(second_pack, ALL_AXES, axis=0, tiled=True)
-
-    qkv_cols = trios * PACK
-    qkv_full = first[:, :qkv_cols]
+    qkv_full = lax.all_gather(qkv_local, ALL_AXES, axis=0, tiled=True)
     dense_pad = jnp.pad(
-        first[:, qkv_cols : qkv_cols + d].reshape(trios, d // trios, d),
+        second[:, 2 * ff :].reshape(trios, d // trios, d),
         ((0, 0), (0, OPACK - d // trios), (0, 0)),
     )
-    vec_full = first[:, qkv_cols + d : qkv_cols + d + 16].reshape(count, r * 16).astype(F32)
-    vecs = []
-    at = 0
-    for w in widths:
-        vecs.append(vec_full[:, at * r : (at + w) * r].reshape(1, count * w * r))
-        at += w
-    gain_one, bias_one, gain_two, bias_two, qkv_shift, dense_shift, up_shift, down_shift = vecs
-    qkv_shift = pack_columns(qkv_shift, trios)
-    up_shift = split_hidden(up_shift, count, r)
-
-    x = tokens.transpose(1, 0, 2).reshape(all_rows, d).astype(F32)
+
+    block_start = (jnp.arange(units, dtype=jnp.int32) * part + c) * rows
+    positions = block_start[:, None, None] + jnp.arange(rows, dtype=jnp.int32) - seg_mine
+    freq = jnp.arange(ROT // 2, dtype=F32)
+    inverse = jnp.exp(freq * (-2.0 * math.log(10000.0) / ROT))
+    angles = positions.astype(F32) * inverse[None, :, None]
+    cos = jnp.cos(angles)
+    sin = jnp.sin(angles)
+
+    packed, normed_one, hat_one = project(
+        toks, trio_full, qkv_shift, gain_one, bias_one, cos, sin
+    )
+    kv_own = packed[:, :, TILE:]
+    kv = jnp.stack([kv_own] + [shift(kv_own, "part", i) for i in range(1, part)])
+    out_low, out_t, lse = attend_forward(meta, packed, kv, seg_mine)
+    attended = exchange(out_low)
+
+    x = token_rows.reshape(all_rows, d).astype(F32)
     cot = cotangent.transpose(1, 0, 2).reshape(all_rows, d)
     cot_float = cot.astype(F32)
     centre = x - jnp.mean(x, -1, keepdims=True)
     spread = lax.rsqrt(jnp.mean(centre * centre, -1, keepdims=True) + EPSILON)
     xhat = centre * spread
-    normed_one = (xhat * gain_one + bias_one).astype(BF)
     normed_two = (xhat * gain_two + bias_two).astype(BF)
-
-    seg_rows = segment.T.reshape(all_rows, 1)
-    token_pos = (unit * part + c) * rows + jnp.arange(rows, dtype=jnp.int32)
-    token_pos = jnp.tile(token_pos, groups)[:, None]
-    lane = jnp.arange(TILE, dtype=jnp.int32)[None, :]
-    in_head = lane % HEAD_DIM
-    freq = (in_head % (ROT // 2)).astype(F32)
-    inverse = jnp.where(in_head < ROT, jnp.exp(freq * (-2.0 * math.log(10000.0) / ROT)), 0.0)
-    angles = (token_pos - seg_rows).astype(F32) * inverse
-    cos = jnp.cos(angles)
-    sin = jnp.sin(angles) * jnp.where(in_head < ROT // 2, -1.0, 1.0)
-    aux = jnp.where(lane == HEAD_DIM, seg_rows // 64, 0) + jnp.where(
-        lane == HEAD_DIM + 1, seg_rows % 64, 0
-    )
-
-    packed = project(
-        normed_one, qkv_full, qkv_shift, cos, sin, aux.astype(F32), rows, trios, groups
-    )
-
-    def exchange(blocks_out):
-        width = blocks_out.shape[-1]
-        return lax.all_to_all(
-            blocks_out.reshape(units * rows, width), "unit", 0, 0, tiled=True
-        ).reshape(units, rows, width)
-
-    mine = exchange(packed)
-    seg_mine = mine[:, :, 4 * TILE + HEAD_DIM : 4 * TILE + HEAD_DIM + 2].astype(jnp.int32)
-    seg_mine = seg_mine[:, :, 0] * 64 + seg_mine[:, :, 1]
-    meta = jnp.concatenate([seg_mine[:, 0], seg_mine[:, -1], c[None]])
-    seg_mine = seg_mine[:, None, :]
-
-    def shift_part(value, i):
-        return lax.ppermute(value, "part", [(p, (p + i) % part) for p in range(part)])
-
-    kv_own = mine[:, :, TILE:]
-    kv = jnp.stack([kv_own] + [shift_part(kv_own, i) for i in range(1, part)])
-
     attended_grad = jnp.einsum(
         "sld,gkd->gslk", cot.reshape(groups, rows, d), dense_pad, preferred_element_type=F32
     ).astype(BF)
-    dout = exchange(attended_grad)
-
-    out_low, out_t, lse = attend_forward(meta, mine, kv, seg_mine)
-    attended = exchange(out_low)
+    dout = exchange(attended_grad.reshape(units, rows, OPACK))
 
     up_full = second[:, :ff]
     down_full = jnp.concatenate(
@@ -605,11 +655,13 @@
     normed_two_grad = inner_back(pre_grad, up_full)
     cot_sum = jnp.sum(cot_float, 0)
 
-    mlp_grads = jnp.concatenate(
-        [up_grad.astype(BF)] + [down_grad[b * d : (b + 1) * d].astype(BF) for b in range(blocks)],
-        1,
-    )
-    mlp_sum = lax.psum_scatter(mlp_grads, ALL_AXES, scatter_dimension=0, tiled=True).astype(F32)
+    def norm_back(grad, gain):
+        gy = grad * gain
+        return spread * (
+            gy - jnp.mean(gy, -1, keepdims=True) - xhat * jnp.mean(gy * xhat, -1, keepdims=True)
+        )
+
+    in_two = norm_back(normed_two_grad, gain_two)
 
     attended = attended.reshape(trios, groups, rows, OPACK).transpose(1, 2, 0, 3)
     attended = attended.reshape(all_rows, trios * OPACK)
@@ -617,71 +669,90 @@
     output = (x + branch_one + second_branch).astype(BF)
     dense_grad = outer_sum(attended, cot).reshape(trios, OPACK, d)[:, : d // trios].reshape(d, d)
 
-    own, others = attend_backward(meta, mine, dout, out_t, lse, kv, seg_mine)
-    rest = own[:, :, TILE:].astype(F32)
-    for i in range(1, part):
-        rest = rest + shift_part(others[i - 1], i).astype(F32)
-    back = exchange(jnp.concatenate([own[:, :, :TILE], rest.astype(BF)], -1))
-    qkv_grad = unturn(back, cos, sin, rows, trios, groups)
-    qkv_grad_w = outer_sum(normed_one, qkv_grad)
-    qkv_shift_grad = unpack_columns(jnp.sum(qkv_grad.astype(F32), 0)[None], trios)
-    normed_one_grad = inner_back(qkv_grad, qkv_full)
-
-    def norm_back(grad, gain):
-        gy = grad * gain
-        part_in = spread * (
-            gy - jnp.mean(gy, -1, keepdims=True) - xhat * jnp.mean(gy * xhat, -1, keepdims=True)
-        )
-        return part_in, jnp.sum(grad * xhat, 0), jnp.sum(grad, 0)
-
-    in_one, gain_one_grad, bias_one_grad = norm_back(normed_one_grad, gain_one)
-    in_two, gain_two_grad, bias_two_grad = norm_back(normed_two_grad, gain_two)
+    vec_grads = jnp.concatenate(
+        [
+            jnp.sum(normed_two_grad * xhat, 0)[None],
+            jnp.sum(normed_two_grad, 0)[None],
+            cot_sum[None],
+            jnp.zeros((5, d), F32),
+        ],
+        0,
+    ).T
+    up_shift_grad = join_hidden(up_shift_grad[None], count, r).reshape(d, blocks)
+    vec_grads = jnp.concatenate(
+        [vec_grads, up_shift_grad, jnp.zeros((d, TILE - 8 - blocks), F32)], 1
+    )
+    mlp_grads = jnp.concatenate(
+        [up_grad.astype(BF)]
+        + [down_grad[b * d : (b + 1) * d].astype(BF) for b in range(blocks)]
+        + [dense_grad.astype(BF), vec_grads.astype(BF)],
+        1,
+    )
+    mlp_grads, kv = lax.optimization_barrier((mlp_grads, kv))
+    mlp_sum = lax.psum_scatter(mlp_grads, ALL_AXES, scatter_dimension=0, tiled=True).astype(F32)
+
+    own, others = attend_backward(meta, packed, dout, out_t, lse, kv, seg_mine)
+    others = [shift(others[i - 1], "part", i) for i in range(1, part)]
+    qkv_grad = unturn(own, others, cos, sin)
+    back = exchange(qkv_grad)
+
+    grad_rows = qkv_grad.reshape(units * rows, PACK)
+    trio_weight = trio_full[:, :PACK].astype(F32)
+    trio_grad = outer_sum(normed_one.reshape(units * rows, d), grad_rows)
+    hat_grad = outer_sum(hat_one.reshape(units * rows, d), grad_rows)
+    shift_grad = jnp.sum(grad_rows.astype(F32), 0)[None]
+    late_vec = jnp.concatenate(
+        [
+            jnp.sum(trio_weight * hat_grad, 1, keepdims=True),
+            jnp.sum(trio_weight * shift_grad, 1, keepdims=True),
+            jnp.zeros((d, TILE - 2), F32),
+        ],
+        1,
+    )
+    late = jnp.concatenate([trio_grad.astype(BF), late_vec.astype(BF)], 1)
+    late = late.reshape(seqs, units, part, r, PACK + TILE)
+    shift_rows = jnp.pad(shift_grad.astype(BF), ((0, 7), (0, TILE)))
+    late = jnp.concatenate(
+        [late, jnp.broadcast_to(shift_rows, (seqs, units, part) + shift_rows.shape)], 3
+    )
+    late = scatter_small(late.transpose(2, 0, 1, 3, 4), "part")
+    late = exchange(scatter_small(late, "seq")).astype(F32)
+    late = jnp.sum(late.reshape(trios, groups, r + 8, PACK + TILE), 1)
+    qkv_weight_grad = unpack_columns(
+        late[:, :r, :PACK].transpose(1, 0, 2).reshape(r, trios * PACK), trios
+    )
+    late_vec = jnp.sum(late[:, :r, PACK : PACK + 2], 0)
+    qkv_shift_grad = unpack_columns(late[:, r, :PACK].reshape(1, trios * PACK), trios)[0]
+    qkv_shift_grad = lax.dynamic_slice_in_dim(qkv_shift_grad, place * 3 * r, 3 * r)
+
+    back = back.reshape(trios, groups, rows, PACK).transpose(1, 2, 0, 3)
+    normed_one_grad = inner_back(back.reshape(all_rows, trios * PACK), qkv_full)
+    in_one = norm_back(normed_one_grad, gain_one)
     tokens_grad = (cot_float + in_one + in_two).astype(BF)
-
-    vec_grads = [
-        gain_one_grad,
-        bias_one_grad,
-        gain_two_grad,
-        bias_two_grad,
-        qkv_shift_grad,
-        cot_sum,
-        join_hidden(up_shift_grad[None], count, r),
-    ]
-    vec_grads = jnp.concatenate([v.reshape(count, -1) for v in vec_grads], 1)
-    vec_grads = jnp.pad(vec_grads, ((0, 0), (0, 16 * r - vec_grads.shape[1])))
-    vec_grads = jnp.pad(vec_grads.reshape(d, 16), ((0, 0), (0, TILE - 16)))
-    last = jnp.concatenate(
-        [qkv_grad_w.astype(BF), dense_grad.astype(BF), vec_grads.astype(BF)], 1
-    )
-    last_sum = lax.psum_scatter(last, ALL_AXES, scatter_dimension=0, tiled=True).astype(F32)
 
     def natural(value):
         return value.reshape(groups, rows, d).transpose(1, 0, 2)
 
-    vec_sum = last_sum[:, qkv_cols + d : qkv_cols + d + 16].reshape(-1)
-    vec_out = []
-    at = 0
-    for w in widths[:7]:
-        vec_out.append(vec_sum[at * r : (at + w) * r])
-        at += w
     down_sum = jnp.concatenate(
         [mlp_sum[:, ff + b * d : ff + (b + 1) * d] for b in range(blocks)], 0
     )
+    vec_sum = mlp_sum[:, 2 * ff + d :]
+    cot_total = vec_sum[:, 2]
     return (
         natural(output),
         natural(tokens_grad),
-        vec_out[0],
-        vec_out[1],
-        vec_out[2],
-        vec_out[3],
-        unpack_columns(last_sum[:, :qkv_cols], trios),
-        vec_out[4],
-        last_sum[:, qkv_cols : qkv_cols + d],
-        vec_out[5],
+        late_vec[:, 0],
+        late_vec[:, 1],
+        vec_sum[:, 0],
+        vec_sum[:, 1],
+        qkv_weight_grad,
+        qkv_shift_grad,
+        mlp_sum[:, 2 * ff : 2 * ff + d],
+        cot_total,
         join_hidden(mlp_sum[:, :ff], count, r),
-        vec_out[6],
+        vec_sum[:, 8 : 8 + blocks].reshape(-1),
         down_sum,
-        vec_out[5],
+        cot_total,
     )
 
 

time: 788 us -> 578 us (0.73)
  waiting for transfers between devices: 308 us -> 184 us
  blocking collectives: 102 us -> 25.5 us
  Pallas kernels: 153 us -> 136 us
    reduce_scatter x1 -> x0, waiting for transfers between devices: 134 us -> none  [on_device(): lax.psum_scatter(mlp_grads, ALL_AXES, scatter_dimension=0, tiled=True)]
    all_to_all x3 -> x5, waiting for transfers between devices: 43.5 us -> 152 us  [exchange(): lax.all_to_all(blocks_out.reshape(-1, width), 'unit', 0, 0, tiled=True)]
    all_to_all x1, blocking collectives: 102 us -> 25.5 us  [exchange(): lax.all_to_all(blocks_out.reshape(-1, width), 'unit', 0, 0, tiled=True)]
    unnamed x5 -> x4, waiting for transfers between devices: 72.7 us -> 0.05 us
    all_gather x1, waiting for transfers between devices: 57.9 us -> 0.02 us  [on_device(): qkv_full = lax.all_gather(qkv_local, ALL_AXES, axis=0, tiled=True)]
    ppermute x2 -> x6, waiting for transfers between devices: 0.01 us -> 31.5 us  [shift(): return lax.ppermute(value, axis, [(p, (p + i) % n) for p in range(n)])]
    pallas_call x1, Pallas kernels: 62.8 us -> 46 us  [attend_forward(): pl.pallas_call(functools.partial(forward_kernel, part, units), grid_spec=...]
    concatenate x1, local copies, waits for them, and re-layouts: 1.1 us -> 16.5 us  [on_device(): jnp.concatenate([up_grad.astype(BF)] + [down_grad[b * d:(b + 1) * d].asty...]
  transfers between devices with their start and end apart: 9 -> 14, of which waited for: 5 -> 10; matrix products, arithmetic and copies ran while one was open for 16% -> 26% of each run, Pallas kernels for 19% -> 24%
where the time goes in v2:
time: 578 us; the launch traced here: 570 us
  waiting for transfers between devices  184 us (32%)
  Pallas kernels  136 us (24%)
  local copies, waits for them, and re-layouts  86.1 us (15%)
  matrix products  59.3 us (10%)
  starting transfers between devices  36.5 us (6%)
  other arithmetic  27.7 us (5%)
  blocking collectives  25.5 us (4%)
  between operations  15.3 us (3%)
    all_to_all x5, waiting for transfers between devices, exchange(): lax.all_to_all(blocks_out.reshape(-1, width), 'unit', 0, 0, tiled=True)  152 us
    pallas_call x1, Pallas kernels, attend_backward(): pl.pallas_call(functools.partial(backward_kernel, part, units), grid_spec...  73.1 us
    pallas_call x1, Pallas kernels, attend_forward(): pl.pallas_call(functools.partial(forward_kernel, part, units), grid_spec=...  46 us
    ppermute x6, waiting for transfers between devices, shift(): return lax.ppermute(value, axis, [(p, (p + i) % n) for p in range(n)])  31.5 us
    all_to_all x1, blocking collectives, exchange(): lax.all_to_all(blocks_out.reshape(-1, width), 'unit', 0, 0, tiled=True)  25.5 us
    dot_general x3, matrix products, inner_back(): lax.dot_general(grad_rows, weight, (((1,), (1,)), ((), ())), preferred_el...  25.5 us
    all_to_all x5, starting transfers between devices, exchange(): lax.all_to_all(blocks_out.reshape(-1, width), 'unit', 0, 0, tiled=True)  24.2 us
    dot_general x5, matrix products, outer_sum(): lax.dot_general(left_rows, right_rows, (((0,), (0,)), ((), ())), preferre...  19.5 us
  transfers between devices with their start and end apart: 14, of which 10 were waited for; matrix products, arithmetic and copies ran while one was open for 26% of the time, Pallas kernels for 24%

profile of v2, /device:TPU:0, one launch (start us, length us, event | category | flops | bytes accessed | tf_op | source)
XLA Modules:
  0.0 570.2 jit_solution(13337388787501777789)
XLA Ops:
  7.2 2.1 reshape.388
  9.7 1.3 reshape.389
  23.4 7.3 %all-to-all-start = ((bf16[8,32,768]{2,1,0:T(8,128)(2,1)}), bf16[8,32,768]{2,1,0:T(8,128)(2,1)S(1)}, u32[]{:S(2)}, u32[]{:S(2)}) async-start(bf16[8,32,768]{2,1,0:T(8,128)(2,1)} %bitcast.11), calls=%async_computation | async-start | bytes 786432 | tf_op jit(solution)/shard_map/all_to_all | solution.py:536
  31.7 1.9 pad_maximum_fusion.2
  33.6 10.8 %all-to-all-done = bf16[8,32,768]{2,1,0:T(8,128)(2,1)S(1)} async-done(((bf16[8,32,768]{2,1,0:T(8,128)(2,1)}), bf16[8,32,768]{2,1,0:T(8,128)(2,1)S(1)}, u32[]{:S(2)}, u32[]{:S(2)}) %all-to-all-start) | async-done | bytes 393248 | tf_op jit(solution)/shard_map/all_to_all | solution.py:536
  44.4 4.5 all-to-all-start.1
  48.9 1.5 collective-permute-start
  50.5 12.1 %collective-permute-done = bf16[8,24,768]{2,1,0:T(8,128)(2,1)S(1)} collective-permute-done((bf16[8,24,768]{2,1,0:T(8,128)(2,1)S(1)}, bf16[8,24,768]{2,1,0:T(8,128)(2,1)S(1)}, u32[]{:S(2)}, u32[]{:S(2)}) %collective-permute-start) | collective-permute-done | bytes 294944 | tf_op jit(solution)/shard_map/ppermute | solution.py:542
  62.9 1.0 multiply_sine_fusion
  67.4 1.2 slice_reduce_fusion.15
  68.6 89.5 %all-to-all-done.1.tok_ref = bf16[8,256,768]{2,1,0:T(8,128)(2,1)} async-done(((bf16[8,256,768]{2,1,0:T(8,128)(2,1)}), bf16[8,256,768]{2,1,0:T(8,128)(2,1)}, u32[]{:S(2)}, u32[]{:S(2)}) %all-to-all-start.1) | async-done | bytes 3145760 | tf_op jit(solution)/shard_map/all_to_all | solution.py:536
  158.1 9.6 %project.1 = (bf16[8,256,640]{2,1,0:T(8,128)(2,1)}, bf16[8,256,768]{2,1,0:T(8,128)(2,1)}, bf16[8,256,768]{2,1,0:T(8,128)(2,1)}) custom-call(bf16[8,256,768]{2,1,0:T(8,128)(2,1)} %all-to-all-done.1.tok_ref, bf16[768,768]{1,0:T(8,128)(2,1)} %bitcast.256, f32[1,640]{1,0:T(1,128)} %dynamic-slice_bitcast_fusion.1.b_ref, f32[1,768]{1,0:T(1,128)} %get-tuple-element.94.gain_ref, ...), custom_call_target="tpu_custom_call" | custom-call | flops 2013265920 | bytes 12058624 | tf_op jit(solution)/shard_map/project/pallas_call | solution.py:94
  167.7 3.4 slice_bitcast_fusion.5
  172.5 3.1 collective-permute-done.2
  175.6 3.9 pad_maximum_fusion.1.kv_ref
  179.5 46.0 %attend_forward.1 = (bf16[8,256,256]{2,1,0:T(8,128)(2,1)}, f32[8,192,256]{2,1,0:T(8,128)}, f32[8,8,256]{2,1,0:T(8,128)}) custom-call(s32[17]{0:T(128)} %pad_add_fusion.meta, bf16[8,256,640]{2,1,0:T(8,128)(2,1)} %get-tuple-element.24.q_ref, bf16[2,8,256,512]{3,2,1,0:T(8,128)(2,1)} %pad_maximum_fusion.1.kv_ref, s32[8,1,256]{2,1,0:T(1,128)} %broadcast_in_dim.58.seg_ref), custom_call_target="tpu_custom_call" | custom-call | flops 12884901888 | bytes 20000000 | tf_op jit(solution)/shard_map/attend_forward/pallas_call | solution.py:387
  225.5 4.0 all-to-all-start.2
  233.8 1.2 reshape_reshape.16
  235.1 1.2 fusion.27
  236.3 18.3 %all-to-all-done.2 = bf16[8,256,256]{2,1,0:T(8,128)(2,1)S(1)} async-done(((bf16[8,256,256]{2,1,0:T(8,128)(2,1)}), bf16[8,256,256]{2,1,0:T(8,128)(2,1)S(1)}, u32[]{:S(2)}, u32[]{:S(2)}) %all-to-all-start.2) | async-done | bytes 1048608 | tf_op jit(solution)/shard_map/all_to_all | solution.py:536
  255.7 1.3 copy.165
  257.0 2.2 fusion.88
  259.3 1.1 slice.441
  260.4 5.0 fusion.77
  265.3 1.0 copy-done.1
  266.4 1.0 fusion.41
  267.4 1.3 copy.163
  268.7 4.6 all-to-all-start.3
  273.9 6.3 %multiply_convert_fusion = (bf16[512,3072]{1,0:T(8,128)(2,1)}, f32[512,3072]{1,0:T(8,128)S(1)}) fusion(f32[3072]{0:T(1024)S(1)} %add.180, bf16[512,768]{1,0:T(8,128)(2,1)} %fusion.27, bf16[768,6912]{1,0:T(8,128)(2,1)} %all-gather.3.cloned.1.call-done), kind=kOutput, calls=%fused_computation.7 | convolution fusion | flops 2425356288 | bytes 14954496 | tf_op jit(solution)/shard_map/dot_general | solution.py:34
  280.2 12.7 %fusion.87 = (bf16[3072]{0:T(1024)(128)(2,1)S(1)}, bf16[512,3072]{1,0:T(8,128)(2,1)S(1)}) fusion(f32[512,3072]{1,0:T(8,128)S(1)} %get-tuple-element.110, f32[3072]{0:T(1024)S(1)} %add.180, bf16[512,768]{1,0:T(8,128)(2,1)S(1)} %bitcast.269, bf16[768,768]{1,0:T(8,128)(2,1)S(1)} %copy-done.15, bf16[768,768]{1,0:T(8,128)(2,1)S(1)} %copy-done.17, ...), kind=kOutput, calls=%fused_computation.201 | convolution fusion | flops 2453664768 | bytes 14960640 | tf_op jit(solution)/shard_map/dot_general | solution.py:44
  293.0 8.1 %fusion.35 = (f32[512]{0:T(512)S(1)}, bf16[768]{0:T(1024)(128)(2,1)S(1)}, f32[512]{0:T(512)}, bf16[768]{0:T(1024)(128)(2,1)S(1)}, f32[512,768]{1,0:T(8,128)}) fusion(f32[768]{0:T(1024)S(1)} %get-tuple-element.46, f32[512]{0:T(512)S(1)} %bitcast.288, f32[512]{0:T(512)S(1)} %bitcast.292, bf16[256,2,768]{2,1,0:T(2,128)(2,1)S(1)} %copy-done, ...), kind=kOutput, calls=%fused_computation.57 | convolution fusion | flops 2419848704 | bytes 10237952 | tf_op jit(solution)/shard_map/dot_general | solution.py:44
  303.0 4.5 convolution_convert_fusion
  307.6 1.7 fusion.78
  309.2 1.3 copy-done.57
  310.5 4.3 convolution_convert_fusion.1
  315.6 16.5 %concatenate.131 = bf16[768,7040]{1,0:T(8,128)(2,1)} concatenate(bf16[768,3072]{1,0:T(8,128)(2,1)} %convolution_convert_fusion.1, bf16[768,768]{1,0:T(8,128)(2,1)} %get-tuple-element.69, bf16[768,768]{1,0:T(8,128)(2,1)} %get-tuple-element.68, bf16[768,768]{1,0:T(8,128)(2,1)S(1)} %get-tuple-element.67, bf16[768,768]{1,0:T(8,128)(2,1)S(1)} %get-tuple-element.66, ...), dimensions={1} | concatenate | bytes 21626880 | tf_op jit(solution)/shard_map/concatenate | solution.py:685
  332.2 73.1 %attend_backward.1 = (bf16[8,256,640]{2,1,0:T(8,128)(2,1)}, bf16[1,8,256,512]{3,2,1,0:T(8,128)(2,1)}) custom-call(s32[17]{0:T(128)} %pad_add_fusion.meta, bf16[8,256,640]{2,1,0:T(8,128)(2,1)} %get-tuple-element.24.q_ref, bf16[8,256,256]{2,1,0:T(8,128)(2,1)} %all-to-all-done.3.do_ref, f32[8,192,256]{2,1,0:T(8,128)} %get-tuple-element.26.ot_ref, ...), custom_call_target="tpu_custom_call" | custom-call | flops 32212254720 | bytes 20000000 | tf_op jit(solution)/shard_map/attend_backward/pallas_call | solution.py:426
  406.1 3.7 collective-permute-done.3.refs_1_
  409.8 7.5 %unturn.1 = bf16[8,256,640]{2,1,0:T(8,128)(2,1)} custom-call(bf16[8,256,640]{2,1,0:T(8,128)(2,1)} %get-tuple-element.29.refs_0_, bf16[8,256,512]{2,1,0:T(8,128)(2,1)} %collective-permute-done.3.refs_1_, f32[8,8,256]{2,1,0:T(8,128)} %get-tuple-element.104.cos_ref.refs_2_, f32[8,8,256]{2,1,0:T(8,128)} %get-tuple-element.103.sin_ref.refs_3_), custom_call_target="tpu_custom_call" | custom-call | tf_op jit(solution)/shard_map/unturn/pallas_call | solution.py:141
  417.3 2.4 convert_reduce_fusion
  420.0 4.2 fusion.10
  424.2 4.1 bitcast_convert_fusion
  429.7 2.2 collective-permute-done.4
  431.9 1.4 fusion.12
  433.4 9.8 %collective-permute-start.5 = (bf16[8,32,768]{2,1,0:T(8,128)(2,1)S(1)}, bf16[8,32,768]{2,1,0:T(8,128)(2,1)S(1)}, u32[]{:S(2)}, u32[]{:S(2)}) collective-permute-start(bf16[8,32,768]{2,1,0:T(8,128)(2,1)S(1)} %dynamic-slice_bitcast_fusion), channel_id=1, source_target_pairs={{0,16},{16,0},{1,17},{17,1},{2,18},{18,2},{3,19},{19,3},{4,20},{20... | collective-permute-start | bytes 1179656 | tf_op jit(solution)/shard_map/ppermute | solution.py:542
  443.2 9.6 %collective-permute-done.5 = bf16[8,32,768]{2,1,0:T(8,128)(2,1)S(1)} collective-permute-done((bf16[8,32,768]{2,1,0:T(8,128)(2,1)S(1)}, bf16[8,32,768]{2,1,0:T(8,128)(2,1)S(1)}, u32[]{:S(2)}, u32[]{:S(2)}) %collective-permute-start.5) | collective-permute-done | bytes 393248 | tf_op jit(solution)/shard_map/ppermute | solution.py:542
  452.9 25.5 %all_to_all.42 = bf16[8,32,768]{2,1,0:T(8,128)(2,1)} all-to-all(bf16[8,32,768]{2,1,0:T(8,128)(2,1)S(1)} %fusion.49), channel_id=1, replica_groups=mesh['seq'=2,'unit'=8,'part'=2] {'unit'}, dimensions={0} | all-to-all | bytes 786432 | tf_op jit(solution)/shard_map/all_to_all | solution.py:536
  478.4 3.8 all-to-all-start.4
  482.3 1.5 pad.18
  484.3 6.0 %fusion.44 = f32[512,768]{1,0:T(8,128)S(1)} fusion(bf16[512,3072]{1,0:T(8,128)(2,1)} %get-tuple-element.109, bf16[768,768]{1,0:T(8,128)(2,1)S(1)} %copy-done.16, bf16[768,768]{1,0:T(8,128)(2,1)S(1)} %copy-done.18, bf16[768,768]{1,0:T(8,128)(2,1)} %get-tuple-element.64, bf16[768,768]{1,0:T(8,128)(2,1)} %get-tuple-element.65), kind=kOutput, calls=%fused_computation.66 | convolution fusion | flops 2434793472 | bytes 9437184 | tf_op jit(solution)/shard_map/dot_general | solution.py:34
  490.4 1.1 fusion.18
  491.4 1.7 copy.223
  498.3 1.6 reshape.398
  500.6 1.0 reshape.397
  505.0 1.6 pad_maximum_fusion.6
  506.6 33.5 %all-to-all-done.4 = bf16[8,256,640]{2,1,0:T(8,128)(2,1)S(1)} async-done(((bf16[8,256,640]{2,1,0:T(8,128)(2,1)}), bf16[8,256,640]{2,1,0:T(8,128)(2,1)S(1)}, u32[]{:S(2)}, u32[]{:S(2)}) %all-to-all-start.4) | async-done | bytes 2621472 | tf_op jit(solution)/shard_map/all_to_all | solution.py:536
  540.1 2.0 copy.168
  542.8 4.7 fusion.76
  547.6 1.4 fusion.34
  548.9 1.7 copy.222
  550.6 1.0 convert_element_type.174
  553.3 1.1 reshape.403
  554.4 2.4 copy.178
  556.8 4.0 reshape.404
  (283 shorter events, 44.4 us)
Async XLA Ops:
  7.2 3.8 copy-start.27
  7.2 3.8 copy-start.29
  7.2 253.2 %all-gather.3.cloned.1.call-start = ((), (), s32[]{:S(2)}) async-start(), calls=%async_computation.7 | async-start | bytes 10948608 | tf_op jit(solution)/shard_map/all_gather | solution.py:605
  9.4 2.4 copy-start.28
  9.4 2.9 copy-start.46
  9.4 3.0 copy-start.47
  9.4 3.1 copy-start.48
  9.4 3.1 copy-start.49
  9.5 3.2 copy-start.50
  9.5 3.3 copy-start.51
  9.5 3.4 copy-start.52
  9.5 3.5 copy-start.53
  9.7 3.9 copy-start.42
  11.0 19.7 %copy-start = (bf16[256,2,768]{2,1,0:T(2,128)(2,1)S(1)}, bf16[256,2,768]{2,1,0:T(2,128)(2,1)}, u32[]{:S(2)}) copy-start(bf16[256,2,768]{2,1,0:T(2,128)(2,1)} %param.15) | copy-start | bytes 2359300
  13.4 20.2 %copy-start.21 = (bf16[3,8,4,640]{3,1,2,0:T(8,128)(2,1)}, bf16[3,8,4,640]{3,1,2,0:T(8,128)(2,1)S(1)}, u32[]{:S(2)}) copy-start(bf16[3,8,4,640]{3,1,2,0:T(8,128)(2,1)S(1)} %copy.191) | copy-start | bytes 368644
  23.4 20.9 %all-to-all-start = ((bf16[8,32,768]{2,1,0:T(8,128)(2,1)}), bf16[8,32,768]{2,1,0:T(8,128)(2,1)S(1)}, u32[]{:S(2)}, u32[]{:S(2)}) async-start(bf16[8,32,768]{2,1,0:T(8,128)(2,1)} %bitcast.11), calls=%async_computation | async-start | bytes 786432 | tf_op jit(solution)/shard_map/all_to_all | solution.py:536
  44.4 113.8 %all-to-all-start.1 = ((bf16[8,256,768]{2,1,0:T(8,128)(2,1)}), bf16[8,256,768]{2,1,0:T(8,128)(2,1)}, u32[]{:S(2)}, u32[]{:S(2)}) async-start(bf16[8,256,768]{2,1,0:T(8,128)(2,1)} %pad_maximum_fusion.2), calls=%async_computation.1 | async-start | bytes 6291456 | tf_op jit(solution)/shard_map/all_to_all | solution.py:536
  48.8 493.8 %all-gather.5.cloned.1.call-start = ((), (), s32[]{:S(2)}) async-start(), calls=%async_computation.8 | async-start | bytes 4055040 | tf_op jit(solution)/shard_map/all_gather | solution.py:606
  48.9 13.7 %collective-permute-start = (bf16[8,24,768]{2,1,0:T(8,128)(2,1)S(1)}, bf16[8,24,768]{2,1,0:T(8,128)(2,1)S(1)}, u32[]{:S(2)}, u32[]{:S(2)}) collective-permute-start(bf16[8,24,768]{2,1,0:T(8,128)(2,1)S(1)} %get-tuple-element.74), channel_id=1, source_target_pairs={{0,16},{16,0},{1,17},{17,1},{2,18},{18,2},{3,19},{19,3},{4,20},{20... | collective-permute-start | bytes 884744 | tf_op jit(solution)/shard_map/ppermute | solution.py:542
  62.7 2.1 collective-permute-start.1
  64.9 93.2 %copy-start.2 = (bf16[2,2,8,24,768]{4,3,0,2,1:T(8,128)(2,1)}, bf16[2,2,8,24,768]{4,3,0,2,1:T(8,128)(2,1)S(1)}, u32[]{:S(2)}) copy-start(bf16[2,2,8,24,768]{4,3,0,2,1:T(8,128)(2,1)S(1)} %maximum_select_fusion) | copy-start | bytes 3538948
  68.6 224.3 %copy-start.30 = (f32[768]{0:T(1024)}, f32[768]{0:T(1024)S(1)}, u32[]{:S(2)}) copy-start(f32[768]{0:T(1024)S(1)} %get-tuple-element.46) | copy-start | bytes 9220
  171.1 4.5 collective-permute-start.2
  225.5 4.6 copy-start.6
  225.5 29.1 %all-to-all-start.2 = ((bf16[8,256,256]{2,1,0:T(8,128)(2,1)}), bf16[8,256,256]{2,1,0:T(8,128)(2,1)S(1)}, u32[]{:S(2)}, u32[]{:S(2)}) async-start(bf16[8,256,256]{2,1,0:T(8,128)(2,1)} %get-tuple-element.25), calls=%async_computation.2 | async-start | bytes 2097152 | tf_op jit(solution)/shard_map/all_to_all | solution.py:536
  230.1 62.9 %copy-start.32 = (f32[1,2,2,128]{3,1,2,0:T(2,128)}, f32[1,2,2,128]{3,1,2,0:T(2,128)S(1)}, u32[]{:S(2)}) copy-start(f32[1,2,2,128]{3,1,2,0:T(2,128)S(1)} %copy.194) | copy-start | bytes 6148
  230.1 62.9 %copy-start.34 = (f32[1,2,2,128]{3,1,2,0:T(2,128)}, f32[1,2,2,128]{3,1,2,0:T(2,128)S(1)}, u32[]{:S(2)}) copy-start(f32[1,2,2,128]{3,1,2,0:T(2,128)S(1)} %copy.193) | copy-start | bytes 6148
  230.9 72.0 %copy-start.9 = (bf16[2,256,768]{2,1,0:T(8,128)(2,1)}, bf16[2,256,768]{2,1,0:T(8,128)(2,1)S(1)}, u32[]{:S(2)}) copy-start(bf16[2,256,768]{2,1,0:T(8,128)(2,1)S(1)} %copy.161) | copy-start | bytes 2359300
  255.7 3.6 copy-start.4
  268.7 63.5 %all-to-all-start.3 = ((bf16[8,256,256]{2,1,0:T(8,128)(2,1)}), bf16[8,256,256]{2,1,0:T(8,128)(2,1)}, u32[]{:S(2)}, u32[]{:S(2)}) async-start(bf16[8,256,256]{2,1,0:T(8,128)(2,1)} %bitcast.43), calls=%async_computation.3 | async-start | bytes 2097152 | tf_op jit(solution)/shard_map/all_to_all | solution.py:536
  273.3 6.9 %copy-start.15 = (bf16[768,768]{1,0:T(8,128)(2,1)S(1)}, bf16[768,768]{1,0:T(8,128)(2,1)}, u32[]{:S(2)}) copy-start(bf16[768,768]{1,0:T(8,128)(2,1)} %get-tuple-element.62) | copy-start | bytes 3538948
  273.3 277.3 %reduce-scatter.4.cloned.1.call-start = ((), (), s32[]{:S(2)}) async-start(), calls=%async_computation.9 | async-start | bytes 11151360
  273.9 6.3 %copy-start.17 = (bf16[768,768]{1,0:T(8,128)(2,1)S(1)}, bf16[768,768]{1,0:T(8,128)(2,1)}, u32[]{:S(2)}) copy-start(bf16[768,768]{1,0:T(8,128)(2,1)} %get-tuple-element.63) | copy-start | bytes 3538948
  273.9 6.3 %copy-start.19 = (bf16[768,768]{1,0:T(8,128)(2,1)S(1)}, bf16[768,768]{1,0:T(8,128)(2,1)}, u32[]{:S(2)}) copy-start(bf16[768,768]{1,0:T(8,128)(2,1)} %get-tuple-element.64) | copy-start | bytes 3538948
  273.9 6.3 %copy-start.20 = (bf16[768,768]{1,0:T(8,128)(2,1)S(1)}, bf16[768,768]{1,0:T(8,128)(2,1)}, u32[]{:S(2)}) copy-start(bf16[768,768]{1,0:T(8,128)(2,1)} %get-tuple-element.65) | copy-start | bytes 3538948
  293.0 8.1 %copy-start.56 = (bf16[512,3072]{1,0:T(8,128)(2,1)}, bf16[512,3072]{1,0:T(8,128)(2,1)S(1)}, u32[]{:S(2)}) copy-start(bf16[512,3072]{1,0:T(8,128)(2,1)S(1)} %get-tuple-element.113) | copy-start | bytes 9437188
  293.0 8.1 %copy-start.36 = (bf16[1,768]{1,0:T(2,128)(2,1)S(1)}, bf16[1,768]{1,0:T(2,128)(2,1)}, u32[]{:S(2)}) copy-start(bf16[1,768]{1,0:T(2,128)(2,1)} %broadcast_in_dim.61) | copy-start | bytes 4612
  293.0 8.1 %copy-start.45 = (bf16[8]{0:T(256)(128)(2,1)S(1)}, bf16[8]{0:T(256)(128)(2,1)}, u32[]{:S(2)}) copy-start(bf16[8]{0:T(256)(128)(2,1)} %pad.51.clone) | copy-start | bytes 52
  307.5 1.7 copy-start.25
  307.6 3.0 copy-start.57
  310.5 5.1 copy-start.23
  310.5 5.1 copy-start.24
  332.2 73.2 %copy-start.3 = (bf16[2,2,8,24,768]{4,3,0,2,1:T(8,128)(2,1)S(1)}, bf16[2,2,8,24,768]{4,3,0,2,1:T(8,128)(2,1)}, u32[]{:S(2)}) copy-start(bf16[2,2,8,24,768]{4,3,0,2,1:T(8,128)(2,1)} %copy-done.2) | copy-start | bytes 3538948
  405.3 4.5 collective-permute-start.3
  417.3 2.7 copy-start.55
  420.0 4.3 copy-start.54
  429.4 2.5 collective-permute-start.4
  433.4 19.4 %collective-permute-start.5 = (bf16[8,32,768]{2,1,0:T(8,128)(2,1)S(1)}, bf16[8,32,768]{2,1,0:T(8,128)(2,1)S(1)}, u32[]{:S(2)}, u32[]{:S(2)}) collective-permute-start(bf16[8,32,768]{2,1,0:T(8,128)(2,1)S(1)} %dynamic-slice_bitcast_fusion), channel_id=1, source_target_pairs={{0,16},{16,0},{1,17},{17,1},{2,18},{18,2},{3,19},{19,3},{4,20},{20... | collective-permute-start | bytes 1179656 | tf_op jit(solution)/shard_map/ppermute | solution.py:542
  478.4 61.6 %all-to-all-start.4 = ((bf16[8,256,640]{2,1,0:T(8,128)(2,1)}), bf16[8,256,640]{2,1,0:T(8,128)(2,1)S(1)}, u32[]{:S(2)}, u32[]{:S(2)}) async-start(bf16[8,256,640]{2,1,0:T(8,128)(2,1)} %unturn.1), calls=%async_computation.4 | async-start | bytes 5242880 | tf_op jit(solution)/shard_map/all_to_all | solution.py:536
  482.3 1.6 copy-start.16
  482.3 2.0 copy-start.18
  484.3 6.0 %copy-start.5 = (bf16[64,8,4,256]{3,1,2,0:T(8,128)(2,1)S(1)}, bf16[64,8,4,256]{3,1,2,0:T(8,128)(2,1)}, u32[]{:S(2)}) copy-start(bf16[64,8,4,256]{3,1,2,0:T(8,128)(2,1)} %copy-done.4) | copy-start | bytes 3145732
  484.3 6.0 %copy-start.8 = (bf16[256,2,768]{2,0,1:T(8,128)(2,1)S(1)}, bf16[256,2,768]{2,0,1:T(8,128)(2,1)}, u32[]{:S(2)}) copy-start(bf16[256,2,768]{2,0,1:T(8,128)(2,1)} %copy-done.7) | copy-start | bytes 2359300
  484.3 6.1 %copy-start.40 = (f32[768]{0:T(1024)S(1)}, f32[768]{0:T(1024)}, u32[]{:S(2)}) copy-start(f32[768]{0:T(1024)} %get-tuple-element.44) | copy-start | bytes 9220
  484.3 6.1 %copy-start.41 = (f32[768]{0:T(1024)S(1)}, f32[768]{0:T(1024)}, u32[]{:S(2)}) copy-start(f32[768]{0:T(1024)} %get-tuple-element.47) | copy-start | bytes 9220
  490.4 2.8 copy-start.43
  490.4 3.4 copy-start.12
  542.8 4.7 copy-start.10
  542.8 4.7 copy-start.13
  542.8 4.7 copy-start.31
  542.8 4.7 copy-start.37
  542.8 4.7 copy-start.38
  552.3 10.6 %copy-start.44 = (f32[24]{0:T(128)}, f32[24]{0:T(128)S(1)}, u32[]{:S(2)}) copy-start(f32[24]{0:T(128)S(1)} %get-tuple-element.150) | copy-start | bytes 292
  554.4 6.4 %copy-start.11 = (bf16[24,7040]{1,0:T(8,128)(2,1)S(1)}, bf16[24,7040]{1,0:T(8,128)(2,1)}, u32[]{:S(2)}) copy-start(bf16[24,7040]{1,0:T(8,128)(2,1)} %reduce-scatter.4.cloned.1.call-done) | copy-start | bytes 1013764
  (8 other events, 6.2 us)
Sparse Core Ops, SparseCore 0:
  11.9 146.7 all-gather.2
  171.3 60.2 all-gather.4
  332.3 146.8 reduce-scatter.3

commit v3 on v2

--- a/solution.py
+++ b/solution.py
@@ -176,36 +176,36 @@
     ).astype(BF)
 
 
-def live_of(seg_row, key_start, query_start, rows):
+def live_of(seg_row, unit, query_start, part, rows, c):
     shape = (rows, rows)
-    key_pos = key_start + lax.broadcasted_iota(jnp.int32, shape, 0)
     query_pos = query_start + lax.broadcasted_iota(jnp.int32, shape, 1)
-    return (key_pos <= query_pos) & (key_pos >= seg_row)
-
-
-def block_loop(meta, part, units, rows, step):
+    row = lax.broadcasted_iota(jnp.int32, shape, 0)
+    pieces = []
+    for i in range(part):
+        key_pos = (unit * part + lax.rem(c - i + part, part)) * rows + row
+        pieces.append((key_pos <= query_pos) & (key_pos >= seg_row))
+    return jnp.concatenate(pieces, 0)
+
+
+def unit_loop(meta, part, units, rows, step):
     j = pl.program_id(0)
-    c = meta[2 * units]
-    diag = j * part + c
-    first = meta[j] // rows
+    first = meta[j] // (rows * part)
     top_seg = meta[units + j]
 
-    def one(kb, unused):
-        where = (lax.rem(c - lax.rem(kb, part) + part, part), kb // part)
-        masked = (kb == diag) | (top_seg > kb * rows)
+    def one(unit, unused):
+        masked = (unit == j) | (top_seg > unit * (rows * part))
 
         @pl.when(masked)
         def _():
-            step(where, kb, diag, True)
+            step(unit, True)
 
         @pl.when(jnp.logical_not(masked))
         def _():
-            step(where, kb, diag, False)
+            step(unit, False)
 
         return unused
 
-    lax.fori_loop(first, diag + 1, one, 0)
-    return diag
+    lax.fori_loop(first, j + 1, one, 0)
 
 
 def forward_kernel(
@@ -213,27 +213,29 @@
 ):
     rows = q_ref.shape[1]
     c = meta[2 * units]
-
-    @pl.when(pl.program_id(0) == 0)
+    j = pl.program_id(0)
+
+    @pl.when(j == 0)
     def _():
-        for i in range(part):
-            p = lax.rem(c - i + part, part)
-            for unit in range(units):
-                kb = unit * part + p
-                vt[kb, :TILE] = flip(kv_ref[i, unit, :, TILE : 2 * TILE]).astype(BF)
-                vt[kb, TILE:] = flip(kv_ref[i, unit, :, 3 * TILE :])[:HEAD_DIM].astype(BF)
+        def turn_values(unit, unused):
+            vt[unit, :TILE] = flip(kv_ref[unit, :, TILE : 2 * TILE]).astype(BF)
+            vt[unit, TILE:] = flip(kv_ref[unit, :, 3 * TILE :])[:HEAD_DIM].astype(BF)
+            return unused
+
+        lax.fori_loop(0, units, turn_values, 0)
 
     query_sides(q_ref, qb)
     top[...] = jnp.full(top.shape, NEG_BIG, F32)
     total[...] = jnp.zeros(total.shape, F32)
     acc[...] = jnp.zeros(acc.shape, F32)
     seg_row = seg_ref[0]
-
-    def step(where, kb, diag, masked):
-        k01 = kv_ref[where[0], where[1], :, 0:TILE]
-        k2 = kv_ref[where[0], where[1], :, 2 * TILE : 3 * TILE]
+    query_start = (j * part + c) * rows
+
+    def step(unit, masked):
+        k01 = kv_ref[unit, :, 0:TILE]
+        k2 = kv_ref[unit, :, 2 * TILE : 3 * TILE]
         if masked:
-            live = live_of(seg_row, kb * rows, diag * rows, rows)
+            live = live_of(seg_row, unit, query_start, part, rows, c)
         scores = [mm(k2 if h == 2 else k01, qb[h]) for h in range(TRIO)]
         if masked:
             scores = [jnp.where(live, score, NEG_BIG) for score in scores]
@@ -248,10 +250,10 @@
         top[0:TRIO] = new
         total[0:TRIO] = total[0:TRIO] * factor + jnp.concatenate(sums, 0)
         for h in range(TRIO):
-            vth = vt[kb, h * HEAD_DIM : (h + 1) * HEAD_DIM]
+            vth = vt[unit, h * HEAD_DIM : (h + 1) * HEAD_DIM]
             acc[h] = acc[h] * factor[h : h + 1] + mm(vth, weights[h].astype(BF))
 
-    block_loop(meta, part, units, rows, step)
+    unit_loop(meta, part, units, rows, step)
     out = [acc[h] / total[h : h + 1] for h in range(TRIO)]
     for h in range(TRIO):
         ot_ref[0, h * HEAD_DIM : (h + 1) * HEAD_DIM] = out[h]
@@ -290,12 +292,12 @@
 
     @pl.when(j == 0)
     def _():
-        for i in range(part):
-            p = lax.rem(c - i + part, part)
-            for unit in range(units):
-                kb = unit * part + p
-                kt[kb, :TILE] = flip(kv_ref[i, unit, :, 0:TILE]).astype(BF)
-                kt[kb, TILE:] = flip(kv_ref[i, unit, :, 2 * TILE : 3 * TILE])[HEAD_DIM:].astype(BF)
+        def turn_keys(unit, unused):
+            kt[unit, :TILE] = flip(kv_ref[unit, :, 0:TILE]).astype(BF)
+            kt[unit, TILE:] = flip(kv_ref[unit, :, 2 * TILE : 3 * TILE])[HEAD_DIM:].astype(BF)
+            return unused
+
+        lax.fori_loop(0, units, turn_keys, 0)
         for ref in (dk01, dv01, dk2, dv2):
             ref[...] = jnp.zeros(ref.shape, F32)
 
@@ -323,46 +325,48 @@
         )
     dqt[...] = jnp.zeros(dqt.shape, F32)
     seg_row = seg_ref[0]
-
-    def step(where, kb, diag, masked):
-        k01 = kv_ref[where[0], where[1], :, 0:TILE]
-        v01 = kv_ref[where[0], where[1], :, TILE : 2 * TILE]
-        k2 = kv_ref[where[0], where[1], :, 2 * TILE : 3 * TILE]
-        v2 = kv_ref[where[0], where[1], :, 3 * TILE :]
+    query_start = (j * part + c) * rows
+
+    def step(unit, masked):
+        k01 = kv_ref[unit, :, 0:TILE]
+        v01 = kv_ref[unit, :, TILE : 2 * TILE]
+        k2 = kv_ref[unit, :, 2 * TILE : 3 * TILE]
+        v2 = kv_ref[unit, :, 3 * TILE :]
         if masked:
-            live = live_of(seg_row, kb * rows, diag * rows, rows)
+            live = live_of(seg_row, unit, query_start, part, rows, c)
+        scores = [mm(k2 if h == 2 else k01, qb[h]) for h in range(TRIO)]
+        dprobs = [mm(v2 if h == 2 else v01, db[h]) for h in range(TRIO)]
         probs = []
         grads = []
         for h in range(TRIO):
-            score = mm(k2 if h == 2 else k01, qb[h])
+            score = scores[h]
             if masked:
                 score = jnp.where(live, score, NEG_BIG)
             prob = jnp.exp(score - lse_ref[0, h : h + 1])
             if masked:
                 prob = jnp.where(live, prob, 0.0)
-            dprob = mm(v2 if h == 2 else v01, db[h])
-            ds = (prob * (dprob - delta[h : h + 1])).astype(BF)
             probs.append(prob.astype(BF))
-            grads.append(ds)
-            kth = kt[kb, h * HEAD_DIM : (h + 1) * HEAD_DIM]
-            dqt[h * HEAD_DIM : (h + 1) * HEAD_DIM] += mm(kth, ds)
-        dv01[kb] += mm(jnp.concatenate(probs[:2], 1), dn[: 2 * rows])
-        dk01[kb] += mm(jnp.concatenate(grads[:2], 1), qn[: 2 * rows])
-        dv2[kb] += mm(probs[2], dn[2 * rows :])
-        dk2[kb] += mm(grads[2], qn[2 * rows :])
-
-    diag = block_loop(meta, part, units, rows, step)
+            grads.append((prob * (dprobs[h] - delta[h : h + 1])).astype(BF))
+        dv01[unit] += mm(jnp.concatenate(probs[:2], 1), dn[: 2 * rows])
+        dk01[unit] += mm(jnp.concatenate(grads[:2], 1), qn[: 2 * rows])
+        dv2[unit] += mm(probs[2], dn[2 * rows :])
+        dk2[unit] += mm(grads[2], qn[2 * rows :])
+        for h in range(TRIO):
+            kth = kt[unit, h * HEAD_DIM : (h + 1) * HEAD_DIM]
+            dqt[h * HEAD_DIM : (h + 1) * HEAD_DIM] += mm(kth, grads[h])
+
+    unit_loop(meta, part, units, rows, step)
     own_ref[j, :, 0:TILE] = (dqt[:TILE] * scale).T.astype(BF)
     dq2 = dqt[TILE:] * scale
-    dk2[diag] += jnp.concatenate([dq2, jnp.zeros_like(dq2)], 0).T
+    dk2[j, 0:rows] += jnp.concatenate([dq2, jnp.zeros_like(dq2)], 0).T
 
     @pl.when(j == units - 1)
     def _():
         for unit in range(units):
             for i in range(part):
-                kb = unit * part + lax.rem(c + i, part)
+                span = slice(i * rows, (i + 1) * rows)
                 for t, ref in enumerate((dk01, dv01, dk2, dv2)):
-                    tile = ref[kb].astype(BF)
+                    tile = ref[unit, span].astype(BF)
                     if i == 0:
                         own_ref[unit, :, (t + 1) * TILE : (t + 2) * TILE] = tile
                     else:
@@ -383,7 +387,7 @@
 
 def attend_forward(meta, packed, kv, seg):
     units, rows, unused = packed.shape
-    part = kv.shape[0]
+    part = kv.shape[1] // rows
     return pl.pallas_call(
         functools.partial(forward_kernel, part, units),
         grid_spec=pltpu.PrefetchScalarGridSpec(
@@ -401,7 +405,7 @@
             ],
             scratch_shapes=[
                 pltpu.VMEM((TRIO, TILE, rows), BF),
-                pltpu.VMEM((units * part, TRIO * HEAD_DIM, rows), BF),
+                pltpu.VMEM((units, TRIO * HEAD_DIM, part * rows), BF),
                 pltpu.VMEM((8, rows), F32),
                 pltpu.VMEM((8, rows), F32),
                 pltpu.VMEM((TRIO, HEAD_DIM, rows), F32),
@@ -420,9 +424,9 @@
 
 def attend_backward(meta, packed, dout, out_t, lse, kv, seg):
     units, rows, unused = packed.shape
-    part = kv.shape[0]
+    part = kv.shape[1] // rows
     others = (max(part - 1, 1), units, rows, 4 * TILE)
-    grads = pltpu.VMEM((units * part, rows, TILE), F32)
+    grads = pltpu.VMEM((units, part * rows, TILE), F32)
     return pl.pallas_call(
         functools.partial(backward_kernel, part, units),
         grid_spec=pltpu.PrefetchScalarGridSpec(
@@ -442,7 +446,7 @@
                 pltpu.VMEM((TRIO, TILE, rows), BF),
                 pltpu.VMEM((TRIO * rows, TILE), BF),
                 pltpu.VMEM((TRIO * rows, TILE), BF),
-                pltpu.VMEM((units * part, TRIO * HEAD_DIM, rows), BF),
+                pltpu.VMEM((units, TRIO * HEAD_DIM, part * rows), BF),
                 pltpu.VMEM((8, rows), F32),
                 pltpu.VMEM((TRIO * HEAD_DIM, rows), F32),
                 grads,
@@ -459,6 +463,87 @@
         cost_estimate=attention_cost(20, units, rows, part),
         name="attend_backward",
     )(meta, packed, dout, out_t, lse, kv, seg)
+
+
+def pack_kernel(trios, groups, w_ref, vec_ref, early_ref, local_ref):
+    d = w_ref.shape[1] // 3
+    w = w_ref[...].astype(F32)
+    width = TRIO * HEAD_DIM
+    zeros = jnp.zeros((w.shape[0], HEAD_DIM), F32)
+    for g in range(trios):
+        q, k, v = (w[:, i * d + g * width : i * d + (g + 1) * width] for i in range(3))
+        tiles = [q[:, :TILE], k[:, :TILE], v[:, :TILE]]
+        tiles.append(jnp.concatenate([q[:, TILE:], k[:, TILE:]], 1))
+        tiles.append(jnp.concatenate([v[:, TILE:], zeros], 1))
+        for t, tile in enumerate(tiles):
+            tile = tile.astype(BF)
+            local_ref[:, g * PACK + t * TILE : g * PACK + (t + 1) * TILE] = tile
+            for s in range(groups):
+                early_ref[g * groups + s, :, t * TILE : (t + 1) * TILE] = tile
+        for s in range(groups):
+            early_ref[g * groups + s, :, PACK:] = vec_ref[s]
+
+
+def pack_early(weight, vec, trios):
+    r = weight.shape[0]
+    groups = vec.shape[0]
+    return pl.pallas_call(
+        functools.partial(pack_kernel, trios, groups),
+        out_shape=[
+            jax.ShapeDtypeStruct((trios * groups, r, PACK + TILE), BF),
+            jax.ShapeDtypeStruct((r, trios * PACK), BF),
+        ],
+        name="pack_early",
+    )(weight, vec)
+
+
+def gradient_kernel(
+    trios, blocks, norm_ref, pre_ref, hidden_ref, cot_ref, att_ref, vec_ref, out_ref
+):
+    i = pl.program_id(0)
+    d = cot_ref.shape[1]
+    where = pl.ds(pl.multiple_of(i * d, d), d)
+
+    @pl.when(i < blocks)
+    def _():
+        out_ref[:, where] = outer_sum(norm_ref[...], pre_ref[...]).astype(BF)
+
+    @pl.when((i >= blocks) & (i < 2 * blocks))
+    def _():
+        out_ref[:, where] = outer_sum(hidden_ref[...], cot_ref[...]).astype(BF)
+
+    @pl.when(i == 2 * blocks)
+    def _():
+        width = d // trios
+        for g in range(trios):
+            part = outer_sum(att_ref[:, g * OPACK : (g + 1) * OPACK], cot_ref[...])
+            out_ref[g * width : (g + 1) * width, where] = part[:width].astype(BF)
+        out_ref[:, (2 * blocks + 1) * d :] = vec_ref[...]
+
+
+def gradients(normed, pre_grad, hidden, cot, attended, vec, trios):
+    rows, d = normed.shape
+    blocks = hidden.shape[1] // d
+    width = (2 * blocks + 1) * d + TILE
+    return pl.pallas_call(
+        functools.partial(gradient_kernel, trios, blocks),
+        grid=(2 * blocks + 1,),
+        in_specs=[
+            pl.BlockSpec((rows, d), lambda i: (0, 0)),
+            pl.BlockSpec((rows, d), lambda i: (0, jnp.minimum(i, blocks - 1))),
+            pl.BlockSpec((rows, d), lambda i: (0, jnp.clip(i - blocks, 0, blocks - 1))),
+            pl.BlockSpec((rows, d), lambda i: (0, 0)),
+            pl.BlockSpec(attended.shape, lambda i: (0, 0)),
+            pl.BlockSpec((d, TILE), lambda i: (0, 0)),
+        ],
+        out_specs=pl.BlockSpec((d, width), lambda i: (0, 0)),
+        out_shape=jax.ShapeDtypeStruct((d, width), BF),
+        compiler_params=params_of("arbitrary"),
+        cost_estimate=pl.CostEstimate(
+            flops=2 * rows * d * width, bytes_accessed=4 * d * width, transcendentals=0
+        ),
+        name="gradients",
+    )(normed, pre_grad, hidden, cot, attended, vec)
 
 
 def pack_columns(matrix, trios):
@@ -541,16 +626,24 @@
         n = lax.axis_size(axis)
         return lax.ppermute(value, axis, [(p, (p + i) % n) for p in range(n)])
 
+    def natural_order(got, me):
+        n = len(got)
+        if n == 2:
+            return jnp.where(me == 0, jnp.stack(got), jnp.stack(got[::-1]))
+        ring = jnp.stack((got + got)[::-1])
+        return lax.dynamic_slice_in_dim(ring, n - 1 - me, n, 0)
+
     def gather_small(value, axis):
         n = lax.axis_size(axis)
-        me = lax.axis_index(axis)
         got = [value] + [shift(value, axis, i) for i in range(1, n)]
-        if n == 2:
-            return jnp.where(me == 0, jnp.stack(got), jnp.stack(got[::-1]))
-        got = jnp.stack(got)
-        return jnp.stack(
-            [lax.dynamic_index_in_dim(got, (me - k + n) % n, 0, False) for k in range(n)]
-        )
+        return natural_order(got, lax.axis_index(axis))
+
+    def exchange_small(value):
+        got = []
+        for i in range(units):
+            piece = lax.dynamic_index_in_dim(value, (unit + i) % units, 0, False)
+            got.append(shift(piece, "unit", i) if i else piece)
+        return natural_order(got, unit)
 
     def scatter_small(value, axis):
         n = lax.axis_size(axis)
@@ -566,25 +659,31 @@
         [v.reshape(r, 1) for v in vectors] + [qkv_bias.reshape(r, 3), fc1_bias.reshape(r, blocks)],
         1,
     )
-    vec = jnp.pad(vec, ((0, 0), (0, TILE - vec.shape[1])))
-    qkv_local = pack_columns(qkv_weight, trios)
-    seg_rows = segment.T
-    seg_pack = jnp.concatenate([seg_rows // 64, seg_rows % 64], 1).astype(BF)
-    seg_pack = jnp.pad(seg_pack[:, None, :], ((0, 0), (0, 7), (0, PACK + TILE - 2 * rows)))
-    early = []
-    for u in range(units):
-        g = u // groups
-        trio_cols = jnp.concatenate([qkv_local[:, g * PACK : (g + 1) * PACK], vec], 1)
-        early += [trio_cols, seg_pack[u % groups]]
-    early = exchange(jnp.concatenate(early, 0).reshape(units, r + 8, PACK + TILE))
     token_rows = tokens.transpose(1, 0, 2)
     toks = exchange(jnp.concatenate([token_rows] * trios, 0))
-
-    seg_mine = early[:, r, : 2 * rows].astype(jnp.int32)
-    seg_mine = seg_mine[:, :rows] * 64 + seg_mine[:, rows:]
+    seg_rows = segment.T
+    seg_lanes = -(-2 * rows // r)
+    seg_pack = jnp.concatenate([seg_rows // 64, seg_rows % 64], 1).astype(BF)
+    seg_pack = jnp.pad(seg_pack, ((0, 0), (0, seg_lanes * r - 2 * rows)))
+    seg_pack = seg_pack.reshape(groups, r, seg_lanes)
+    vec = jnp.pad(vec, ((0, 0), (0, 16 - vec.shape[1])))
+    vec = jnp.concatenate(
+        [
+            jnp.broadcast_to(vec, (groups, r, 16)),
+            seg_pack,
+            jnp.zeros((groups, r, TILE - 16 - seg_lanes), BF),
+        ],
+        -1,
+    )
+    early, qkv_local = pack_early(qkv_weight, vec, trios)
+    early = exchange_small(early)
+
+    seg_mine = early[:, :, PACK + 16 : PACK + 16 + seg_lanes].astype(jnp.int32)
+    seg_mine = seg_mine.reshape(units, r * seg_lanes)
+    seg_mine = seg_mine[:, :rows] * 64 + seg_mine[:, rows : 2 * rows]
     meta = jnp.concatenate([seg_mine[:, 0], seg_mine[:, -1], c[None]])
     seg_mine = seg_mine[:, None, :]
-    trio_full = gather_small(gather_small(early[:, :r], "seq"), "part")
+    trio_full = gather_small(gather_small(early, "seq"), "part")
     trio_full = trio_full.transpose(1, 2, 0, 3, 4).reshape(d, PACK + TILE)
     vec_full = trio_full[:, PACK:].astype(F32)
     vec_rows = vec_full[:, :8].T
@@ -621,7 +720,7 @@
         toks, trio_full, qkv_shift, gain_one, bias_one, cos, sin
     )
     kv_own = packed[:, :, TILE:]
-    kv = jnp.stack([kv_own] + [shift(kv_own, "part", i) for i in range(1, part)])
+    kv = jnp.concatenate([kv_own] + [shift(kv_own, "part", i) for i in range(1, part)], 1)
     out_low, out_t, lse = attend_forward(meta, packed, kv, seg_mine)
     attended = exchange(out_low)
 
@@ -648,9 +747,8 @@
         jnp.exp(-0.5 * hidden_pre * hidden_pre) * (1.0 / math.sqrt(2.0 * math.pi))
     )
     pre_grad = (inner_back(cot, down_full) * slope).astype(BF)
+    hidden_low, pre_grad, attended = lax.optimization_barrier((hidden_low, pre_grad, attended))
     second_branch = mm(hidden_low, down_full) + down_shift
-    down_grad = outer_sum(hidden_low, cot)
-    up_grad = outer_sum(normed_two, pre_grad)
     up_shift_grad = jnp.sum(pre_grad.astype(F32), 0)
     normed_two_grad = inner_back(pre_grad, up_full)
     cot_sum = jnp.sum(cot_float, 0)
@@ -667,7 +765,6 @@
     attended = attended.reshape(all_rows, trios * OPACK)
     branch_one = mm(attended, dense_pad.reshape(trios * OPACK, d)) + dense_shift
     output = (x + branch_one + second_branch).astype(BF)
-    dense_grad = outer_sum(attended, cot).reshape(trios, OPACK, d)[:, : d // trios].reshape(d, d)
 
     vec_grads = jnp.concatenate(
         [
@@ -682,17 +779,14 @@
     vec_grads = jnp.concatenate(
         [vec_grads, up_shift_grad, jnp.zeros((d, TILE - 8 - blocks), F32)], 1
     )
-    mlp_grads = jnp.concatenate(
-        [up_grad.astype(BF)]
-        + [down_grad[b * d : (b + 1) * d].astype(BF) for b in range(blocks)]
-        + [dense_grad.astype(BF), vec_grads.astype(BF)],
-        1,
+    mlp_grads = gradients(
+        normed_two, pre_grad, hidden_low, cot, attended, vec_grads.astype(BF), trios
     )
     mlp_grads, kv = lax.optimization_barrier((mlp_grads, kv))
     mlp_sum = lax.psum_scatter(mlp_grads, ALL_AXES, scatter_dimension=0, tiled=True).astype(F32)
 
     own, others = attend_backward(meta, packed, dout, out_t, lse, kv, seg_mine)
-    others = [shift(others[i - 1], "part", i) for i in range(1, part)]
+    others = [shift(others[i - 1], "part", part - i) for i in range(1, part)]
     qkv_grad = unturn(own, others, cos, sin)
     back = exchange(qkv_grad)
 
@@ -716,7 +810,7 @@
         [late, jnp.broadcast_to(shift_rows, (seqs, units, part) + shift_rows.shape)], 3
     )
     late = scatter_small(late.transpose(2, 0, 1, 3, 4), "part")
-    late = exchange(scatter_small(late, "seq")).astype(F32)
+    late = exchange_small(scatter_small(late, "seq")).astype(F32)
     late = jnp.sum(late.reshape(trios, groups, r + 8, PACK + TILE), 1)
     qkv_weight_grad = unpack_columns(
         late[:, :r, :PACK].transpose(1, 0, 2).reshape(r, trios * PACK), trios
@@ -725,22 +819,12 @@
     qkv_shift_grad = unpack_columns(late[:, r, :PACK].reshape(1, trios * PACK), trios)[0]
     qkv_shift_grad = lax.dynamic_slice_in_dim(qkv_shift_grad, place * 3 * r, 3 * r)
 
-    back = back.reshape(trios, groups, rows, PACK).transpose(1, 2, 0, 3)
-    normed_one_grad = inner_back(back.reshape(all_rows, trios * PACK), qkv_full)
-    in_one = norm_back(normed_one_grad, gain_one)
-    tokens_grad = (cot_float + in_one + in_two).astype(BF)
-
-    def natural(value):
-        return value.reshape(groups, rows, d).transpose(1, 0, 2)
-
     down_sum = jnp.concatenate(
         [mlp_sum[:, ff + b * d : ff + (b + 1) * d] for b in range(blocks)], 0
     )
     vec_sum = mlp_sum[:, 2 * ff + d :]
     cot_total = vec_sum[:, 2]
-    return (
-        natural(output),
-        natural(tokens_grad),
+    param_grads = (
         late_vec[:, 0],
         late_vec[:, 1],
         vec_sum[:, 0],
@@ -754,6 +838,17 @@
         down_sum,
         cot_total,
     )
+    param_grads, back = lax.optimization_barrier((param_grads, back))
+
+    back = back.reshape(trios, groups, rows, PACK).transpose(1, 2, 0, 3)
+    normed_one_grad = inner_back(back.reshape(all_rows, trios * PACK), qkv_full)
+    in_one = norm_back(normed_one_grad, gain_one)
+    tokens_grad = (cot_float + in_one + in_two).astype(BF)
+
+    def natural(value):
+        return value.reshape(groups, rows, d).transpose(1, 0, 2)
+
+    return (natural(output), natural(tokens_grad)) + tuple(param_grads)
 
 
 def solution(mesh):

time: 578 us -> 566 us (0.979)
  starting transfers between devices: 36.5 us -> 69 us
  local copies, waits for them, and re-layouts: 86.1 us -> 66.5 us
  Pallas kernels: 136 us -> 118 us
  matrix products: 59.3 us -> 49.2 us
    all_to_all x5 -> x3, waiting for transfers between devices: 152 us -> 18.5 us  [exchange(): lax.all_to_all(blocks_out.reshape(-1, width), 'unit', 0, 0, tiled=True)]
    ppermute x6 -> x20, waiting for transfers between devices: 31.5 us -> 161 us  [shift(): return lax.ppermute(value, axis, [(p, (p + i) % n) for p in range(n)])]
    pallas_call x1, Pallas kernels: 73.1 us -> 47.8 us  [attend_backward(): pl.pallas_call(functools.partial(backward_kernel, part, units), grid_spec...]
    ppermute x6 -> x20, starting transfers between devices: 11.7 us -> 36.8 us  [shift(): return lax.ppermute(value, axis, [(p, (p + i) % n) for p in range(n)])]
    concatenate x2, local copies, waits for them, and re-layouts: 17.1 us -> 0.15 us  [the longest x1 0.08 us: on_device(): jnp.concatenate([vec_grads, up_shift_grad, jnp.zeros((d, TILE - 8 - block...]
    pallas_call x0 -> x2, Pallas kernels: none -> 16.9 us  [the longest x1 15.2 us: gradients(): pl.pallas_call(functools.partial(gradient_kernel, trios, blocks), grid=(2...]
    dot_general x5 -> x2, matrix products: 19.5 us -> 8.38 us  [outer_sum(): lax.dot_general(left_rows, right_rows, (((0,), (0,)), ((), ())), preferre...]
    pallas_call x1, Pallas kernels: 46 us -> 36.4 us  [attend_forward(): pl.pallas_call(functools.partial(forward_kernel, part, units), grid_spec=...]
  transfers between devices with their start and end apart: 14 -> 26, of which waited for: 10 -> 11; matrix products, arithmetic and copies ran while one was open for 26% -> 20% of each run, Pallas kernels for 24% -> 19%
where the time goes in v3:
time: 566 us; the launch traced here: 555 us
  waiting for transfers between devices  179 us (32%)
  Pallas kernels  118 us (21%)
  starting transfers between devices  69 us (12%)
  local copies, waits for them, and re-layouts  66.5 us (12%)
  matrix products  49.2 us (9%)
  blocking collectives  30 us (5%)
  other arithmetic  27.7 us (5%)
  between operations  15.3 us (3%)
    ppermute x20, waiting for transfers between devices, shift(): return lax.ppermute(value, axis, [(p, (p + i) % n) for p in range(n)])  161 us
    pallas_call x1, Pallas kernels, attend_backward(): pl.pallas_call(functools.partial(backward_kernel, part, units), grid_spec...  47.8 us
    ppermute x20, starting transfers between devices, shift(): return lax.ppermute(value, axis, [(p, (p + i) % n) for p in range(n)])  36.8 us
    pallas_call x1, Pallas kernels, attend_forward(): pl.pallas_call(functools.partial(forward_kernel, part, units), grid_spec=...  36.4 us
    all_to_all x3, starting transfers between devices, exchange(): lax.all_to_all(blocks_out.reshape(-1, width), 'unit', 0, 0, tiled=True)  32.1 us
    all_to_all x1, blocking collectives, exchange(): lax.all_to_all(blocks_out.reshape(-1, width), 'unit', 0, 0, tiled=True)  30 us
    dot_general x3, matrix products, inner_back(): lax.dot_general(grad_rows, weight, (((1,), (1,)), ((), ())), preferred_el...  25.4 us
    all_to_all x3, waiting for transfers between devices, exchange(): lax.all_to_all(blocks_out.reshape(-1, width), 'unit', 0, 0, tiled=True)  18.5 us
  transfers between devices with their start and end apart: 26, of which 11 were waited for; matrix products, arithmetic and copies ran while one was open for 20% of the time, Pallas kernels for 19%

profile of v3, /device:TPU:0, one launch (start us, length us, event | category | flops | bytes accessed | tf_op | source)
XLA Modules:
  0.0 555.2 jit_solution(15133650191058222150)
XLA Ops:
  7.2 2.1 reshape.340
  9.7 1.3 reshape.341
  13.8 1.8 pack_early.1
  16.4 6.1 %collective-permute-start = (bf16[24,768]{1,0:T(8,128)(2,1)S(1)}, bf16[24,768]{1,0:T(8,128)(2,1)S(1)}, u32[]{:S(2)}, u32[]{:S(2)}) collective-permute-start(bf16[24,768]{1,0:T(8,128)(2,1)S(1)} %get-tuple-element.116), channel_id=1, source_target_pairs={{0,14},{2,0},{4,2},{6,4},{8,6},{10,8},{12,10},{14,12},{1,15},{3,1}... | collective-permute-start | bytes 110600 | tf_op jit(solution)/shard_map/ppermute | solution.py:627
  22.9 3.0 collective-permute-start.3
  26.9 1.8 pad_maximum_fusion.2
  28.7 6.1 %all-to-all-start = ((bf16[8,256,768]{2,1,0:T(8,128)(2,1)}), bf16[8,256,768]{2,1,0:T(8,128)(2,1)}, u32[]{:S(2)}, u32[]{:S(2)}) async-start(bf16[8,256,768]{2,1,0:T(8,128)(2,1)} %pad_maximum_fusion.2), calls=%async_computation | async-start | bytes 6291456 | tf_op jit(solution)/shard_map/all_to_all | solution.py:621
  34.8 2.1 collective-permute-start.5
  36.9 1.5 collective-permute-start.6
  38.4 66.0 %collective-permute-done.5 = bf16[24,768]{1,0:T(8,128)(2,1)S(1)} collective-permute-done((bf16[24,768]{1,0:T(8,128)(2,1)S(1)}, bf16[24,768]{1,0:T(8,128)(2,1)S(1)}, u32[]{:S(2)}, u32[]{:S(2)}) %collective-permute-start.5) | collective-permute-done | bytes 36896 | tf_op jit(solution)/shard_map/ppermute | solution.py:627
  104.5 1.3 collective-permute-done.6
  107.4 1.4 collective-permute-start.7
  108.9 5.3 collective-permute-done.7
  115.8 1.5 collective-permute-done.8
  119.3 1.2 fusion.72
  120.5 13.6 %all-to-all-done.tok_ref = bf16[8,256,768]{2,1,0:T(8,128)(2,1)} async-done(((bf16[8,256,768]{2,1,0:T(8,128)(2,1)}), bf16[8,256,768]{2,1,0:T(8,128)(2,1)}, u32[]{:S(2)}, u32[]{:S(2)}) %all-to-all-start) | async-done | bytes 3145760 | tf_op jit(solution)/shard_map/all_to_all | solution.py:621
  134.0 9.6 %project.1 = (bf16[8,256,640]{2,1,0:T(8,128)(2,1)}, bf16[8,256,768]{2,1,0:T(8,128)(2,1)}, bf16[8,256,768]{2,1,0:T(8,128)(2,1)}) custom-call(bf16[8,256,768]{2,1,0:T(8,128)(2,1)} %all-to-all-done.tok_ref, bf16[768,768]{1,0:T(8,128)(2,1)} %bitcast.279, f32[1,640]{1,0:T(1,128)} %fusion.56.b_ref, f32[1,768]{1,0:T(1,128)} %get-tuple-element.124.gain_ref, ...), custom_call_target="tpu_custom_call" | custom-call | flops 2013265920 | bytes 12058624 | tf_op jit(solution)/shard_map/project/pallas_call | solution.py:94
  143.7 1.8 slice.217
  146.2 1.9 reduce.4
  148.0 2.1 copy.120
  152.2 1.2 fusion.25.norm_ref
  153.4 4.1 pad_maximum_fusion.1.kv_ref
  157.5 36.4 %attend_forward.1 = (bf16[8,256,256]{2,1,0:T(8,128)(2,1)}, f32[8,192,256]{2,1,0:T(8,128)}, f32[8,8,256]{2,1,0:T(8,128)}) custom-call(s32[17]{0:T(128)} %pad_add_fusion.meta, bf16[8,256,640]{2,1,0:T(8,128)(2,1)} %get-tuple-element.43.q_ref, bf16[8,512,512]{2,1,0:T(8,128)(2,1)} %pad_maximum_fusion.1.kv_ref, s32[8,1,256]{2,1,0:T(1,128)} %broadcast_in_dim.61.seg_ref), custom_call_target="tpu_custom_call" | custom-call | flops 12884901888 | bytes 20000000 | tf_op jit(solution)/shard_map/attend_forward/pallas_call | solution.py:391
  193.9 22.5 %all-to-all-start.1 = ((bf16[8,256,256]{2,1,0:T(8,128)(2,1)}), bf16[8,256,256]{2,1,0:T(8,128)(2,1)S(1)}, u32[]{:S(2)}, u32[]{:S(2)}) async-start(bf16[8,256,256]{2,1,0:T(8,128)(2,1)} %get-tuple-element.44), calls=%async_computation.1 | async-start | bytes 2097152 | tf_op jit(solution)/shard_map/all_to_all | solution.py:621
  216.5 6.2 %multiply_convert_fusion = (bf16[512,3072]{1,0:T(8,128)(2,1)}, f32[512,3072]{1,0:T(8,128)S(1)}) fusion(f32[3072]{0:T(1024)S(1)} %add.292, bf16[512,768]{1,0:T(8,128)(2,1)S(1)} %copy-done.19, bf16[768,6912]{1,0:T(8,128)(2,1)} %all-gather.3.cloned.1.call-done), kind=kOutput, calls=%fused_computation.7 | convolution fusion | flops 2425356288 | bytes 14954496 | tf_op jit(solution)/shard_map/dot_general | solution.py:34
  225.1 13.4 %fusion.5.pre_ref = bf16[512,3072]{1,0:T(8,128)(2,1)} fusion(f32[512,3072]{1,0:T(8,128)S(1)} %get-tuple-element.143, bf16[512,768]{1,0:T(8,128)(2,1)S(1)} %bitcast.290, f32[3072]{0:T(1024)S(1)} %add.292, bf16[768,768]{1,0:T(8,128)(2,1)S(1)} %get-tuple-element.94, bf16[768,768]{1,0:T(8,128)(2,1)S(1)} %get-tuple-element.95, ...), kind=kOutput, calls=%fused_computation.6 | convolution fusion | flops 2452094976 | bytes 14954496 | tf_op jit(solution)/shard_map/dot_general | solution.py:44
  238.5 5.0 all-to-all-done.1
  244.3 1.2 copy.151
  245.5 2.5 reduce.5
  248.4 7.3 %fusion.33 = (f32[512]{0:T(512)S(1)}, bf16[768]{0:T(1024)(128)(2,1)S(1)}, f32[512]{0:T(512)S(1)}, bf16[768]{0:T(1024)(128)(2,1)S(1)}, f32[512,768]{1,0:T(8,128)}) fusion(f32[768]{0:T(1024)S(1)} %get-tuple-element.125, f32[512]{0:T(512)S(1)} %bitcast.306, f32[512]{0:T(512)S(1)} %bitcast.310, bf16[256,2,768]{2,1,0:T(2,128)(2,1)S(1)} %copy-done, ...), kind=kOutput, calls=%fused_computation.52 | convolution fusion | flops 2419848704 | bytes 10237952 | tf_op jit(solution)/shard_map/dot_general | solution.py:44
  256.8 15.2 %gradients.1 = bf16[768,7040]{1,0:T(8,128)(2,1)} custom-call(bf16[512,768]{1,0:T(8,128)(2,1)} %fusion.25.norm_ref, bf16[512,3072]{1,0:T(8,128)(2,1)} %fusion.5.pre_ref, bf16[512,3072]{1,0:T(8,128)(2,1)} %get-tuple-element.46.hidden_ref, bf16[512,768]{1,0:T(8,128)(2,1)} %bitcast.289, bf16[512,1024]{1,0:T(8,128)(2,1)} %bitcast.296, ...), custom_call_target="tpu_custom_call" | custom-call | flops 5536481280 | bytes 21626880 | tf_op jit(solution)/shard_map/gradients/pallas_call | solution.py:528
  273.1 2.0 fusion.41
  275.1 1.5 copy.126
  276.5 30.0 %all_to_all.27.do_ref = bf16[8,256,256]{2,1,0:T(8,128)(2,1)} all-to-all(bf16[8,256,256]{2,1,0:T(8,128)(2,1)S(1)} %bitcast.283), channel_id=1, replica_groups=mesh['seq'=2,'unit'=8,'part'=2] {'unit'}, dimensions={0} | all-to-all | bytes 2097152 | tf_op jit(solution)/shard_map/all_to_all | solution.py:621
  306.6 47.8 %attend_backward.1 = (bf16[8,256,640]{2,1,0:T(8,128)(2,1)}, bf16[1,8,256,512]{3,2,1,0:T(8,128)(2,1)}) custom-call(s32[17]{0:T(128)} %pad_add_fusion.meta, bf16[8,256,640]{2,1,0:T(8,128)(2,1)} %get-tuple-element.43.q_ref, bf16[8,256,256]{2,1,0:T(8,128)(2,1)} %all_to_all.27.do_ref, f32[8,192,256]{2,1,0:T(8,128)} %get-tuple-element.48.ot_ref, ...), custom_call_target="tpu_custom_call" | custom-call | flops 32212254720 | bytes 20000000 | tf_op jit(solution)/shard_map/attend_backward/pallas_call | solution.py:430
  355.6 1.6 copy.146
  357.2 1.7 collective-permute-done.10.refs_1_
  358.9 7.5 %unturn.1 = bf16[8,256,640]{2,1,0:T(8,128)(2,1)} custom-call(bf16[8,256,640]{2,1,0:T(8,128)(2,1)} %get-tuple-element.52.refs_0_, bf16[8,256,512]{2,1,0:T(8,128)(2,1)} %collective-permute-done.10.refs_1_, f32[8,8,256]{2,1,0:T(8,128)} %get-tuple-element.137.cos_ref.refs_2_, f32[8,8,256]{2,1,0:T(8,128)} %get-tuple-element.136.sin_ref.refs_3_), custom_call_target="tpu_custom_call" | custom-call | tf_op jit(solution)/shard_map/unturn/pallas_call | solution.py:141
  366.4 2.4 convert_reduce_fusion
  369.1 4.3 fusion.10
  373.4 4.0 bitcast_convert_fusion
  377.5 1.3 maximum_maximum_fusion
  378.8 1.6 copy.132
  382.0 6.2 %fusion.45 = f32[512,768]{1,0:T(8,128)S(1)} fusion(bf16[512,3072]{1,0:T(8,128)(2,1)} %get-tuple-element.46.hidden_ref, bf16[768,768]{1,0:T(8,128)(2,1)S(1)} %copy-done.13, bf16[768,768]{1,0:T(8,128)(2,1)S(1)} %copy-done.15, bf16[768,768]{1,0:T(8,128)(2,1)} %copy-done.16, bf16[768,768]{1,0:T(8,128)(2,1)} %copy-done.17), kind=kOutput, calls=%fused_computation.64 | convolution fusion | flops 2434793472 | bytes 9437184 | tf_op jit(solution)/shard_map/dot_general | solution.py:34
  390.8 9.2 %collective-permute-done.12 = bf16[8,32,768]{2,1,0:T(8,128)(2,1)S(1)} collective-permute-done((bf16[8,32,768]{2,1,0:T(8,128)(2,1)S(1)}, bf16[8,32,768]{2,1,0:T(8,128)(2,1)S(1)}, u32[]{:S(2)}, u32[]{:S(2)}) %collective-permute-start.12) | collective-permute-done | bytes 393248 | tf_op jit(solution)/shard_map/ppermute | solution.py:627
  401.5 10.6 %collective-permute-start.13 = (bf16[32,768]{1,0:T(8,128)(2,1)}, bf16[32,768]{1,0:T(8,128)(2,1)S(1)}, u32[]{:S(2)}, u32[]{:S(2)}) collective-permute-start(bf16[32,768]{1,0:T(8,128)(2,1)} %get-tuple-element.104), channel_id=1, source_target_pairs={{0,14},{2,0},{4,2},{6,4},{8,6},{10,8},{12,10},{14,12},{1,15},{3,1}... | collective-permute-start | bytes 147464 | tf_op jit(solution)/shard_map/ppermute | solution.py:627
  412.7 1.7 copy.175
  414.4 3.6 all-to-all-start.3
  418.0 3.8 collective-permute-start.14
  422.3 3.3 collective-permute-start.16
  426.7 41.2 %collective-permute-done.14 = bf16[32,768]{1,0:T(8,128)(2,1)S(1)} collective-permute-done((bf16[32,768]{1,0:T(8,128)(2,1)}, bf16[32,768]{1,0:T(8,128)(2,1)S(1)}, u32[]{:S(2)}, u32[]{:S(2)}) %collective-permute-start.14) | collective-permute-done | bytes 49184 | tf_op jit(solution)/shard_map/ppermute | solution.py:627
  467.9 2.6 collective-permute-start.19
  470.5 32.4 %collective-permute-done.16 = bf16[32,768]{1,0:T(8,128)(2,1)S(1)} collective-permute-done((bf16[32,768]{1,0:T(8,128)(2,1)}, bf16[32,768]{1,0:T(8,128)(2,1)S(1)}, u32[]{:S(2)}, u32[]{:S(2)}) %collective-permute-start.16) | collective-permute-done | bytes 49184 | tf_op jit(solution)/shard_map/ppermute | solution.py:627
  503.0 1.9 collective-permute-done.17
  511.2 1.6 reshape.358
  517.9 1.6 pad_maximum_fusion.6
  519.5 1.6 slice.297
  521.2 3.3 reshape.363
  524.4 3.9 copy.137
  528.3 4.0 reshape.364
  535.4 1.5 fusion.69
  537.6 2.0 copy.138
  540.4 4.7 fusion.67
  546.3 1.7 copy.174
  (290 shorter events, 45.5 us)
Async XLA Ops:
  7.2 3.8 copy-start.21
  7.2 3.8 copy-start.22
  7.2 209.2 %all-gather.3.cloned.1.call-start = ((), (), s32[]{:S(2)}) async-start(), calls=%async_computation.5 | async-start | bytes 10948608 | tf_op jit(solution)/shard_map/all_gather | solution.py:704
  9.4 2.5 copy-start.32
  9.4 2.6 copy-start.34
  9.4 2.7 copy-start.35
  9.4 2.8 copy-start.36
  9.4 2.9 copy-start.37
  9.5 3.0 copy-start.38
  9.5 3.1 copy-start.39
  9.5 3.2 copy-start.40
  9.5 3.3 copy-start.41
  9.5 16.4 %copy-start = (bf16[256,2,768]{2,1,0:T(2,128)(2,1)S(1)}, bf16[256,2,768]{2,1,0:T(2,128)(2,1)}, u32[]{:S(2)}) copy-start(bf16[256,2,768]{2,1,0:T(2,128)(2,1)} %param.15) | copy-start | bytes 2359300
  16.4 18.4 %collective-permute-start = (bf16[24,768]{1,0:T(8,128)(2,1)S(1)}, bf16[24,768]{1,0:T(8,128)(2,1)S(1)}, u32[]{:S(2)}, u32[]{:S(2)}) collective-permute-start(bf16[24,768]{1,0:T(8,128)(2,1)S(1)} %get-tuple-element.116), channel_id=1, source_target_pairs={{0,14},{2,0},{4,2},{6,4},{8,6},{10,8},{12,10},{14,12},{1,15},{3,1}... | collective-permute-start | bytes 110600 | tf_op jit(solution)/shard_map/ppermute | solution.py:627
  22.5 14.4 %collective-permute-start.1 = (bf16[24,768]{1,0:T(8,128)(2,1)S(1)}, bf16[24,768]{1,0:T(8,128)(2,1)S(1)}, u32[]{:S(2)}, u32[]{:S(2)}) collective-permute-start(bf16[24,768]{1,0:T(8,128)(2,1)S(1)} %get-tuple-element.115), channel_id=1, source_target_pairs={{0,12},{2,14},{4,0},{6,2},{8,4},{10,6},{12,8},{14,10},{1,13},{3,15... | collective-permute-start | bytes 110600 | tf_op jit(solution)/shard_map/ppermute | solution.py:627
  22.9 15.4 %collective-permute-start.2 = (bf16[24,768]{1,0:T(8,128)(2,1)S(1)}, bf16[24,768]{1,0:T(8,128)(2,1)S(1)}, u32[]{:S(2)}, u32[]{:S(2)}) collective-permute-start(bf16[24,768]{1,0:T(8,128)(2,1)S(1)} %get-tuple-element.114), channel_id=1, source_target_pairs={{0,10},{2,12},{4,14},{6,0},{8,2},{10,4},{12,6},{14,8},{1,11},{3,13... | collective-permute-start | bytes 110600 | tf_op jit(solution)/shard_map/ppermute | solution.py:627
  22.9 15.5 %collective-permute-start.3 = (bf16[24,768]{1,0:T(8,128)(2,1)S(1)}, bf16[24,768]{1,0:T(8,128)(2,1)S(1)}, u32[]{:S(2)}, u32[]{:S(2)}) collective-permute-start(bf16[24,768]{1,0:T(8,128)(2,1)S(1)} %get-tuple-element.113), channel_id=1, source_target_pairs={{0,8},{2,10},{4,12},{6,14},{8,0},{10,2},{12,4},{14,6},{1,9},{3,11}... | collective-permute-start | bytes 110600 | tf_op jit(solution)/shard_map/ppermute | solution.py:627
  25.9 12.5 %collective-permute-start.4 = (bf16[24,768]{1,0:T(8,128)(2,1)S(1)}, bf16[24,768]{1,0:T(8,128)(2,1)S(1)}, u32[]{:S(2)}, u32[]{:S(2)}) collective-permute-start(bf16[24,768]{1,0:T(8,128)(2,1)S(1)} %get-tuple-element.112), channel_id=1, source_target_pairs={{0,6},{2,8},{4,10},{6,12},{8,14},{10,0},{12,2},{14,4},{1,7},{3,9},... | collective-permute-start | bytes 110600 | tf_op jit(solution)/shard_map/ppermute | solution.py:627
  26.0 0.9 copy-start.5
  28.7 105.3 %all-to-all-start = ((bf16[8,256,768]{2,1,0:T(8,128)(2,1)}), bf16[8,256,768]{2,1,0:T(8,128)(2,1)}, u32[]{:S(2)}, u32[]{:S(2)}) async-start(bf16[8,256,768]{2,1,0:T(8,128)(2,1)} %pad_maximum_fusion.2), calls=%async_computation | async-start | bytes 6291456 | tf_op jit(solution)/shard_map/all_to_all | solution.py:621
  34.8 69.6 %collective-permute-start.5 = (bf16[24,768]{1,0:T(8,128)(2,1)S(1)}, bf16[24,768]{1,0:T(8,128)(2,1)S(1)}, u32[]{:S(2)}, u32[]{:S(2)}) collective-permute-start(bf16[24,768]{1,0:T(8,128)(2,1)S(1)} %get-tuple-element.111), channel_id=1, source_target_pairs={{0,4},{2,6},{4,8},{6,10},{8,12},{10,14},{12,0},{14,2},{1,5},{3,7},... | collective-permute-start | bytes 110600 | tf_op jit(solution)/shard_map/ppermute | solution.py:627
  36.9 68.9 %collective-permute-start.6 = (bf16[24,768]{1,0:T(8,128)(2,1)S(1)}, bf16[24,768]{1,0:T(8,128)(2,1)S(1)}, u32[]{:S(2)}, u32[]{:S(2)}) collective-permute-start(bf16[24,768]{1,0:T(8,128)(2,1)S(1)} %get-tuple-element.110), channel_id=1, source_target_pairs={{0,2},{2,4},{4,6},{6,8},{8,10},{10,12},{12,14},{14,0},{1,3},{3,5},... | collective-permute-start | bytes 110600 | tf_op jit(solution)/shard_map/ppermute | solution.py:627
  107.4 6.9 %collective-permute-start.7 = (bf16[8,24,768]{2,1,0:T(8,128)(2,1)S(1)}, bf16[8,24,768]{2,1,0:T(8,128)(2,1)S(1)}, u32[]{:S(2)}, u32[]{:S(2)}) collective-permute-start(bf16[8,24,768]{2,1,0:T(8,128)(2,1)S(1)} %constant_dynamic-slice_fusion.2), channel_id=1, source_target_pairs={{0,16},{16,0},{1,17},{17,1},{2,18},{18,2},{3,19},{19,3},{4,20},{20... | collective-permute-start | bytes 884744 | tf_op jit(solution)/shard_map/ppermute | solution.py:627
  114.4 2.9 collective-permute-start.8
  117.6 16.4 %copy-start.1 = (bf16[2,8,2,24,768]{4,3,2,1,0:T(8,128)(2,1)}, bf16[2,8,2,24,768]{4,3,2,1,0:T(8,128)(2,1)S(1)}, u32[]{:S(2)}) copy-start(bf16[2,8,2,24,768]{4,3,2,1,0:T(8,128)(2,1)S(1)} %copy.115) | copy-start | bytes 3538948
  120.5 127.9 %copy-start.23 = (f32[768]{0:T(1024)}, f32[768]{0:T(1024)S(1)}, u32[]{:S(2)}) copy-start(f32[768]{0:T(1024)S(1)} %get-tuple-element.125) | copy-start | bytes 9220
  145.5 7.9 %collective-permute-start.9 = (bf16[8,256,512]{2,1,0:T(8,128)(2,1)S(1)}, bf16[8,256,512]{2,1,0:T(8,128)(2,1)}, u32[]{:S(2)}, u32[]{:S(2)}) collective-permute-start(bf16[8,256,512]{2,1,0:T(8,128)(2,1)S(1)} %slice.217), channel_id=1, source_target_pairs={{0,1},{1,0},{2,3},{3,2},{4,5},{5,4},{6,7},{7,6},{8,9},{9,8},{10,11... | collective-permute-start | bytes 6291464 | tf_op jit(solution)/shard_map/ppermute | solution.py:627
  146.1 102.2 %copy-start.25 = (f32[1,2,2,128]{3,1,2,0:T(2,128)}, f32[1,2,2,128]{3,1,2,0:T(2,128)S(1)}, u32[]{:S(2)}) copy-start(f32[1,2,2,128]{3,1,2,0:T(2,128)S(1)} %copy.150) | copy-start | bytes 6148
  146.2 102.2 %copy-start.27 = (f32[1,2,2,128]{3,1,2,0:T(2,128)}, f32[1,2,2,128]{3,1,2,0:T(2,128)S(1)}, u32[]{:S(2)}) copy-start(f32[1,2,2,128]{3,1,2,0:T(2,128)S(1)} %copy.149) | copy-start | bytes 6148
  193.9 22.5 %copy-start.19 = (bf16[512,768]{1,0:T(8,128)(2,1)S(1)}, bf16[512,768]{1,0:T(8,128)(2,1)}, u32[]{:S(2)}) copy-start(bf16[512,768]{1,0:T(8,128)(2,1)} %fusion.25.norm_ref) | copy-start | bytes 2359300
  193.9 49.6 %all-to-all-start.1 = ((bf16[8,256,256]{2,1,0:T(8,128)(2,1)}), bf16[8,256,256]{2,1,0:T(8,128)(2,1)S(1)}, u32[]{:S(2)}, u32[]{:S(2)}) async-start(bf16[8,256,256]{2,1,0:T(8,128)(2,1)} %get-tuple-element.44), calls=%async_computation.1 | async-start | bytes 2097152 | tf_op jit(solution)/shard_map/all_to_all | solution.py:621
  216.4 303.1 %reduce-scatter.4.cloned.1.call-start = ((), (), s32[]{:S(2)}) async-start(), calls=%async_computation.7 | async-start | bytes 11151360
  216.5 6.2 %copy-start.3 = (bf16[768,6912]{1,0:T(8,128)(2,1)S(1)}, bf16[768,6912]{1,0:T(8,128)(2,1)}, u32[]{:S(2)}) copy-start(bf16[768,6912]{1,0:T(8,128)(2,1)} %all-gather.3.cloned.1.call-done) | copy-start | bytes 31850500
  222.7 2.5 copy-start.7
  223.0 1.1 copy-start.12
  223.1 1.4 copy-start.14
  223.1 1.7 copy-start.16
  223.1 2.1 copy-start.17
  271.9 1.1 copy-start.4
  272.0 268.2 %all-gather.5.cloned.1.call-start = ((), (), s32[]{:S(2)}) async-start(), calls=%async_computation.6 | async-start | bytes 4055040 | tf_op jit(solution)/shard_map/all_gather | solution.py:705
  306.6 47.9 %copy-start.2 = (bf16[2,8,2,24,768]{4,3,2,1,0:T(8,128)(2,1)S(1)}, bf16[2,8,2,24,768]{4,3,2,1,0:T(8,128)(2,1)}, u32[]{:S(2)}) copy-start(bf16[2,8,2,24,768]{4,3,2,1,0:T(8,128)(2,1)} %copy-done.1) | copy-start | bytes 3538948
  354.4 4.5 collective-permute-start.10
  366.3 2.7 copy-start.43
  369.0 4.4 copy-start.42
  380.3 1.3 copy-start.13
  380.3 1.6 copy-start.15
  380.5 7.8 %collective-permute-start.11 = (bf16[2,8,32,768]{3,2,1,0:T(8,128)(2,1)S(1)}, bf16[2,8,32,768]{3,2,1,0:T(8,128)(2,1)S(1)}, u32[]{:S(2)}, u32[]{:S(2)}) collective-permute-start(bf16[2,8,32,768]{3,2,1,0:T(8,128)(2,1)S(1)} %fusion.47), channel_id=1, source_target_pairs={{0,1},{1,0},{2,3},{3,2},{4,5},{5,4},{6,7},{7,6},{8,9},{9,8},{10,11... | collective-permute-start | bytes 2359304 | tf_op jit(solution)/shard_map/ppermute | solution.py:627
  388.3 1.1 copy-start.6
  388.3 1.5 copy-start.18
  388.6 11.4 %collective-permute-start.12 = (bf16[8,32,768]{2,1,0:T(8,128)(2,1)S(1)}, bf16[8,32,768]{2,1,0:T(8,128)(2,1)S(1)}, u32[]{:S(2)}, u32[]{:S(2)}) collective-permute-start(bf16[8,32,768]{2,1,0:T(8,128)(2,1)S(1)} %dynamic-slice_bitcast_fusion), channel_id=1, source_target_pairs={{0,16},{16,0},{1,17},{17,1},{2,18},{18,2},{3,19},{19,3},{4,20},{20... | collective-permute-start | bytes 1179656 | tf_op jit(solution)/shard_map/ppermute | solution.py:627
  401.5 24.1 %collective-permute-start.13 = (bf16[32,768]{1,0:T(8,128)(2,1)}, bf16[32,768]{1,0:T(8,128)(2,1)S(1)}, u32[]{:S(2)}, u32[]{:S(2)}) collective-permute-start(bf16[32,768]{1,0:T(8,128)(2,1)} %get-tuple-element.104), channel_id=1, source_target_pairs={{0,14},{2,0},{4,2},{6,4},{8,6},{10,8},{12,10},{14,12},{1,15},{3,1}... | collective-permute-start | bytes 147464 | tf_op jit(solution)/shard_map/ppermute | solution.py:627
  414.4 123.2 %all-to-all-start.3 = ((bf16[8,256,640]{2,1,0:T(8,128)(2,1)}), bf16[8,256,640]{2,1,0:T(8,128)(2,1)S(1)}, u32[]{:S(2)}, u32[]{:S(2)}) async-start(bf16[8,256,640]{2,1,0:T(8,128)(2,1)} %unturn.1), calls=%async_computation.3 | async-start | bytes 5242880 | tf_op jit(solution)/shard_map/all_to_all | solution.py:621
  418.0 49.9 %collective-permute-start.14 = (bf16[32,768]{1,0:T(8,128)(2,1)}, bf16[32,768]{1,0:T(8,128)(2,1)S(1)}, u32[]{:S(2)}, u32[]{:S(2)}) collective-permute-start(bf16[32,768]{1,0:T(8,128)(2,1)} %get-tuple-element.103), channel_id=1, source_target_pairs={{0,12},{2,14},{4,0},{6,2},{8,4},{10,6},{12,8},{14,10},{1,13},{3,15... | collective-permute-start | bytes 147464 | tf_op jit(solution)/shard_map/ppermute | solution.py:627
  421.8 48.7 %collective-permute-start.15 = (bf16[32,768]{1,0:T(8,128)(2,1)}, bf16[32,768]{1,0:T(8,128)(2,1)S(1)}, u32[]{:S(2)}, u32[]{:S(2)}) collective-permute-start(bf16[32,768]{1,0:T(8,128)(2,1)} %get-tuple-element.102), channel_id=1, source_target_pairs={{0,10},{2,12},{4,14},{6,0},{8,2},{10,4},{12,6},{14,8},{1,11},{3,13... | collective-permute-start | bytes 147464 | tf_op jit(solution)/shard_map/ppermute | solution.py:627
  422.3 80.6 %collective-permute-start.16 = (bf16[32,768]{1,0:T(8,128)(2,1)}, bf16[32,768]{1,0:T(8,128)(2,1)S(1)}, u32[]{:S(2)}, u32[]{:S(2)}) collective-permute-start(bf16[32,768]{1,0:T(8,128)(2,1)} %get-tuple-element.101), channel_id=1, source_target_pairs={{0,8},{2,10},{4,12},{6,14},{8,0},{10,2},{12,4},{14,6},{1,9},{3,11}... | collective-permute-start | bytes 147464 | tf_op jit(solution)/shard_map/ppermute | solution.py:627
  425.6 79.3 %collective-permute-start.17 = (bf16[32,768]{1,0:T(8,128)(2,1)}, bf16[32,768]{1,0:T(8,128)(2,1)S(1)}, u32[]{:S(2)}, u32[]{:S(2)}) collective-permute-start(bf16[32,768]{1,0:T(8,128)(2,1)} %get-tuple-element.100), channel_id=1, source_target_pairs={{0,6},{2,8},{4,10},{6,12},{8,14},{10,0},{12,2},{14,4},{1,7},{3,9},... | collective-permute-start | bytes 147464 | tf_op jit(solution)/shard_map/ppermute | solution.py:627
  425.6 79.3 %collective-permute-start.18 = (bf16[32,768]{1,0:T(8,128)(2,1)S(1)}, bf16[32,768]{1,0:T(8,128)(2,1)S(1)}, u32[]{:S(2)}, u32[]{:S(2)}) collective-permute-start(bf16[32,768]{1,0:T(8,128)(2,1)S(1)} %get-tuple-element.99), channel_id=1, source_target_pairs={{0,4},{2,6},{4,8},{6,10},{8,12},{10,14},{12,0},{14,2},{1,5},{3,7},... | collective-permute-start | bytes 147464 | tf_op jit(solution)/shard_map/ppermute | solution.py:627
  467.9 37.0 %collective-permute-start.19 = (bf16[32,768]{1,0:T(8,128)(2,1)S(1)}, bf16[32,768]{1,0:T(8,128)(2,1)S(1)}, u32[]{:S(2)}, u32[]{:S(2)}) collective-permute-start(bf16[32,768]{1,0:T(8,128)(2,1)S(1)} %get-tuple-element.98), channel_id=1, source_target_pairs={{0,2},{2,4},{4,6},{6,8},{8,10},{10,12},{12,14},{14,0},{1,3},{3,5},... | collective-permute-start | bytes 147464 | tf_op jit(solution)/shard_map/ppermute | solution.py:627
  535.4 12.6 %copy-start.33 = (f32[24]{0:T(128)}, f32[24]{0:T(128)S(1)}, u32[]{:S(2)}) copy-start(f32[24]{0:T(128)S(1)} %get-tuple-element.179) | copy-start | bytes 292
  540.4 4.7 copy-start.8
  540.4 4.7 copy-start.10
  540.4 4.7 copy-start.24
  540.4 4.8 copy-start.29
  540.4 4.8 copy-start.30
  (6 other events, 4.2 us)
Sparse Core Ops, SparseCore 0:
  11.9 139.5 all-gather.2
  272.1 140.9 reduce-scatter.3
  416.0 87.8 all-gather.4

commit v4 on v3

--- a/solution.py
+++ b/solution.py
@@ -68,7 +68,7 @@
 
 
 def project_kernel(
-    tok_ref, w_ref, b_ref, gain_ref, bias_ref, cos_ref, sin_ref, out_ref, norm_ref, hat_ref
+    tok_ref, w_ref, b_ref, gain_ref, bias_ref, cos_ref, sin_ref, out_ref, kv_ref, norm_ref, hat_ref
 ):
     x = tok_ref[0].astype(F32)
     centre = x - jnp.mean(x, -1, keepdims=True)
@@ -83,11 +83,15 @@
         tile = y[:, t * TILE : (t + 1) * TILE]
         if t in (0, 1, 3):
             tile = turn(tile, cos, sin)
-        out_ref[0, :, t * TILE : (t + 1) * TILE] = tile.astype(BF)
+        tile = tile.astype(BF)
+        out_ref[0, :, t * TILE : (t + 1) * TILE] = tile
+        if t > 0:
+            kv_ref[0, :, (t - 1) * TILE : t * TILE] = tile
 
 
 def project(toks, weight, bias, gain, offset, cos, sin):
-    units, rows, d = toks.shape
+    units, unused, d = toks.shape
+    rows = cos.shape[2]
     tok_spec = pl.BlockSpec((1, rows, d), lambda j: (j, 0, 0))
     row_spec = pl.BlockSpec((1, d), lambda j: (0, 0))
     turn_spec = pl.BlockSpec((1, ROT // 2, rows), lambda j: (j, 0, 0))
@@ -103,9 +107,15 @@
             turn_spec,
             turn_spec,
         ],
-        out_specs=[pl.BlockSpec((1, rows, PACK), lambda j: (j, 0, 0)), tok_spec, tok_spec],
+        out_specs=[
+            pl.BlockSpec((1, rows, PACK), lambda j: (j, 0, 0)),
+            pl.BlockSpec((1, rows, PACK - TILE), lambda j: (j, 0, 0)),
+            tok_spec,
+            tok_spec,
+        ],
         out_shape=[
             jax.ShapeDtypeStruct((units, rows, PACK), BF),
+            jax.ShapeDtypeStruct((units, rows, PACK - TILE), BF),
             jax.ShapeDtypeStruct((units, rows, d), BF),
             jax.ShapeDtypeStruct((units, rows, d), BF),
         ],
@@ -208,15 +218,27 @@
     lax.fori_loop(first, j + 1, one, 0)
 
 
-def forward_kernel(
-    part, units, meta, q_ref, kv_ref, seg_ref, o_ref, ot_ref, lse_ref, qb, vt, top, total, acc
-):
+def join_parts(part, refs, kv_ref):
+    rows = refs[0].shape[1]
+
+    def one(unit, unused):
+        for i in range(part):
+            kv_ref[unit, i * rows : (i + 1) * rows] = refs[i][unit]
+        return unused
+
+    lax.fori_loop(0, refs[0].shape[0], one, 0)
+
+
+def forward_kernel(part, units, meta, q_ref, *refs):
+    seg_ref, o_ref, ot_ref, lse_ref, kv_ref, qb, vt, top, total, acc = refs[part:]
     rows = q_ref.shape[1]
     c = meta[2 * units]
     j = pl.program_id(0)
 
     @pl.when(j == 0)
     def _():
+        join_parts(part, refs[:part], kv_ref)
+
         def turn_values(unit, unused):
             vt[unit, :TILE] = flip(kv_ref[unit, :, TILE : 2 * TILE]).astype(BF)
             vt[unit, TILE:] = flip(kv_ref[unit, :, 3 * TILE :])[:HEAD_DIM].astype(BF)
@@ -262,36 +284,17 @@
     o_ref[0, :, TILE:] = jnp.concatenate([out[2], jnp.zeros_like(out[2])], 0).T.astype(BF)
 
 
-def backward_kernel(
-    part,
-    units,
-    meta,
-    q_ref,
-    do_ref,
-    ot_ref,
-    lse_ref,
-    kv_ref,
-    seg_ref,
-    own_ref,
-    oth_ref,
-    qb,
-    db,
-    qn,
-    dn,
-    kt,
-    delta,
-    dqt,
-    dk01,
-    dv01,
-    dk2,
-    dv2,
-):
+def backward_kernel(part, units, meta, q_ref, do_ref, ot_ref, lse_ref, *refs):
+    seg_ref, own_ref, oth_ref, kv_ref, qb, db, qn, dn, kt, delta, dqt = refs[part : part + 11]
+    dk01, dv01, dk2, dv2 = refs[part + 11 :]
     rows = q_ref.shape[1]
     c = meta[2 * units]
     j = pl.program_id(0)
 
     @pl.when(j == 0)
     def _():
+        join_parts(part, refs[:part], kv_ref)
+
         def turn_keys(unit, unused):
             kt[unit, :TILE] = flip(kv_ref[unit, :, 0:TILE]).astype(BF)
             kt[unit, TILE:] = flip(kv_ref[unit, :, 2 * TILE : 3 * TILE])[HEAD_DIM:].astype(BF)
@@ -387,7 +390,7 @@
 
 def attend_forward(meta, packed, kv, seg):
     units, rows, unused = packed.shape
-    part = kv.shape[1] // rows
+    part = len(kv)
     return pl.pallas_call(
         functools.partial(forward_kernel, part, units),
         grid_spec=pltpu.PrefetchScalarGridSpec(
@@ -395,7 +398,7 @@
             grid=(units,),
             in_specs=[
                 pl.BlockSpec((1, rows, PACK), lambda j, meta: (j, 0, 0)),
-                whole_spec(kv.shape),
+                *[whole_spec(piece.shape) for piece in kv],
                 pl.BlockSpec((1, 1, rows), lambda j, meta: (j, 0, 0)),
             ],
             out_specs=[
@@ -404,6 +407,7 @@
                 pl.BlockSpec((1, 8, rows), lambda j, meta: (j, 0, 0)),
             ],
             scratch_shapes=[
+                pltpu.VMEM((units, part * rows, PACK - TILE), BF),
                 pltpu.VMEM((TRIO, TILE, rows), BF),
                 pltpu.VMEM((units, TRIO * HEAD_DIM, part * rows), BF),
                 pltpu.VMEM((8, rows), F32),
@@ -419,12 +423,12 @@
         compiler_params=params_of("arbitrary"),
         cost_estimate=attention_cost(8, units, rows, part),
         name="attend_forward",
-    )(meta, packed, kv, seg)
+    )(meta, packed, *kv, seg)
 
 
 def attend_backward(meta, packed, dout, out_t, lse, kv, seg):
     units, rows, unused = packed.shape
-    part = kv.shape[1] // rows
+    part = len(kv)
     others = (max(part - 1, 1), units, rows, 4 * TILE)
     grads = pltpu.VMEM((units, part * rows, TILE), F32)
     return pl.pallas_call(
@@ -437,11 +441,12 @@
                 pl.BlockSpec((1, rows, OPACK), lambda j, meta: (j, 0, 0)),
                 pl.BlockSpec((1, TRIO * HEAD_DIM, rows), lambda j, meta: (j, 0, 0)),
                 pl.BlockSpec((1, 8, rows), lambda j, meta: (j, 0, 0)),
-                whole_spec(kv.shape),
+                *[whole_spec(piece.shape) for piece in kv],
                 pl.BlockSpec((1, 1, rows), lambda j, meta: (j, 0, 0)),
             ],
             out_specs=[whole_spec(packed.shape), whole_spec(others)],
             scratch_shapes=[
+                pltpu.VMEM((units, part * rows, PACK - TILE), BF),
                 pltpu.VMEM((TRIO, TILE, rows), BF),
                 pltpu.VMEM((TRIO, TILE, rows), BF),
                 pltpu.VMEM((TRIO * rows, TILE), BF),
@@ -462,7 +467,7 @@
         compiler_params=params_of("arbitrary"),
         cost_estimate=attention_cost(20, units, rows, part),
         name="attend_backward",
-    )(meta, packed, dout, out_t, lse, kv, seg)
+    )(meta, packed, dout, out_t, lse, *kv, seg)
 
 
 def pack_kernel(trios, groups, w_ref, vec_ref, early_ref, local_ref):
@@ -497,53 +502,174 @@
     )(weight, vec)
 
 
+def feed_kernel(
+    x_ref, cot_ref, up_ref, down_ref, shift_ref, hid_ref, pre_ref, sum_ref, second_ref, back_ref
+):
+    pre = mm(x_ref[...], up_ref[...]) + shift_ref[...]
+    grad = inner_back(cot_ref[...], down_ref[...])
+    cdf = 0.5 * (1.0 + lax.erf(pre * math.sqrt(0.5)))
+    hidden = (pre * cdf).astype(BF)
+    slope = cdf + pre * (jnp.exp(-0.5 * pre * pre) * (1.0 / math.sqrt(2.0 * math.pi)))
+    pre_grad = (grad * slope).astype(BF)
+    hid_ref[...] = hidden
+    pre_ref[...] = pre_grad
+    sum_ref[...] = jnp.sum(pre_grad.astype(F32), 0, keepdims=True)
+    second = mm(hidden, down_ref[...])
+    back = inner_back(pre_grad, up_ref[...])
+
+    @pl.when(pl.program_id(0) == 0)
+    def _():
+        second_ref[...] = second
+        back_ref[...] = back
+
+    @pl.when(pl.program_id(0) > 0)
+    def _():
+        second_ref[...] += second
+        back_ref[...] += back
+
+
+def feed_forward(x, cot, weights, shift, blocks):
+    rows, d = x.shape
+    ff = blocks * d
+    half = d // 2
+    wide = pl.BlockSpec((rows, d), lambda i: (0, 0))
+    column = pl.BlockSpec((rows, half), lambda i: (0, i))
+    line = pl.BlockSpec((1, half), lambda i: (0, i))
+    return pl.pallas_call(
+        feed_kernel,
+        grid=(2 * blocks,),
+        in_specs=[
+            wide,
+            wide,
+            pl.BlockSpec((d, half), lambda i: (0, i)),
+            pl.BlockSpec((half, d), lambda i: (i % 2, blocks + i // 2)),
+            line,
+        ],
+        out_specs=[column, column, line, wide, wide],
+        out_shape=[
+            jax.ShapeDtypeStruct((rows, ff), BF),
+            jax.ShapeDtypeStruct((rows, ff), BF),
+            jax.ShapeDtypeStruct((1, ff), F32),
+            jax.ShapeDtypeStruct((rows, d), F32),
+            jax.ShapeDtypeStruct((rows, d), F32),
+        ],
+        compiler_params=params_of("arbitrary"),
+        cost_estimate=pl.CostEstimate(
+            flops=8 * rows * d * ff, bytes_accessed=4 * d * ff, transcendentals=2 * rows * ff
+        ),
+        name="feed_forward",
+    )(x, cot, weights, weights, shift)
+
+
 def gradient_kernel(
-    trios, blocks, norm_ref, pre_ref, hidden_ref, cot_ref, att_ref, vec_ref, out_ref
+    trios, ups, per, norm_ref, pre_ref, hidden_ref, cot_ref, att_ref, cols_ref, out_ref
 ):
     i = pl.program_id(0)
-    d = cot_ref.shape[1]
-    where = pl.ds(pl.multiple_of(i * d, d), d)
-
-    @pl.when(i < blocks)
+    d = norm_ref.shape[1]
+
+    @pl.when(i < ups)
     def _():
-        out_ref[:, where] = outer_sum(norm_ref[...], pre_ref[...]).astype(BF)
-
-    @pl.when((i >= blocks) & (i < 2 * blocks))
+        out_ref[...] = outer_sum(norm_ref[...], pre_ref[...]).astype(BF)
+
+    @pl.when((i >= ups) & (i < 2 * ups))
     def _():
-        out_ref[:, where] = outer_sum(hidden_ref[...], cot_ref[...]).astype(BF)
-
-    @pl.when(i == 2 * blocks)
+        out_ref[...] = outer_sum(hidden_ref[...], cot_ref[...]).astype(BF)
+
+    @pl.when(i == 2 * ups)
     def _():
         width = d // trios
         for g in range(trios):
-            part = outer_sum(att_ref[:, g * OPACK : (g + 1) * OPACK], cot_ref[...])
-            out_ref[g * width : (g + 1) * width, where] = part[:width].astype(BF)
-        out_ref[:, (2 * blocks + 1) * d :] = vec_ref[...]
-
-
-def gradients(normed, pre_grad, hidden, cot, attended, vec, trios):
+            part = outer_sum(att_ref[:, g * OPACK : (g + 1) * OPACK], cols_ref[...])
+            out_ref[g * width : (g + 1) * width] = part[:width].astype(BF)
+
+
+def gradients(normed, pre_grad, hidden, cot, attended, cols, trios):
     rows, d = normed.shape
-    blocks = hidden.shape[1] // d
-    width = (2 * blocks + 1) * d + TILE
+    width = cols.shape[1]
+    per = d // width
+    ups = hidden.shape[1] // width
+
+    def down(i):
+        return jnp.clip(i - ups, 0, ups - 1)
+
     return pl.pallas_call(
-        functools.partial(gradient_kernel, trios, blocks),
-        grid=(2 * blocks + 1,),
+        functools.partial(gradient_kernel, trios, ups, per),
+        grid=(2 * ups + 1,),
         in_specs=[
             pl.BlockSpec((rows, d), lambda i: (0, 0)),
-            pl.BlockSpec((rows, d), lambda i: (0, jnp.minimum(i, blocks - 1))),
-            pl.BlockSpec((rows, d), lambda i: (0, jnp.clip(i - blocks, 0, blocks - 1))),
-            pl.BlockSpec((rows, d), lambda i: (0, 0)),
+            pl.BlockSpec((rows, width), lambda i: (0, jnp.minimum(i, ups - 1))),
+            pl.BlockSpec((rows, d), lambda i: (0, down(i) // per)),
+            pl.BlockSpec((rows, width), lambda i: (0, down(i) % per)),
             pl.BlockSpec(attended.shape, lambda i: (0, 0)),
-            pl.BlockSpec((d, TILE), lambda i: (0, 0)),
-        ],
-        out_specs=pl.BlockSpec((d, width), lambda i: (0, 0)),
-        out_shape=jax.ShapeDtypeStruct((d, width), BF),
+            pl.BlockSpec((rows, width), lambda i: (0, 0)),
+        ],
+        out_specs=pl.BlockSpec((d, width), lambda i: (0, i)),
+        out_shape=jax.ShapeDtypeStruct((d, (2 * ups + 1) * width), BF),
         compiler_params=params_of("arbitrary"),
         cost_estimate=pl.CostEstimate(
-            flops=2 * rows * d * width, bytes_accessed=4 * d * width, transcendentals=0
+            flops=2 * rows * d * (2 * ups + 1) * width, bytes_accessed=0, transcendentals=0
         ),
         name="gradients",
-    )(normed, pre_grad, hidden, cot, attended, vec)
+    )(normed, pre_grad, hidden, cot, attended, cols)
+
+
+def trio_kernel(norm_ref, hat_ref, grad_ref, w_ref, vec_ref, late_ref, shift_ref, own, hat):
+    j = pl.program_id(0)
+    d = norm_ref.shape[2]
+    grad = grad_ref[...].reshape(-1, PACK)
+    own_part = outer_sum(norm_ref[...].reshape(-1, d), grad)
+    hat_part = outer_sum(hat_ref[...].reshape(-1, d), grad)
+    sums = jnp.sum(grad.astype(F32), 0, keepdims=True)
+
+    @pl.when(j == 0)
+    def _():
+        own[...] = own_part
+        hat[...] = hat_part
+        shift_ref[...] = sums
+
+    @pl.when(j > 0)
+    def _():
+        own[...] += own_part
+        hat[...] += hat_part
+        shift_ref[...] += sums
+
+    @pl.when(j == pl.num_programs(0) - 1)
+    def _():
+        late_ref[:, :PACK] = own[...].astype(BF)
+        weight = w_ref[...].astype(F32)
+        lane = lane_of(vec_ref.shape)
+        vec = vec_ref[...]
+        vec = jnp.where(lane == 0, jnp.sum(weight * hat[...], 1, keepdims=True), vec)
+        vec = jnp.where(lane == 1, jnp.sum(weight * shift_ref[...], 1, keepdims=True), vec)
+        late_ref[:, PACK:] = vec.astype(BF)
+
+
+def trio_gradient(normed, hat, grad, weight, vec):
+    units, rows, d = normed.shape
+    tok_spec = pl.BlockSpec((2, rows, d), lambda j: (j, 0, 0))
+    return pl.pallas_call(
+        trio_kernel,
+        grid=(units // 2,),
+        in_specs=[
+            tok_spec,
+            tok_spec,
+            pl.BlockSpec((2, rows, PACK), lambda j: (j, 0, 0)),
+            pl.BlockSpec((d, PACK), lambda j: (0, 0)),
+            pl.BlockSpec((d, TILE), lambda j: (0, 0)),
+        ],
+        out_specs=[
+            pl.BlockSpec((d, PACK + TILE), lambda j: (0, 0)),
+            pl.BlockSpec((1, PACK), lambda j: (0, 0)),
+        ],
+        scratch_shapes=[pltpu.VMEM((d, PACK), F32), pltpu.VMEM((d, PACK), F32)],
+        out_shape=[
+            jax.ShapeDtypeStruct((d, PACK + TILE), BF),
+            jax.ShapeDtypeStruct((1, PACK), F32),
+        ],
+        compiler_params=params_of("arbitrary"),
+        cost_estimate=pl.CostEstimate(flops=0, bytes_accessed=0, transcendentals=0),
+        name="trio_gradient",
+    )(normed, hat, grad, weight, vec)
 
 
 def pack_columns(matrix, trios):
@@ -638,12 +764,22 @@
         got = [value] + [shift(value, axis, i) for i in range(1, n)]
         return natural_order(got, lax.axis_index(axis))
 
-    def exchange_small(value):
-        got = []
-        for i in range(units):
-            piece = lax.dynamic_index_in_dim(value, (unit + i) % units, 0, False)
-            got.append(shift(piece, "unit", i) if i else piece)
-        return natural_order(got, unit)
+    def swap_parts(value):
+        got = [lax.dynamic_index_in_dim(value, c, 0, False)]
+        for i in range(1, part):
+            piece = lax.dynamic_index_in_dim(value, (c + i) % part, 0, False)
+            got.append(shift(piece, "part", i))
+        return natural_order(got, c)
+
+    def all_parts(value):
+        return jnp.concatenate([value] + [shift(value, "part", i) for i in range(1, part)], 0)
+
+    def sum_parts(value):
+        n = value.shape[0] // part
+        total = value[:n]
+        for i in range(1, part):
+            total = total + shift(value[i * n : (i + 1) * n], "part", part - i)
+        return total
 
     def scatter_small(value, axis):
         n = lax.axis_size(axis)
@@ -660,7 +796,6 @@
         1,
     )
     token_rows = tokens.transpose(1, 0, 2)
-    toks = exchange(jnp.concatenate([token_rows] * trios, 0))
     seg_rows = segment.T
     seg_lanes = -(-2 * rows // r)
     seg_pack = jnp.concatenate([seg_rows // 64, seg_rows % 64], 1).astype(BF)
@@ -676,7 +811,9 @@
         -1,
     )
     early, qkv_local = pack_early(qkv_weight, vec, trios)
-    early = exchange_small(early)
+    toks = jnp.concatenate([jnp.concatenate([token_rows] * trios, 0), early], 1)
+    toks = exchange(toks)
+    early = toks[:, rows:]
 
     seg_mine = early[:, :, PACK + 16 : PACK + 16 + seg_lanes].astype(jnp.int32)
     seg_mine = seg_mine.reshape(units, r * seg_lanes)
@@ -695,16 +832,26 @@
     up_shift = split_hidden(vec_full[:, 9 : 9 + blocks].reshape(1, ff), count, r)
 
     feed_blocks = output_feed_weight.reshape(blocks, r, d)
-    second_pack = jnp.concatenate(
-        [split_hidden(fc1_weight, count, r)]
-        + [feed_blocks[b] for b in range(blocks)]
-        + [dense_weight],
-        1,
-    )
-    second = lax.all_gather(second_pack, ALL_AXES, axis=0, tiled=True)
-    qkv_full = lax.all_gather(qkv_local, ALL_AXES, axis=0, tiled=True)
+    first_pack = jnp.concatenate([qkv_local, dense_weight], 1)
+    first = lax.all_gather(first_pack, ALL_AXES, axis=0, tiled=True)
+    half = blocks // part
+    up_local = split_hidden(fc1_weight, count, r)
+    second_pack = jnp.stack(
+        [
+            jnp.concatenate(
+                [up_local[:, p * half * d : (p + 1) * half * d]]
+                + [feed_blocks[b] for b in range(p * half, (p + 1) * half)],
+                1,
+            )
+            for p in range(part)
+        ]
+    )
+    second_pack = swap_parts(second_pack).reshape(part * r, 2 * half * d)
+    second_pack, toks = lax.optimization_barrier((second_pack, toks))
+    second = lax.all_gather(second_pack, ("seq", "unit"), axis=0, tiled=True)
+    qkv_full = first[:, : trios * PACK]
     dense_pad = jnp.pad(
-        second[:, 2 * ff :].reshape(trios, d // trios, d),
+        first[:, trios * PACK :].reshape(trios, d // trios, d),
         ((0, 0), (0, OPACK - d // trios), (0, 0)),
     )
 
@@ -716,13 +863,10 @@
     cos = jnp.cos(angles)
     sin = jnp.sin(angles)
 
-    packed, normed_one, hat_one = project(
+    packed, kv_own, normed_one, hat_one = project(
         toks, trio_full, qkv_shift, gain_one, bias_one, cos, sin
     )
-    kv_own = packed[:, :, TILE:]
-    kv = jnp.concatenate([kv_own] + [shift(kv_own, "part", i) for i in range(1, part)], 1)
-    out_low, out_t, lse = attend_forward(meta, packed, kv, seg_mine)
-    attended = exchange(out_low)
+    kv = [kv_own] + [shift(kv_own, "part", i) for i in range(1, part)]
 
     x = token_rows.reshape(all_rows, d).astype(F32)
     cot = cotangent.transpose(1, 0, 2).reshape(all_rows, d)
@@ -734,24 +878,25 @@
     attended_grad = jnp.einsum(
         "sld,gkd->gslk", cot.reshape(groups, rows, d), dense_pad, preferred_element_type=F32
     ).astype(BF)
+    attended_grad, meta = lax.optimization_barrier((attended_grad, meta))
     dout = exchange(attended_grad.reshape(units, rows, OPACK))
-
-    up_full = second[:, :ff]
-    down_full = jnp.concatenate(
-        [second[:, ff + b * d : ff + (b + 1) * d] for b in range(blocks)], 0
-    )
-    hidden_pre = mm(normed_two, up_full) + up_shift
-    cdf = 0.5 * (1.0 + lax.erf(hidden_pre * math.sqrt(0.5)))
-    hidden_low = (hidden_pre * cdf).astype(BF)
-    slope = cdf + hidden_pre * (
-        jnp.exp(-0.5 * hidden_pre * hidden_pre) * (1.0 / math.sqrt(2.0 * math.pi))
-    )
-    pre_grad = (inner_back(cot, down_full) * slope).astype(BF)
+    out_low, out_t, lse = attend_forward(meta, packed, kv, seg_mine)
+    dout, out_low = lax.optimization_barrier((dout, out_low))
+    attended = exchange(out_low)
+
+    normed_two, dout = lax.optimization_barrier((normed_two, dout))
+    normed_all = all_parts(normed_two)
+    cot_all = all_parts(cot)
+    up_shift = lax.dynamic_slice_in_dim(up_shift, c * half * d, half * d, 1)
+    hidden_low, pre_grad, up_shift_grad, second_branch, normed_two_grad = feed_forward(
+        normed_all, cot_all, second, up_shift, half
+    )
     hidden_low, pre_grad, attended = lax.optimization_barrier((hidden_low, pre_grad, attended))
-    second_branch = mm(hidden_low, down_full) + down_shift
-    up_shift_grad = jnp.sum(pre_grad.astype(F32), 0)
-    normed_two_grad = inner_back(pre_grad, up_full)
-    cot_sum = jnp.sum(cot_float, 0)
+    second_branch = sum_parts(second_branch)
+    normed_two_grad = sum_parts(normed_two_grad)
+    up_shift_grad = lax.dynamic_update_slice_in_dim(
+        jnp.zeros((1, ff), F32), up_shift_grad, c * half * d, 1
+    )
 
     def norm_back(grad, gain):
         gy = grad * gain
@@ -759,86 +904,88 @@
             gy - jnp.mean(gy, -1, keepdims=True) - xhat * jnp.mean(gy * xhat, -1, keepdims=True)
         )
 
-    in_two = norm_back(normed_two_grad, gain_two)
-
     attended = attended.reshape(trios, groups, rows, OPACK).transpose(1, 2, 0, 3)
     attended = attended.reshape(all_rows, trios * OPACK)
-    branch_one = mm(attended, dense_pad.reshape(trios * OPACK, d)) + dense_shift
-    output = (x + branch_one + second_branch).astype(BF)
-
-    vec_grads = jnp.concatenate(
-        [
-            jnp.sum(normed_two_grad * xhat, 0)[None],
-            jnp.sum(normed_two_grad, 0)[None],
-            cot_sum[None],
-            jnp.zeros((5, d), F32),
-        ],
-        0,
-    ).T
-    up_shift_grad = join_hidden(up_shift_grad[None], count, r).reshape(d, blocks)
-    vec_grads = jnp.concatenate(
-        [vec_grads, up_shift_grad, jnp.zeros((d, TILE - 8 - blocks), F32)], 1
-    )
+    dense_cols = d // part
+    cols = lax.dynamic_slice_in_dim(cot_all, c * dense_cols, dense_cols, 1)
+    cols = jnp.pad(cols, ((0, 0), (0, -dense_cols % TILE)))
     mlp_grads = gradients(
-        normed_two, pre_grad, hidden_low, cot, attended, vec_grads.astype(BF), trios
-    )
-    mlp_grads, kv = lax.optimization_barrier((mlp_grads, kv))
-    mlp_sum = lax.psum_scatter(mlp_grads, ALL_AXES, scatter_dimension=0, tiled=True).astype(F32)
+        normed_all, pre_grad, hidden_low, cot_all, all_parts(attended), cols, trios
+    )
+    mlp_grads, dout = lax.optimization_barrier((mlp_grads, dout))
+    mlp_sum = lax.psum_scatter(mlp_grads, ("seq", "unit"), scatter_dimension=0, tiled=True)
 
     own, others = attend_backward(meta, packed, dout, out_t, lse, kv, seg_mine)
     others = [shift(others[i - 1], "part", part - i) for i in range(1, part)]
     qkv_grad = unturn(own, others, cos, sin)
     back = exchange(qkv_grad)
 
-    grad_rows = qkv_grad.reshape(units * rows, PACK)
-    trio_weight = trio_full[:, :PACK].astype(F32)
-    trio_grad = outer_sum(normed_one.reshape(units * rows, d), grad_rows)
-    hat_grad = outer_sum(hat_one.reshape(units * rows, d), grad_rows)
-    shift_grad = jnp.sum(grad_rows.astype(F32), 0)[None]
-    late_vec = jnp.concatenate(
+    attended, second_branch, normed_two_grad, qkv_grad = lax.optimization_barrier(
+        (attended, second_branch, normed_two_grad, qkv_grad)
+    )
+    branch_one = mm(attended, dense_pad.reshape(trios * OPACK, d)) + dense_shift
+    output = (x + branch_one + second_branch + down_shift).astype(BF)
+    in_two = norm_back(normed_two_grad, gain_two)
+    vec_grads = jnp.concatenate(
         [
-            jnp.sum(trio_weight * hat_grad, 1, keepdims=True),
-            jnp.sum(trio_weight * shift_grad, 1, keepdims=True),
-            jnp.zeros((d, TILE - 2), F32),
-        ],
-        1,
-    )
-    late = jnp.concatenate([trio_grad.astype(BF), late_vec.astype(BF)], 1)
+            jnp.zeros((2, d), F32),
+            jnp.sum(normed_two_grad * xhat, 0)[None],
+            jnp.sum(normed_two_grad, 0)[None],
+            jnp.sum(cot_float, 0)[None],
+            jnp.zeros((3, d), F32),
+        ],
+        0,
+    ).T
+    up_shift_grad = join_hidden(up_shift_grad, count, r).reshape(d, blocks)
+
+    vec_grads = jnp.concatenate(
+        [vec_grads, up_shift_grad, jnp.zeros((d, TILE - 8 - blocks), F32)], 1
+    )
+    late, shift_grad = trio_gradient(normed_one, hat_one, qkv_grad, trio_full, vec_grads)
     late = late.reshape(seqs, units, part, r, PACK + TILE)
     shift_rows = jnp.pad(shift_grad.astype(BF), ((0, 7), (0, TILE)))
     late = jnp.concatenate(
         [late, jnp.broadcast_to(shift_rows, (seqs, units, part) + shift_rows.shape)], 3
     )
     late = scatter_small(late.transpose(2, 0, 1, 3, 4), "part")
-    late = exchange_small(scatter_small(late, "seq")).astype(F32)
+    late = scatter_small(late, "seq")
+    late, back, mlp_sum = lax.optimization_barrier((late, back, mlp_sum))
+    late = exchange(late).astype(F32)
     late = jnp.sum(late.reshape(trios, groups, r + 8, PACK + TILE), 1)
     qkv_weight_grad = unpack_columns(
         late[:, :r, :PACK].transpose(1, 0, 2).reshape(r, trios * PACK), trios
     )
-    late_vec = jnp.sum(late[:, :r, PACK : PACK + 2], 0)
+    late_vec = jnp.sum(late[:, :r, PACK:], 0)
     qkv_shift_grad = unpack_columns(late[:, r, :PACK].reshape(1, trios * PACK), trios)[0]
     qkv_shift_grad = lax.dynamic_slice_in_dim(qkv_shift_grad, place * 3 * r, 3 * r)
 
+    mlp_sum = swap_parts(mlp_sum.reshape(part, r, -1)).astype(F32)
+    up_sum = jnp.concatenate([mlp_sum[p, :, : half * d] for p in range(part)], 1)
     down_sum = jnp.concatenate(
-        [mlp_sum[:, ff + b * d : ff + (b + 1) * d] for b in range(blocks)], 0
-    )
-    vec_sum = mlp_sum[:, 2 * ff + d :]
-    cot_total = vec_sum[:, 2]
+        [
+            mlp_sum[p, :, (half + b) * d : (half + b + 1) * d]
+            for p in range(part)
+            for b in range(half)
+        ],
+        0,
+    )
+    dense_sum = jnp.concatenate(
+        [mlp_sum[p, :, 2 * half * d : 2 * half * d + dense_cols] for p in range(part)], 1
+    )
     param_grads = (
         late_vec[:, 0],
         late_vec[:, 1],
-        vec_sum[:, 0],
-        vec_sum[:, 1],
+        late_vec[:, 2],
+        late_vec[:, 3],
         qkv_weight_grad,
         qkv_shift_grad,
-        mlp_sum[:, 2 * ff : 2 * ff + d],
-        cot_total,
-        join_hidden(mlp_sum[:, :ff], count, r),
-        vec_sum[:, 8 : 8 + blocks].reshape(-1),
+        dense_sum,
+        late_vec[:, 4],
+        join_hidden(up_sum, count, r),
+        late_vec[:, 8 : 8 + blocks].reshape(-1),
         down_sum,
-        cot_total,
-    )
-    param_grads, back = lax.optimization_barrier((param_grads, back))
+        late_vec[:, 4],
+    )
 
     back = back.reshape(trios, groups, rows, PACK).transpose(1, 2, 0, 3)
     normed_one_grad = inner_back(back.reshape(all_rows, trios * PACK), qkv_full)

time: 566 us -> 522 us (0.922)
  Pallas kernels: 118 us -> 162 us
  matrix products: 49.2 us -> 8.84 us
  starting transfers between devices: 69 us -> 32.1 us
  blocking collectives: 30 us -> 0 us
  other arithmetic: 27.7 us -> 43.8 us
  waiting for transfers between devices: 179 us -> 185 us
    ppermute x20 -> x13, waiting for transfers between devices: 161 us -> 27.4 us  [shift(): return lax.ppermute(value, axis, [(p, (p + i) % n) for p in range(n)])]
    all_to_all x3 -> x5, waiting for transfers between devices: 18.5 us -> 96.7 us  [exchange(): lax.all_to_all(blocks_out.reshape(-1, width), 'unit', 0, 0, tiled=True)]
    all_gather x2, waiting for transfers between devices: 0.04 us -> 34.3 us  [the longest x1 34.3 us: on_device(): second = lax.all_gather(second_pack, ('seq', 'unit'), axis=0, tiled=True)]
    pallas_call x1 -> x3, Pallas kernels: 15.2 us -> 48.3 us  [the longest x1 22.4 us: feed_forward(): pl.pallas_call(feed_kernel, grid=(2 * blocks,), in_specs=[wide, wide, pl....]
    all_to_all x1 -> x0, blocking collectives: 30 us -> none  [exchange(): lax.all_to_all(blocks_out.reshape(-1, width), 'unit', 0, 0, tiled=True)]
    ppermute x20 -> x13, starting transfers between devices: 36.8 us -> 7.31 us  [shift(): return lax.ppermute(value, axis, [(p, (p + i) % n) for p in range(n)])]
    reduce_scatter x0 -> x1, waiting for transfers between devices: none -> 26.2 us  [on_device(): lax.psum_scatter(mlp_grads, ('seq', 'unit'), scatter_dimension=0, tiled=T...]
    dot_general x3 -> x1, matrix products: 25.4 us -> 4.72 us  [inner_back(): lax.dot_general(grad_rows, weight, (((1,), (1,)), ((), ())), preferred_el...]
  transfers between devices with their start and end apart: 26 -> 21, of which waited for: 11 -> 11; matrix products, arithmetic and copies ran while one was open for 20% -> 17% of each run, Pallas kernels for 19% -> 28%
where the time goes in v4:
time: 522 us; the launch traced here: 512 us
  waiting for transfers between devices  185 us (35%)
  Pallas kernels  162 us (31%)
  local copies, waits for them, and re-layouts  65.8 us (13%)
  other arithmetic  43.8 us (8%)
  starting transfers between devices  32.1 us (6%)
  between operations  14.8 us (3%)
  matrix products  8.84 us (2%)
    all_to_all x5, waiting for transfers between devices, exchange(): lax.all_to_all(blocks_out.reshape(-1, width), 'unit', 0, 0, tiled=True)  96.7 us
    pallas_call x1, Pallas kernels, attend_backward(): pl.pallas_call(functools.partial(backward_kernel, part, units), grid_spec...  53.5 us
    pallas_call x1, Pallas kernels, attend_forward(): pl.pallas_call(functools.partial(forward_kernel, part, units), grid_spec=...  40.8 us
    all_gather x1, waiting for transfers between devices, on_device(): second = lax.all_gather(second_pack, ('seq', 'unit'), axis=0, tiled=True)  34.3 us
    ppermute x13, waiting for transfers between devices, shift(): return lax.ppermute(value, axis, [(p, (p + i) % n) for p in range(n)])  27.4 us
    reduce_scatter x1, waiting for transfers between devices, on_device(): lax.psum_scatter(mlp_grads, ('seq', 'unit'), scatter_dimension=0, tiled=T...  26.2 us
    all_to_all x5, starting transfers between devices, exchange(): lax.all_to_all(blocks_out.reshape(-1, width), 'unit', 0, 0, tiled=True)  24.7 us
    pallas_call x1, Pallas kernels, feed_forward(): pl.pallas_call(feed_kernel, grid=(2 * blocks,), in_specs=[wide, wide, pl....  22.4 us
  transfers between devices with their start and end apart: 21, of which 11 were waited for; matrix products, arithmetic and copies ran while one was open for 17% of the time, Pallas kernels for 28%

profile of v4, /device:TPU:0, one launch (start us, length us, event | category | flops | bytes accessed | tf_op | source)
XLA Modules:
  0.0 512.4 jit_solution(1632780989566712230)
XLA Ops:
  14.9 1.8 pack_early.1
  16.7 1.6 pad_maximum_fusion.5
  18.4 1.2 copy.149
  19.6 2.1 pad_maximum_fusion
  21.7 7.3 %all-to-all-start = ((bf16[8,280,768]{2,1,0:T(8,128)(2,1)}), bf16[8,280,768]{2,1,0:T(8,128)(2,1)S(1)}, u32[]{:S(2)}, u32[]{:S(2)}) async-start(bf16[8,280,768]{2,1,0:T(8,128)(2,1)} %pad_maximum_fusion), calls=%async_computation | async-start | bytes 6881280 | tf_op jit(solution)/shard_map/all_to_all | solution.py:747
  29.0 3.0 reshape.348
  32.0 2.2 copy.104
  34.2 2.8 reshape.349
  39.6 1.7 collective-permute-done.2
  41.3 1.9 maximum_select_fusion.4
  43.2 73.1 %all-to-all-done.tok_ref = bf16[8,280,768]{2,1,0:T(8,128)(2,1)S(1)} async-done(((bf16[8,280,768]{2,1,0:T(8,128)(2,1)}), bf16[8,280,768]{2,1,0:T(8,128)(2,1)S(1)}, u32[]{:S(2)}, u32[]{:S(2)}) %all-to-all-start) | async-done | bytes 3440672 | tf_op jit(solution)/shard_map/all_to_all | solution.py:747
  117.4 1.5 collective-permute-start
  118.9 11.8 %collective-permute-done = bf16[8,24,768]{2,1,0:T(8,128)(2,1)} collective-permute-done((bf16[8,24,768]{2,1,0:T(8,128)(2,1)}, bf16[8,24,768]{2,1,0:T(8,128)(2,1)}, u32[]{:S(2)}, u32[]{:S(2)}) %collective-permute-start) | collective-permute-done | bytes 294944 | tf_op jit(solution)/shard_map/ppermute | solution.py:753
  130.7 2.1 maximum_select_fusion.2
  135.3 1.4 maximum_select_fusion.1
  136.8 1.4 fusion.38
  139.1 1.7 fusion.65
  143.0 10.5 %project.1 = (bf16[8,256,640]{2,1,0:T(8,128)(2,1)}, bf16[8,256,512]{2,1,0:T(8,128)(2,1)}, bf16[8,256,768]{2,1,0:T(8,128)(2,1)}, bf16[8,256,768]{2,1,0:T(8,128)(2,1)}) custom-call(bf16[8,280,768]{2,1,0:T(8,128)(2,1)} %copy-done.7, bf16[768,768]{1,0:T(8,128)(2,1)} %bitcast.221, f32[1,640]{1,0:T(1,128)} %fusion.53.b_ref, f32[1,768]{1,0:T(1,128)} %copy.105.gain_ref, ...), custom_call_target="tpu_custom_call" | custom-call | flops 2013265920 | bytes 12058624 | tf_op jit(solution)/shard_map/project/pallas_call | solution.py:98
  155.6 1.4 slice.263
  157.9 2.0 fusion.35
  159.9 2.3 copy.103
  162.2 3.6 all-to-all-start.1
  166.8 40.8 %attend_forward.1 = (bf16[8,256,256]{2,1,0:T(8,128)(2,1)}, f32[8,192,256]{2,1,0:T(8,128)}, f32[8,8,256]{2,1,0:T(8,128)}) custom-call(s32[17]{0:T(128)} %pad_add_fusion.meta, bf16[8,256,640]{2,1,0:T(8,128)(2,1)} %get-tuple-element.57.q_ref, bf16[8,256,512]{2,1,0:T(8,128)(2,1)} %get-tuple-element.58.refs_0_, ...), custom_call_target="tpu_custom_call" | custom-call | flops 12884901888 | bytes 20000000 | tf_op jit(solution)/shard_map/attend_forward/pallas_call | solution.py:394
  208.6 5.0 all-to-all-start.2
  213.7 1.2 fusion.15
  214.9 1.4 collective-permute-start.4
  216.3 2.4 pad_maximum_fusion.2.cot_ref
  219.7 2.1 constant_dynamic-update-slice_fusion.1
  221.9 2.1 constant_dynamic-update-slice_fusion.x_ref.norm_ref
  223.9 34.3 %all-gather.5.cloned.1.call-done.up_ref.down_ref = bf16[768,3072]{1,0:T(8,128)(2,1)} async-done(((bf16[48,3072]{1,0:T(8,128)(2,1)}), bf16[768,3072]{1,0:T(8,128)(2,1)}) %all-gather.5.cloned.1.call-update) | async-done | bytes 4718608 | tf_op jit(solution)/shard_map/all_gather | solution.py:851
  258.2 22.4 %feed_forward.1 = (bf16[1024,1536]{1,0:T(8,128)(2,1)}, bf16[1024,1536]{1,0:T(8,128)(2,1)}, f32[1,1536]{1,0:T(1,128)}, f32[1024,768]{1,0:T(8,128)}, f32[1024,768]{1,0:T(8,128)}) custom-call(bf16[1024,768]{1,0:T(8,128)(2,1)} %constant_dynamic-update-slice_fusion.x_ref.norm_ref, bf16[1024,768]{1,0:T(8,128)(2,1)} %pad_maximum_fusion.2.cot_ref, ...), custom_call_target="tpu_custom_call" | custom-call | flops 9663676416 | bytes 4718592 | tf_op jit(solution)/shard_map/feed_forward/pallas_call | solution.py:538
  281.8 2.2 fusion.43.cols_ref
  284.5 2.7 pad_maximum_fusion.1.att_ref
  287.3 15.0 %gradients.1 = bf16[768,3456]{1,0:T(8,128)(2,1)} custom-call(bf16[1024,768]{1,0:T(8,128)(2,1)} %constant_dynamic-update-slice_fusion.x_ref.norm_ref, bf16[1024,1536]{1,0:T(8,128)(2,1)} %get-tuple-element.69.pre_ref, bf16[1024,1536]{1,0:T(8,128)(2,1)} %get-tuple-element.70.hidden_ref, bf16[1024,768]{1,0:T(8,128)(2,1)} %pad_maximum_fusion.2.cot_ref, ...), custom_call_target="tpu_custom_call" | custom-call | flops 5435817984 | tf_op jit(solution)/shard_map/gradients/pallas_call | solution.py:595
  302.3 53.5 %attend_backward.1 = (bf16[8,256,640]{2,1,0:T(8,128)(2,1)}, bf16[1,8,256,512]{3,2,1,0:T(8,128)(2,1)}) custom-call(s32[17]{0:T(128)} %pad_add_fusion.meta, bf16[8,256,640]{2,1,0:T(8,128)(2,1)} %get-tuple-element.57.q_ref, bf16[8,256,256]{2,1,0:T(8,128)(2,1)} %copy-done.13, f32[8,192,256]{2,1,0:T(8,128)} %get-tuple-element.73.ot_ref, ...), custom_call_target="tpu_custom_call" | custom-call | flops 32212254720 | bytes 20000000 | tf_op jit(solution)/shard_map/attend_backward/pallas_call | solution.py:434
  355.8 1.3 collective-permute-start.9
  357.2 5.1 collective-permute-done.9.refs_1_
  362.3 7.7 %unturn.1.grad_ref = bf16[8,256,640]{2,1,0:T(8,128)(2,1)} custom-call(bf16[8,256,640]{2,1,0:T(8,128)(2,1)} %get-tuple-element.75.refs_0_, bf16[8,256,512]{2,1,0:T(8,128)(2,1)} %collective-permute-done.9.refs_1_, f32[8,8,256]{2,1,0:T(8,128)} %get-tuple-element.156.cos_ref.refs_2_, f32[8,8,256]{2,1,0:T(8,128)} %get-tuple-element.155.sin_ref.refs_3_), custom_call_target="tpu_custom_call" | custom-call | tf_op jit(solution)/shard_map/unturn/pallas_call | solution.py:151
  370.0 4.4 all-to-all-start.3
  374.4 2.7 slice.225
  382.4 3.4 slice_add_fusion.1
  385.9 1.6 slice_add_fusion
  387.5 1.4 fusion.23
  390.6 1.4 concatenate.114
  392.0 1.6 copy.111
  393.6 1.9 maximum_maximum_fusion.vec_ref
  395.6 10.9 %trio_gradient.1 = (bf16[768,768]{1,0:T(8,128)(2,1)}, f32[1,640]{1,0:T(1,128)}) custom-call(bf16[8,256,768]{2,1,0:T(8,128)(2,1)} %get-tuple-element.79.norm_ref, bf16[8,256,768]{2,1,0:T(8,128)(2,1)} %get-tuple-element.80.hat_ref, bf16[8,256,640]{2,1,0:T(8,128)(2,1)} %unturn.1.grad_ref, bf16[768,768]{1,0:T(8,128)(2,1)} %bitcast.222, ...), custom_call_target="tpu_custom_call" | custom-call | tf_op jit(solution)/shard_map/trio_gradient/pallas_call | solution.py:650
  407.2 2.0 fusion.40
  409.5 1.5 pad.18
  411.9 1.4 fusion.2
  413.3 1.7 collective-permute-start.11
  415.1 2.1 fusion.72
  417.2 7.4 %collective-permute-done.11 = bf16[8,32,768]{2,1,0:T(8,128)(2,1)S(1)} collective-permute-done((bf16[8,32,768]{2,1,0:T(8,128)(2,1)S(1)}, bf16[8,32,768]{2,1,0:T(8,128)(2,1)S(1)}, u32[]{:S(2)}, u32[]{:S(2)}) %collective-permute-start.11) | collective-permute-done | bytes 393248 | tf_op jit(solution)/shard_map/ppermute | solution.py:753
  425.4 17.9 %all-to-all-done.3 = bf16[8,256,640]{2,1,0:T(8,128)(2,1)} async-done(((bf16[8,256,640]{2,1,0:T(8,128)(2,1)}), bf16[8,256,640]{2,1,0:T(8,128)(2,1)}, u32[]{:S(2)}, u32[]{:S(2)}) %all-to-all-start.3) | async-done | bytes 2621472 | tf_op jit(solution)/shard_map/all_to_all | solution.py:747
  443.3 26.2 %reduce-scatter.2.cloned.1.call-done = bf16[48,3456]{1,0:T(8,128)(2,1)} async-done(((bf16[768,3456]{1,0:T(8,128)(2,1)}), bf16[48,3456]{1,0:T(8,128)(2,1)}) %reduce-scatter.2.cloned.1.call-update) | async-done | bytes 331792 | tf_op jit(solution)/shard_map/reduce_scatter | solution.py:916
  469.6 3.8 copy.113
  474.1 4.7 fusion.63
  479.5 1.6 fusion.22
  481.1 1.7 copy.148
  482.8 1.7 copy.147
  484.5 4.4 all-to-all-start.4
  490.3 1.2 copy.118
  491.6 2.6 reshape.372
  495.5 5.7 %all-to-all-done.4 = bf16[8,32,768]{2,1,0:T(8,128)(2,1)S(1)} async-done(((bf16[8,32,768]{2,1,0:T(8,128)(2,1)}), bf16[8,32,768]{2,1,0:T(8,128)(2,1)S(1)}, u32[]{:S(2)}, u32[]{:S(2)}) %all-to-all-start.4) | async-done | bytes 393248 | tf_op jit(solution)/shard_map/all_to_all | solution.py:747
  (211 shorter events, 43.2 us)
Async XLA Ops:
  7.2 148.4 %all-gather.3.cloned.1.call-start = ((), (), s32[]{:S(2)}) async-start(), calls=%async_computation.6 | async-start | bytes 5271552 | tf_op jit(solution)/shard_map/all_gather | solution.py:836
  16.7 2.9 copy-start.15
  21.7 94.6 %all-to-all-start = ((bf16[8,280,768]{2,1,0:T(8,128)(2,1)}), bf16[8,280,768]{2,1,0:T(8,128)(2,1)S(1)}, u32[]{:S(2)}, u32[]{:S(2)}) async-start(bf16[8,280,768]{2,1,0:T(8,128)(2,1)} %pad_maximum_fusion), calls=%async_computation | async-start | bytes 6881280 | tf_op jit(solution)/shard_map/all_to_all | solution.py:747
  28.9 229.3 %all-gather.5.cloned.1.call-start = ((), (), s32[]{:S(2)}) async-start(), calls=%async_computation.7 | async-start | bytes 5013504 | tf_op jit(solution)/shard_map/all_gather | solution.py:851
  39.6 1.7 collective-permute-start.2
  116.3 20.5 %copy-start.7 = (bf16[8,280,768]{2,1,0:T(8,128)(2,1)}, bf16[8,280,768]{2,1,0:T(8,128)(2,1)S(1)}, u32[]{:S(2)}) copy-start(bf16[8,280,768]{2,1,0:T(8,128)(2,1)S(1)} %all-to-all-done.tok_ref) | copy-start | bytes 10321924
  117.4 13.3 %collective-permute-start = (bf16[8,24,768]{2,1,0:T(8,128)(2,1)}, bf16[8,24,768]{2,1,0:T(8,128)(2,1)}, u32[]{:S(2)}, u32[]{:S(2)}) collective-permute-start(bf16[8,24,768]{2,1,0:T(8,128)(2,1)} %get-tuple-element.115), channel_id=1, source_target_pairs={{0,16},{16,0},{1,17},{17,1},{2,18},{18,2},{3,19},{19,3},{4,20},{20... | collective-permute-start | bytes 884744 | tf_op jit(solution)/shard_map/ppermute | solution.py:753
  132.8 4.0 collective-permute-start.1
  138.3 2.5 copy-start.2
  143.0 11.1 %copy-start.8 = (bf16[256,2,768]{2,1,0:T(2,128)(2,1)S(1)}, bf16[256,2,768]{2,1,0:T(2,128)(2,1)}, u32[]{:S(2)}) copy-start(bf16[256,2,768]{2,1,0:T(2,128)(2,1)} %param.29) | copy-start | bytes 2359300
  153.5 1.2 copy-start
  153.5 13.4 %collective-permute-start.3 = (bf16[8,256,512]{2,1,0:T(8,128)(2,1)}, bf16[8,256,512]{2,1,0:T(8,128)(2,1)}, u32[]{:S(2)}, u32[]{:S(2)}) collective-permute-start(bf16[8,256,512]{2,1,0:T(8,128)(2,1)} %get-tuple-element.58.refs_0_), channel_id=1, source_target_pairs={{0,1},{1,0},{2,3},{3,2},{4,5},{5,4},{6,7},{7,6},{8,9},{9,8},{10,11... | collective-permute-start | bytes 6291464 | tf_op jit(solution)/shard_map/ppermute | solution.py:753
  154.2 62.1 %collective-permute-start.5 = (bf16[512,768]{1,0:T(8,128)(2,1)S(1)}, bf16[512,768]{1,0:T(8,128)(2,1)}, u32[]{:S(2)}, u32[]{:S(2)}) collective-permute-start(bf16[512,768]{1,0:T(8,128)(2,1)S(1)} %bitcast.216), channel_id=1, source_target_pairs={{0,1},{1,0},{2,3},{3,2},{4,5},{5,4},{6,7},{7,6},{8,9},{9,8},{10,11... | collective-permute-start | bytes 2359304 | tf_op jit(solution)/shard_map/ppermute | solution.py:753
  156.9 1.0 copy-start.4
  162.2 45.4 %all-to-all-start.1 = ((bf16[8,256,256]{2,1,0:T(8,128)(2,1)}), bf16[8,256,256]{2,1,0:T(8,128)(2,1)S(1)}, u32[]{:S(2)}, u32[]{:S(2)}) async-start(bf16[8,256,256]{2,1,0:T(8,128)(2,1)} %bitcast.24), calls=%async_computation.1 | async-start | bytes 2097152 | tf_op jit(solution)/shard_map/all_to_all | solution.py:747
  166.2 221.3 %copy-start.16 = (f32[1,2,2,128]{3,1,2,0:T(2,128)}, f32[1,2,2,128]{3,1,2,0:T(2,128)S(1)}, u32[]{:S(2)}) copy-start(f32[1,2,2,128]{3,1,2,0:T(2,128)S(1)} %copy.121) | copy-start | bytes 6148
  166.2 221.3 %copy-start.18 = (f32[1,2,2,128]{3,1,2,0:T(2,128)}, f32[1,2,2,128]{3,1,2,0:T(2,128)S(1)}, u32[]{:S(2)}) copy-start(f32[1,2,2,128]{3,1,2,0:T(2,128)S(1)} %copy.120) | copy-start | bytes 6148
  207.6 1.0 copy-start.13
  208.6 72.0 %all-to-all-start.2 = ((bf16[8,256,256]{2,1,0:T(8,128)(2,1)}), bf16[8,256,256]{2,1,0:T(8,128)(2,1)S(1)}, u32[]{:S(2)}, u32[]{:S(2)}) async-start(bf16[8,256,256]{2,1,0:T(8,128)(2,1)} %get-tuple-element.65), calls=%async_computation.2 | async-start | bytes 2097152 | tf_op jit(solution)/shard_map/all_to_all | solution.py:747
  213.7 255.9 %reduce-scatter.2.cloned.1.call-start = ((), (), s32[]{:S(2)}) async-start(), calls=%async_computation.8 | async-start | bytes 5640192 | tf_op jit(solution)/shard_map/reduce_scatter | solution.py:916
  214.9 6.9 %collective-permute-start.4 = (bf16[512,768]{1,0:T(8,128)(2,1)}, bf16[512,768]{1,0:T(8,128)(2,1)}, u32[]{:S(2)}, u32[]{:S(2)}) collective-permute-start(bf16[512,768]{1,0:T(8,128)(2,1)} %fusion.15), channel_id=1, source_target_pairs={{0,1},{1,0},{2,3},{3,2},{4,5},{5,4},{6,7},{7,6},{8,9},{9,8},{10,11... | collective-permute-start | bytes 2359304 | tf_op jit(solution)/shard_map/ppermute | solution.py:753
  281.7 5.6 %copy-start.5 = (bf16[64,8,4,256]{3,1,2,0:T(8,128)(2,1)}, bf16[64,8,4,256]{3,1,2,0:T(8,128)(2,1)S(1)}, u32[]{:S(2)}) copy-start(bf16[64,8,4,256]{3,1,2,0:T(8,128)(2,1)S(1)} %copy.122) | copy-start | bytes 3145732
  281.7 2.9 collective-permute-start.8
  302.3 54.8 %copy-start.11 = (f32[1024,768]{1,0:T(8,128)S(1)}, f32[1024,768]{1,0:T(8,128)}, u32[]{:S(2)}) copy-start(f32[1024,768]{1,0:T(8,128)} %get-tuple-element.67) | copy-start | bytes 9437188
  355.8 6.6 %collective-permute-start.9 = (bf16[8,256,512]{2,1,0:T(8,128)(2,1)}, bf16[8,256,512]{2,1,0:T(8,128)(2,1)}, u32[]{:S(2)}, u32[]{:S(2)}) collective-permute-start(bf16[8,256,512]{2,1,0:T(8,128)(2,1)} %bitcast.262), channel_id=1, source_target_pairs={{0,1},{1,0},{2,3},{3,2},{4,5},{5,4},{6,7},{7,6},{8,9},{9,8},{10,11... | collective-permute-start | bytes 6291464 | tf_op jit(solution)/shard_map/ppermute | solution.py:753
  357.2 25.2 %collective-permute-start.6 = (f32[512,768]{1,0:T(8,128)S(1)}, f32[512,768]{1,0:T(8,128)}, u32[]{:S(2)}, u32[]{:S(2)}) collective-permute-start(f32[512,768]{1,0:T(8,128)S(1)} %slice.223), channel_id=1, source_target_pairs={{0,1},{1,0},{2,3},{3,2},{4,5},{5,4},{6,7},{7,6},{8,9},{9,8},{10,11... | collective-permute-start | bytes 4718600 | tf_op jit(solution)/shard_map/ppermute | solution.py:753
  370.0 73.3 %all-to-all-start.3 = ((bf16[8,256,640]{2,1,0:T(8,128)(2,1)}), bf16[8,256,640]{2,1,0:T(8,128)(2,1)}, u32[]{:S(2)}, u32[]{:S(2)}) async-start(bf16[8,256,640]{2,1,0:T(8,128)(2,1)} %unturn.1.grad_ref), calls=%async_computation.3 | async-start | bytes 5242880 | tf_op jit(solution)/shard_map/all_to_all | solution.py:747
  374.4 3.1 copy-start.9
  374.4 5.0 copy-start.24
  377.2 8.7 %collective-permute-start.7 = (f32[512,768]{1,0:T(8,128)}, f32[512,768]{1,0:T(8,128)}, u32[]{:S(2)}, u32[]{:S(2)}) collective-permute-start(f32[512,768]{1,0:T(8,128)} %slice.225), channel_id=1, source_target_pairs={{0,1},{1,0},{2,3},{3,2},{4,5},{5,4},{6,7},{7,6},{8,9},{9,8},{10,11... | collective-permute-start | bytes 4718600 | tf_op jit(solution)/shard_map/ppermute | solution.py:753
  382.4 3.5 copy-start.10
  409.3 1.7 copy-start.23
  409.3 2.6 collective-permute-start.10
  409.5 2.4 copy-start.3
  411.0 4.1 copy-start.22
  411.0 4.1 copy-start.6
  413.3 11.3 %collective-permute-start.11 = (bf16[8,32,768]{2,1,0:T(8,128)(2,1)S(1)}, bf16[8,32,768]{2,1,0:T(8,128)(2,1)S(1)}, u32[]{:S(2)}, u32[]{:S(2)}) collective-permute-start(bf16[8,32,768]{2,1,0:T(8,128)(2,1)S(1)} %dynamic-slice_bitcast_fusion), channel_id=1, source_target_pairs={{0,16},{16,0},{1,17},{17,1},{2,18},{18,2},{3,19},{19,3},{4,20},{20... | collective-permute-start | bytes 1179656 | tf_op jit(solution)/shard_map/ppermute | solution.py:753
  473.3 0.7 copy-start.17
  473.3 0.7 copy-start.19
  473.4 0.7 copy-start.25
  474.0 4.8 copy-start.14
  474.0 5.5 %copy-start.1 = (f32[512,768]{1,0:T(8,128)S(1)}, f32[512,768]{1,0:T(8,128)}, u32[]{:S(2)}) copy-start(f32[512,768]{1,0:T(8,128)} %slice_add_fusion.1) | copy-start | bytes 4718596
  474.0 5.5 %copy-start.12 = (f32[512,768]{1,0:T(8,128)S(1)}, f32[512,768]{1,0:T(8,128)}, u32[]{:S(2)}) copy-start(f32[512,768]{1,0:T(8,128)} %fusion.72) | copy-start | bytes 4718596
  474.0 5.5 %copy-start.20 = (f32[768]{0:T(1024)S(1)}, f32[768]{0:T(1024)}, u32[]{:S(2)}) copy-start(f32[768]{0:T(1024)} %get-tuple-element.130) | copy-start | bytes 9220
  474.0 5.5 %copy-start.21 = (f32[768]{0:T(1024)S(1)}, f32[768]{0:T(1024)}, u32[]{:S(2)}) copy-start(f32[768]{0:T(1024)} %get-tuple-element.131) | copy-start | bytes 9220
  479.5 9.4 %collective-permute-start.12 = (bf16[24,3456]{1,0:T(8,128)(2,1)}, bf16[24,3456]{1,0:T(8,128)(2,1)S(1)}, u32[]{:S(2)}, u32[]{:S(2)}) collective-permute-start(bf16[24,3456]{1,0:T(8,128)(2,1)} %get-tuple-element.134), channel_id=1, source_target_pairs={{0,1},{1,0},{2,3},{3,2},{4,5},{5,4},{6,7},{7,6},{8,9},{9,8},{10,11... | collective-permute-start | bytes 497672 | tf_op jit(solution)/shard_map/ppermute | solution.py:753
  484.5 16.7 %all-to-all-start.4 = ((bf16[8,32,768]{2,1,0:T(8,128)(2,1)}), bf16[8,32,768]{2,1,0:T(8,128)(2,1)S(1)}, u32[]{:S(2)}, u32[]{:S(2)}) async-start(bf16[8,32,768]{2,1,0:T(8,128)(2,1)} %fusion.44), calls=%async_computation.5 | async-start | bytes 786432 | tf_op jit(solution)/shard_map/all_to_all | solution.py:747
  502.3 3.3 copy-start.26
Sparse Core Ops, SparseCore 0:
  18.5 123.3 all-gather.2
  145.2 113.0 all-gather.4
  302.4 167.0 reduce-scatter.1

commit v5 on v4

--- a/solution.py
+++ b/solution.py
@@ -67,10 +67,30 @@
     return jnp.concatenate(cos_head * 2, 0).T, jnp.concatenate(sin_head * 2, 0).T
 
 
+def first_place(rel):
+    return rel % 2 * 4 + rel // 2 % 2 * 2 + rel // 4
+
+
+def second_place(rel):
+    return rel // 2 % 2 * 4 + rel % 2 * 2 + rel // 4
+
+
 def project_kernel(
-    tok_ref, w_ref, b_ref, gain_ref, bias_ref, cos_ref, sin_ref, out_ref, kv_ref, norm_ref, hat_ref
+    place_ref,
+    one_ref,
+    two_ref,
+    w_ref,
+    b_ref,
+    gain_ref,
+    bias_ref,
+    cos_ref,
+    sin_ref,
+    out_ref,
+    kv_ref,
+    norm_ref,
+    hat_ref,
 ):
-    x = tok_ref[0].astype(F32)
+    x = jnp.concatenate([one_ref[0], two_ref[0]], 0).astype(F32)
     centre = x - jnp.mean(x, -1, keepdims=True)
     spread = jnp.mean(centre * centre, -1, keepdims=True)
     hat = centre * lax.rsqrt(spread + EPSILON)
@@ -89,30 +109,40 @@
             kv_ref[0, :, (t - 1) * TILE : t * TILE] = tile
 
 
-def project(toks, weight, bias, gain, offset, cos, sin):
-    units, unused, d = toks.shape
-    rows = cos.shape[2]
-    tok_spec = pl.BlockSpec((1, rows, d), lambda j: (j, 0, 0))
-    row_spec = pl.BlockSpec((1, d), lambda j: (0, 0))
-    turn_spec = pl.BlockSpec((1, ROT // 2, rows), lambda j: (j, 0, 0))
+def half_specs(rows, d):
+    return [
+        pl.BlockSpec((1, rows // 2, d), lambda j, place: (first_place(j ^ place[0]), 0, 0)),
+        pl.BlockSpec((1, rows // 2, d), lambda j, place: (second_place(j ^ place[0]), 0, 0)),
+    ]
+
+
+def project(place, toks, weight, bias, gain, offset, cos, sin):
+    units, unused, rows = cos.shape
+    d = toks[0].shape[2]
+    tok_spec = pl.BlockSpec((1, rows, d), lambda j, place: (j, 0, 0))
+    row_spec = pl.BlockSpec((1, d), lambda j, place: (0, 0))
+    turn_spec = pl.BlockSpec((1, ROT // 2, rows), lambda j, place: (j, 0, 0))
     return pl.pallas_call(
         project_kernel,
-        grid=(units,),
-        in_specs=[
-            tok_spec,
-            pl.BlockSpec((d, PACK), lambda j: (0, 0)),
-            pl.BlockSpec((1, PACK), lambda j: (0, 0)),
-            row_spec,
-            row_spec,
-            turn_spec,
-            turn_spec,
-        ],
-        out_specs=[
-            pl.BlockSpec((1, rows, PACK), lambda j: (j, 0, 0)),
-            pl.BlockSpec((1, rows, PACK - TILE), lambda j: (j, 0, 0)),
-            tok_spec,
-            tok_spec,
-        ],
+        grid_spec=pltpu.PrefetchScalarGridSpec(
+            num_scalar_prefetch=1,
+            grid=(units,),
+            in_specs=half_specs(rows, d)
+            + [
+                pl.BlockSpec((d, PACK), lambda j, place: (0, 0)),
+                pl.BlockSpec((1, PACK), lambda j, place: (0, 0)),
+                row_spec,
+                row_spec,
+                turn_spec,
+                turn_spec,
+            ],
+            out_specs=[
+                pl.BlockSpec((1, rows, PACK), lambda j, place: (j, 0, 0)),
+                pl.BlockSpec((1, rows, PACK - TILE), lambda j, place: (j, 0, 0)),
+                tok_spec,
+                tok_spec,
+            ],
+        ),
         out_shape=[
             jax.ShapeDtypeStruct((units, rows, PACK), BF),
             jax.ShapeDtypeStruct((units, rows, PACK - TILE), BF),
@@ -126,12 +156,12 @@
             transcendentals=0,
         ),
         name="project",
-    )(toks, weight, bias, gain, offset, cos, sin)
-
-
-def unturn_kernel(*refs):
-    own_ref, cos_ref, sin_ref, out_ref = refs[0], refs[-3], refs[-2], refs[-1]
-    others = refs[1:-3]
+    )(place, *toks, weight, bias, gain, offset, cos, sin)
+
+
+def unturn_kernel(place_ref, own_ref, *refs):
+    w_ref, cos_ref, sin_ref, out_ref, one_ref, two_ref = refs[-6:]
+    others = refs[:-6]
     cos, sin = turn_tables(cos_ref[0], sin_ref[0])
     for t in range(5):
         tile = own_ref[0, :, t * TILE : (t + 1) * TILE].astype(F32)
@@ -141,22 +171,33 @@
         if t in (0, 1, 3):
             tile = turn(tile, cos, -sin)
         out_ref[0, :, t * TILE : (t + 1) * TILE] = tile.astype(BF)
-
-
-def unturn(own, others, cos, sin):
+    back = inner_back(out_ref[0], w_ref[...]).astype(BF)
+    rows = back.shape[0] // 2
+    one_ref[0] = back[:rows]
+    two_ref[0] = back[rows:]
+
+
+def unturn(place, own, others, weight, cos, sin):
     units, rows, unused = own.shape
-    turn_spec = pl.BlockSpec((1, ROT // 2, rows), lambda j: (j, 0, 0))
-    own_spec = pl.BlockSpec((1, rows, PACK), lambda j: (j, 0, 0))
-    other_spec = pl.BlockSpec((1, rows, PACK - TILE), lambda j: (j, 0, 0))
+    d = weight.shape[0]
+    turn_spec = pl.BlockSpec((1, ROT // 2, rows), lambda j, place: (j, 0, 0))
+    own_spec = pl.BlockSpec((1, rows, PACK), lambda j, place: (j, 0, 0))
+    other_spec = pl.BlockSpec((1, rows, PACK - TILE), lambda j, place: (j, 0, 0))
+    half = jax.ShapeDtypeStruct((units, rows // 2, d), BF)
     return pl.pallas_call(
         unturn_kernel,
-        grid=(units,),
-        in_specs=[own_spec] + [other_spec] * len(others) + [turn_spec, turn_spec],
-        out_specs=own_spec,
-        out_shape=jax.ShapeDtypeStruct(own.shape, BF),
+        grid_spec=pltpu.PrefetchScalarGridSpec(
+            num_scalar_prefetch=1,
+            grid=(units,),
+            in_specs=[own_spec]
+            + [other_spec] * len(others)
+            + [pl.BlockSpec((d, PACK), lambda j, place: (0, 0)), turn_spec, turn_spec],
+            out_specs=[own_spec] + half_specs(rows, d),
+        ),
+        out_shape=[jax.ShapeDtypeStruct(own.shape, BF), half, half],
         compiler_params=params_of("arbitrary"),
         name="unturn",
-    )(own, *others, cos, sin)
+    )(place, own, *others, weight, cos, sin)
 
 
 def flip(tile):
@@ -484,9 +525,9 @@
             tile = tile.astype(BF)
             local_ref[:, g * PACK + t * TILE : g * PACK + (t + 1) * TILE] = tile
             for s in range(groups):
-                early_ref[g * groups + s, :, t * TILE : (t + 1) * TILE] = tile
+                early_ref[s * trios + g, :, t * TILE : (t + 1) * TILE] = tile
         for s in range(groups):
-            early_ref[g * groups + s, :, PACK:] = vec_ref[s]
+            early_ref[s * trios + g, :, PACK:] = vec_ref[s]
 
 
 def pack_early(weight, vec, trios):
@@ -561,56 +602,43 @@
     )(x, cot, weights, weights, shift)
 
 
-def gradient_kernel(
-    trios, ups, per, norm_ref, pre_ref, hidden_ref, cot_ref, att_ref, cols_ref, out_ref
-):
+def gradient_kernel(ups, norm_ref, pre_ref, hidden_ref, cot_ref, out_ref):
     i = pl.program_id(0)
-    d = norm_ref.shape[1]
 
     @pl.when(i < ups)
     def _():
         out_ref[...] = outer_sum(norm_ref[...], pre_ref[...]).astype(BF)
 
-    @pl.when((i >= ups) & (i < 2 * ups))
+    @pl.when(i >= ups)
     def _():
         out_ref[...] = outer_sum(hidden_ref[...], cot_ref[...]).astype(BF)
 
-    @pl.when(i == 2 * ups)
-    def _():
-        width = d // trios
-        for g in range(trios):
-            part = outer_sum(att_ref[:, g * OPACK : (g + 1) * OPACK], cols_ref[...])
-            out_ref[g * width : (g + 1) * width] = part[:width].astype(BF)
-
-
-def gradients(normed, pre_grad, hidden, cot, attended, cols, trios):
+
+def gradients(normed, pre_grad, hidden, cot):
     rows, d = normed.shape
-    width = cols.shape[1]
-    per = d // width
+    width = d // 2
     ups = hidden.shape[1] // width
 
     def down(i):
         return jnp.clip(i - ups, 0, ups - 1)
 
     return pl.pallas_call(
-        functools.partial(gradient_kernel, trios, ups, per),
-        grid=(2 * ups + 1,),
+        functools.partial(gradient_kernel, ups),
+        grid=(2 * ups,),
         in_specs=[
             pl.BlockSpec((rows, d), lambda i: (0, 0)),
             pl.BlockSpec((rows, width), lambda i: (0, jnp.minimum(i, ups - 1))),
-            pl.BlockSpec((rows, d), lambda i: (0, down(i) // per)),
-            pl.BlockSpec((rows, width), lambda i: (0, down(i) % per)),
-            pl.BlockSpec(attended.shape, lambda i: (0, 0)),
-            pl.BlockSpec((rows, width), lambda i: (0, 0)),
+            pl.BlockSpec((rows, d), lambda i: (0, down(i) // 2)),
+            pl.BlockSpec((rows, width), lambda i: (0, down(i) % 2)),
         ],
         out_specs=pl.BlockSpec((d, width), lambda i: (0, i)),
-        out_shape=jax.ShapeDtypeStruct((d, (2 * ups + 1) * width), BF),
+        out_shape=jax.ShapeDtypeStruct((d, 2 * ups * width), BF),
         compiler_params=params_of("arbitrary"),
         cost_estimate=pl.CostEstimate(
-            flops=2 * rows * d * (2 * ups + 1) * width, bytes_accessed=0, transcendentals=0
+            flops=4 * rows * d * ups * width, bytes_accessed=0, transcendentals=0
         ),
         name="gradients",
-    )(normed, pre_grad, hidden, cot, attended, cols)
+    )(normed, pre_grad, hidden, cot)
 
 
 def trio_kernel(norm_ref, hat_ref, grad_ref, w_ref, vec_ref, late_ref, shift_ref, own, hat):
@@ -752,6 +780,50 @@
         n = lax.axis_size(axis)
         return lax.ppermute(value, axis, [(p, (p + i) % n) for p in range(n)])
 
+    def flip_unit(value, bit):
+        return lax.ppermute(value, "unit", [(u, u ^ bit) for u in range(units)])
+
+    def pick(value, index, axis):
+        return lax.dynamic_index_in_dim(value, index, axis, False)
+
+    bits = (unit // trios, unit // 2 % 2, unit % 2)
+
+    def exchange_small(value):
+        shape = value.shape
+        value = value.reshape((2, 2, 2) + shape[1:])
+        for axis, bit in enumerate((trios, 2, 1)):
+            keep = pick(value, bits[axis], axis)
+            value = jnp.stack([keep, flip_unit(pick(value, 1 - bits[axis], axis), bit)], axis)
+        for axis in range(3):
+            value = jnp.where(bits[axis] == 0, value, jnp.flip(value, axis))
+        return value.reshape(shape)
+
+    def spread_tokens(value):
+        keep = pick(value, bits[0], 0)
+        both = jnp.stack([keep, flip_unit(pick(value, 1 - bits[0], 0), trios)])
+        one, two = both[:, : rows // 2], both[:, rows // 2 :]
+        one = jnp.stack([one, flip_unit(one, 2)])
+        two = jnp.stack([two, flip_unit(two, 1)])
+        one = jnp.stack([one, flip_unit(one, 1)])
+        two = jnp.stack([two, flip_unit(two, 2)])
+        return one.reshape(units, rows // 2, d), two.reshape(units, rows // 2, d)
+
+    def add(a, b):
+        return (a.astype(F32) + b.astype(F32)).astype(BF)
+
+    def collect_tokens(one, two):
+        one = one.reshape(2, 2, 2, rows // 2, d)
+        two = two.reshape(2, 2, 2, rows // 2, d)
+        one = add(one[0], flip_unit(one[1], 1))
+        two = add(two[0], flip_unit(two[1], 2))
+        one = add(one[0], flip_unit(one[1], 2))
+        two = add(two[0], flip_unit(two[1], 1))
+        both = jnp.concatenate([one, two], 1)
+        other = flip_unit(both[1], trios)
+        return jnp.where(
+            bits[0] == 0, jnp.stack([both[0], other]), jnp.stack([other, both[0]])
+        )
+
     def natural_order(got, me):
         n = len(got)
         if n == 2:
@@ -811,9 +883,8 @@
         -1,
     )
     early, qkv_local = pack_early(qkv_weight, vec, trios)
-    toks = jnp.concatenate([jnp.concatenate([token_rows] * trios, 0), early], 1)
-    toks = exchange(toks)
-    early = toks[:, rows:]
+    early = exchange_small(early)
+    toks = spread_tokens(token_rows)
 
     seg_mine = early[:, :, PACK + 16 : PACK + 16 + seg_lanes].astype(jnp.int32)
     seg_mine = seg_mine.reshape(units, r * seg_lanes)
@@ -828,31 +899,29 @@
         vec_rows[i : i + 1] for i in range(6)
     )
     qkv_shift = pack_columns(vec_full[:, 6:9].reshape(1, 3 * d), trios).reshape(trios, PACK)
-    qkv_shift = lax.dynamic_slice_in_dim(qkv_shift, unit // groups, 1, 0)
+    qkv_shift = lax.dynamic_slice_in_dim(qkv_shift, unit % trios, 1, 0)
     up_shift = split_hidden(vec_full[:, 9 : 9 + blocks].reshape(1, ff), count, r)
 
     feed_blocks = output_feed_weight.reshape(blocks, r, d)
-    first_pack = jnp.concatenate([qkv_local, dense_weight], 1)
-    first = lax.all_gather(first_pack, ALL_AXES, axis=0, tiled=True)
     half = blocks // part
+    dense_cols = d // part
     up_local = split_hidden(fc1_weight, count, r)
     second_pack = jnp.stack(
         [
             jnp.concatenate(
                 [up_local[:, p * half * d : (p + 1) * half * d]]
-                + [feed_blocks[b] for b in range(p * half, (p + 1) * half)],
+                + [feed_blocks[b] for b in range(p * half, (p + 1) * half)]
+                + [dense_weight[:, p * dense_cols : (p + 1) * dense_cols]],
                 1,
             )
             for p in range(part)
         ]
     )
-    second_pack = swap_parts(second_pack).reshape(part * r, 2 * half * d)
-    second_pack, toks = lax.optimization_barrier((second_pack, toks))
+    second_pack = swap_parts(second_pack).reshape(part * r, -1)
     second = lax.all_gather(second_pack, ("seq", "unit"), axis=0, tiled=True)
-    qkv_full = first[:, : trios * PACK]
+    dense_full = gather_small(second[:, 2 * half * d :], "part").transpose(1, 0, 2)
     dense_pad = jnp.pad(
-        first[:, trios * PACK :].reshape(trios, d // trios, d),
-        ((0, 0), (0, OPACK - d // trios), (0, 0)),
+        dense_full.reshape(trios, d // trios, d), ((0, 0), (0, OPACK - d // trios), (0, 0))
     )
 
     block_start = (jnp.arange(units, dtype=jnp.int32) * part + c) * rows
@@ -863,8 +932,9 @@
     cos = jnp.cos(angles)
     sin = jnp.sin(angles)
 
+    place_unit = unit[None]
     packed, kv_own, normed_one, hat_one = project(
-        toks, trio_full, qkv_shift, gain_one, bias_one, cos, sin
+        place_unit, toks, trio_full, qkv_shift, gain_one, bias_one, cos, sin
     )
     kv = [kv_own] + [shift(kv_own, "part", i) for i in range(1, part)]
 
@@ -876,22 +946,20 @@
     xhat = centre * spread
     normed_two = (xhat * gain_two + bias_two).astype(BF)
     attended_grad = jnp.einsum(
-        "sld,gkd->gslk", cot.reshape(groups, rows, d), dense_pad, preferred_element_type=F32
+        "sld,gkd->sglk", cot.reshape(groups, rows, d), dense_pad, preferred_element_type=F32
     ).astype(BF)
-    attended_grad, meta = lax.optimization_barrier((attended_grad, meta))
     dout = exchange(attended_grad.reshape(units, rows, OPACK))
     out_low, out_t, lse = attend_forward(meta, packed, kv, seg_mine)
-    dout, out_low = lax.optimization_barrier((dout, out_low))
+    normed_two, out_low = lax.optimization_barrier((normed_two, out_low))
     attended = exchange(out_low)
 
-    normed_two, dout = lax.optimization_barrier((normed_two, dout))
     normed_all = all_parts(normed_two)
     cot_all = all_parts(cot)
     up_shift = lax.dynamic_slice_in_dim(up_shift, c * half * d, half * d, 1)
     hidden_low, pre_grad, up_shift_grad, second_branch, normed_two_grad = feed_forward(
         normed_all, cot_all, second, up_shift, half
     )
-    hidden_low, pre_grad, attended = lax.optimization_barrier((hidden_low, pre_grad, attended))
+    hidden_low, pre_grad, dout = lax.optimization_barrier((hidden_low, pre_grad, dout))
     second_branch = sum_parts(second_branch)
     normed_two_grad = sum_parts(normed_two_grad)
     up_shift_grad = lax.dynamic_update_slice_in_dim(
@@ -904,25 +972,22 @@
             gy - jnp.mean(gy, -1, keepdims=True) - xhat * jnp.mean(gy * xhat, -1, keepdims=True)
         )
 
-    attended = attended.reshape(trios, groups, rows, OPACK).transpose(1, 2, 0, 3)
-    attended = attended.reshape(all_rows, trios * OPACK)
-    dense_cols = d // part
-    cols = lax.dynamic_slice_in_dim(cot_all, c * dense_cols, dense_cols, 1)
-    cols = jnp.pad(cols, ((0, 0), (0, -dense_cols % TILE)))
-    mlp_grads = gradients(
-        normed_all, pre_grad, hidden_low, cot_all, all_parts(attended), cols, trios
-    )
+    mlp_grads = gradients(normed_all, pre_grad, hidden_low, cot_all)
     mlp_grads, dout = lax.optimization_barrier((mlp_grads, dout))
     mlp_sum = lax.psum_scatter(mlp_grads, ("seq", "unit"), scatter_dimension=0, tiled=True)
 
     own, others = attend_backward(meta, packed, dout, out_t, lse, kv, seg_mine)
     others = [shift(others[i - 1], "part", part - i) for i in range(1, part)]
-    qkv_grad = unturn(own, others, cos, sin)
-    back = exchange(qkv_grad)
+    own, attended = lax.optimization_barrier((own, attended))
+    qkv_grad, back_one, back_two = unturn(place_unit, own, others, trio_full, cos, sin)
+    back = collect_tokens(back_one, back_two)
 
     attended, second_branch, normed_two_grad, qkv_grad = lax.optimization_barrier(
         (attended, second_branch, normed_two_grad, qkv_grad)
     )
+    attended = attended.reshape(groups, trios, rows, OPACK).transpose(0, 2, 1, 3)
+    attended = attended.reshape(all_rows, trios * OPACK)
+    dense_grad = outer_sum(attended, cot).reshape(trios, OPACK, d)[:, : d // trios].reshape(d, d)
     branch_one = mm(attended, dense_pad.reshape(trios * OPACK, d)) + dense_shift
     output = (x + branch_one + second_branch + down_shift).astype(BF)
     in_two = norm_back(normed_two_grad, gain_two)
@@ -942,20 +1007,22 @@
         [vec_grads, up_shift_grad, jnp.zeros((d, TILE - 8 - blocks), F32)], 1
     )
     late, shift_grad = trio_gradient(normed_one, hat_one, qkv_grad, trio_full, vec_grads)
-    late = late.reshape(seqs, units, part, r, PACK + TILE)
-    shift_rows = jnp.pad(shift_grad.astype(BF), ((0, 7), (0, TILE)))
+    late = jnp.concatenate([late, dense_grad.astype(BF)], 1)
+    late = late.reshape(seqs, units, part, r, -1)
+    width = late.shape[-1]
+    shift_rows = jnp.pad(shift_grad.astype(BF), ((0, 7), (0, width - PACK)))
     late = jnp.concatenate(
         [late, jnp.broadcast_to(shift_rows, (seqs, units, part) + shift_rows.shape)], 3
     )
     late = scatter_small(late.transpose(2, 0, 1, 3, 4), "part")
-    late = scatter_small(late, "seq")
-    late, back, mlp_sum = lax.optimization_barrier((late, back, mlp_sum))
-    late = exchange(late).astype(F32)
-    late = jnp.sum(late.reshape(trios, groups, r + 8, PACK + TILE), 1)
+    late = exchange_small(scatter_small(late, "seq")).astype(F32)
+    late = jnp.sum(late.reshape(groups, trios, r + 8, width), 0)
     qkv_weight_grad = unpack_columns(
         late[:, :r, :PACK].transpose(1, 0, 2).reshape(r, trios * PACK), trios
     )
-    late_vec = jnp.sum(late[:, :r, PACK:], 0)
+    late_rest = jnp.sum(late[:, :r, PACK:], 0)
+    late_vec = late_rest[:, :TILE]
+    dense_sum = late_rest[:, TILE:]
     qkv_shift_grad = unpack_columns(late[:, r, :PACK].reshape(1, trios * PACK), trios)[0]
     qkv_shift_grad = lax.dynamic_slice_in_dim(qkv_shift_grad, place * 3 * r, 3 * r)
 
@@ -968,9 +1035,6 @@
             for b in range(half)
         ],
         0,
-    )
-    dense_sum = jnp.concatenate(
-        [mlp_sum[p, :, 2 * half * d : 2 * half * d + dense_cols] for p in range(part)], 1
     )
     param_grads = (
         late_vec[:, 0],
@@ -987,8 +1051,7 @@
         late_vec[:, 4],
     )
 
-    back = back.reshape(trios, groups, rows, PACK).transpose(1, 2, 0, 3)
-    normed_one_grad = inner_back(back.reshape(all_rows, trios * PACK), qkv_full)
+    normed_one_grad = back.reshape(all_rows, d).astype(F32)
     in_one = norm_back(normed_one_grad, gain_one)
     tokens_grad = (cot_float + in_one + in_two).astype(BF)
 

time: 522 us -> 509 us (0.975)
  waiting for transfers between devices: 185 us -> 168 us
  starting transfers between devices: 32.1 us -> 46.3 us
    ppermute x0 -> x16, waiting for transfers between devices: none -> 133 us  [flip_unit(): return lax.ppermute(value, 'unit', [(u, u ^ bit) for u in range(units)])]
    all_to_all x5 -> x2, waiting for transfers between devices: 96.7 us -> 16.1 us  [exchange(): lax.all_to_all(blocks_out.reshape(-1, width), 'unit', 0, 0, tiled=True)]
    all_gather x1, waiting for transfers between devices: 34.3 us -> 1.64 us  [on_device(): second = lax.all_gather(second_pack, ('seq', 'unit'), axis=0, tiled=True)]
    reduce_scatter x1, waiting for transfers between devices: 26.2 us -> 0.01 us  [on_device(): lax.psum_scatter(mlp_grads, ('seq', 'unit'), scatter_dimension=0, tiled=T...]
    ppermute x0 -> x16, starting transfers between devices: none -> 23.7 us  [flip_unit(): return lax.ppermute(value, 'unit', [(u, u ^ bit) for u in range(units)])]
    all_to_all x5 -> x2, starting transfers between devices: 24.7 us -> 12.2 us  [exchange(): lax.all_to_all(blocks_out.reshape(-1, width), 'unit', 0, 0, tiled=True)]
    ppermute x13, waiting for transfers between devices: 27.4 us -> 17.2 us  [shift(): return lax.ppermute(value, axis, [(p, (p + i) % n) for p in range(n)])]
    another operation x0 -> x9, other arithmetic: none -> 7.49 us  [the longest x2 3.67 us: spread_tokens(): one = jnp.stack([one, flip_unit(one, 1)])]
  transfers between devices with their start and end apart: 21 -> 33, of which waited for: 11 -> 16; matrix products, arithmetic and copies ran while one was open for 17% -> 18% of each run, Pallas kernels for 28% -> 32%
where the time goes in v5:
time: 509 us; the launch traced here: 502 us
  waiting for transfers between devices  168 us (33%)
  Pallas kernels  163 us (32%)
  local copies, waits for them, and re-layouts  64 us (13%)
  starting transfers between devices  46.3 us (9%)
  other arithmetic  40.5 us (8%)
  between operations  15.6 us (3%)
    ppermute x16, waiting for transfers between devices, flip_unit(): return lax.ppermute(value, 'unit', [(u, u ^ bit) for u in range(units)])  133 us
    pallas_call x1, Pallas kernels, attend_backward(): pl.pallas_call(functools.partial(backward_kernel, part, units), grid_spec...  53.4 us
    pallas_call x1, Pallas kernels, attend_forward(): pl.pallas_call(functools.partial(forward_kernel, part, units), grid_spec=...  40.8 us
    ppermute x16, starting transfers between devices, flip_unit(): return lax.ppermute(value, 'unit', [(u, u ^ bit) for u in range(units)])  23.7 us
    pallas_call x1, Pallas kernels, feed_forward(): pl.pallas_call(feed_kernel, grid=(2 * blocks,), in_specs=[wide, wide, pl....  21.8 us
    ppermute x13, waiting for transfers between devices, shift(): return lax.ppermute(value, axis, [(p, (p + i) % n) for p in range(n)])  17.2 us
    all_to_all x2, waiting for transfers between devices, exchange(): lax.all_to_all(blocks_out.reshape(-1, width), 'unit', 0, 0, tiled=True)  16.1 us
    pallas_call x1, Pallas kernels, gradients(): pl.pallas_call(functools.partial(gradient_kernel, ups), grid=(2 * ups,),...  12.8 us
  transfers between devices with their start and end apart: 33, of which 16 were waited for; matrix products, arithmetic and copies ran while one was open for 18% of the time, Pallas kernels for 32%

profile of v5, /device:TPU:0, one launch (start us, length us, event | category | flops | bytes accessed | tf_op | source)
XLA Modules:
  0.0 502.3 jit_solution(4210046755808125063)
XLA Ops:
  8.1 2.1 reshape.411
  16.3 1.8 pack_early.1
  19.1 4.0 collective-permute-start
  23.4 20.6 %collective-permute-done = bf16[2,2,24,768]{3,2,1,0:T(8,128)(2,1)S(1)} collective-permute-done((bf16[2,2,24,768]{3,2,1,0:T(8,128)(2,1)S(1)}, bf16[2,2,24,768]{3,2,1,0:T(8,128)(2,1)S(1)}, u32[]{:S(2)}, u32[]{:S(2)}) %collective-permute-start) | collective-permute-done | bytes 147488 | tf_op jit(solution)/shard_map/ppermute | solution.py:784
  44.0 1.7 collective-permute-start.1
  45.7 11.1 %collective-permute-done.1 = bf16[2,2,24,768]{3,2,1,0:T(8,128)(2,1)S(1)} collective-permute-done((bf16[2,2,24,768]{3,2,1,0:T(8,128)(2,1)S(1)}, bf16[2,2,24,768]{3,2,1,0:T(8,128)(2,1)S(1)}, u32[]{:S(2)}, u32[]{:S(2)}) %collective-permute-start.1) | collective-permute-done | bytes 147488 | tf_op jit(solution)/shard_map/ppermute | solution.py:784
  56.8 1.6 collective-permute-start.2
  59.1 7.1 %collective-permute-done.2 = bf16[2,2,24,768]{3,2,1,0:T(8,128)(2,1)S(1)} collective-permute-done((bf16[2,2,24,768]{3,2,1,0:T(8,128)(2,1)S(1)}, bf16[2,2,24,768]{3,2,1,0:T(8,128)(2,1)S(1)}, u32[]{:S(2)}, u32[]{:S(2)}) %collective-permute-start.2) | collective-permute-done | bytes 147488 | tf_op jit(solution)/shard_map/ppermute | solution.py:784
  66.4 1.7 collective-permute-start.8
  68.3 8.7 %collective-permute-done.8 = bf16[8,24,768]{2,1,0:T(8,128)(2,1)S(1)} collective-permute-done((bf16[8,24,768]{2,1,0:T(8,128)(2,1)S(1)}, bf16[8,24,768]{2,1,0:T(8,128)(2,1)S(1)}, u32[]{:S(2)}, u32[]{:S(2)}) %collective-permute-start.8) | collective-permute-done | bytes 294944 | tf_op jit(solution)/shard_map/ppermute | solution.py:781
  79.2 1.4 collective-permute-start.7
  81.8 1.4 collective-permute-start.5
  89.0 1.9 slice_reduce_fusion.15
  90.9 1.7 copy.87.gain_ref
  94.8 18.8 %collective-permute-done.7 = bf16[2,2,128,768]{3,2,1,0:T(8,128)(2,1)} collective-permute-done((bf16[2,2,128,768]{3,2,1,0:T(8,128)(2,1)}, bf16[2,2,128,768]{3,2,1,0:T(8,128)(2,1)}, u32[]{:S(2)}, u32[]{:S(2)}) %collective-permute-start.7) | collective-permute-done | bytes 786464 | tf_op jit(solution)/shard_map/ppermute | solution.py:784
  113.6 2.6 pad_maximum_fusion.2
  116.2 2.4 pad_maximum_fusion.1
  118.6 11.3 %project.1 = (bf16[8,256,640]{2,1,0:T(8,128)(2,1)}, bf16[8,256,512]{2,1,0:T(8,128)(2,1)}, bf16[8,256,768]{2,1,0:T(8,128)(2,1)}, bf16[8,256,768]{2,1,0:T(8,128)(2,1)}) custom-call(s32[1]{0:T(128)} %bitcast.18.place_ref, bf16[8,128,768]{2,1,0:T(8,128)(2,1)} %bitcast.313, bf16[8,128,768]{2,1,0:T(8,128)(2,1)} %bitcast.312, bf16[768,768]{1,0:T(8,128)(2,1)} %bitcast.285, ...), custom_call_target="tpu_custom_call" | custom-call | flops 2013265920 | bytes 12058624 | tf_op jit(solution)/shard_map/project/pallas_call | solution.py:125
  131.2 1.6 all-gather.2.cloned.1.call-done.up_ref.down_ref
  137.6 2.2 copy.92
  139.8 3.1 reshape.414
  143.0 3.1 fusion.41
  146.1 2.3 copy.94
  148.3 7.8 %all-to-all-start = ((bf16[8,256,256]{2,1,0:T(8,128)(2,1)}), bf16[8,256,256]{2,1,0:T(8,128)(2,1)}, u32[]{:S(2)}, u32[]{:S(2)}) async-start(bf16[8,256,256]{2,1,0:T(8,128)(2,1)} %bitcast.292), calls=%async_computation | async-start | bytes 2097152 | tf_op jit(solution)/shard_map/all_to_all | solution.py:775
  156.2 40.8 %attend_forward.1 = (bf16[8,256,256]{2,1,0:T(8,128)(2,1)}, f32[8,192,256]{2,1,0:T(8,128)}, f32[8,8,256]{2,1,0:T(8,128)}) custom-call(s32[17]{0:T(128)} %pad_add_fusion.meta, bf16[8,256,640]{2,1,0:T(8,128)(2,1)} %get-tuple-element.48.q_ref, bf16[8,256,512]{2,1,0:T(8,128)(2,1)} %get-tuple-element.49.refs_0_, ...), custom_call_target="tpu_custom_call" | custom-call | flops 12884901888 | bytes 20000000 | tf_op jit(solution)/shard_map/attend_forward/pallas_call | solution.py:435
  197.0 1.6 collective-permute-start.11
  198.6 2.4 pad_maximum_fusion.3.cot_ref
  205.6 21.8 %feed_forward.1 = (bf16[1024,1536]{1,0:T(8,128)(2,1)}, bf16[1024,1536]{1,0:T(8,128)(2,1)}, f32[1,1536]{1,0:T(1,128)}, f32[1024,768]{1,0:T(8,128)}, f32[1024,768]{1,0:T(8,128)}) custom-call(bf16[1024,768]{1,0:T(8,128)(2,1)} %copy-done.21, bf16[1024,768]{1,0:T(8,128)(2,1)} %pad_maximum_fusion.3.cot_ref, ...), custom_call_target="tpu_custom_call" | custom-call | flops 9663676416 | bytes 4718592 | tf_op jit(solution)/shard_map/feed_forward/pallas_call | solution.py:579
  227.4 2.7 slice.276
  230.1 12.8 %gradients.1 = bf16[768,3072]{1,0:T(8,128)(2,1)} custom-call(bf16[1024,768]{1,0:T(8,128)(2,1)} %copy-done.21, bf16[1024,1536]{1,0:T(8,128)(2,1)} %get-tuple-element.54.pre_ref, bf16[1024,1536]{1,0:T(8,128)(2,1)} %get-tuple-element.55.hidden_ref, bf16[1024,768]{1,0:T(8,128)(2,1)} %pad_maximum_fusion.3.cot_ref), custom_call_target="tpu_custom_call" | custom-call | flops 4831838208 | tf_op jit(solution)/shard_map/gradients/pallas_call | solution.py:625
  242.9 53.4 %attend_backward.1 = (bf16[8,256,640]{2,1,0:T(8,128)(2,1)}, bf16[1,8,256,512]{3,2,1,0:T(8,128)(2,1)}) custom-call(s32[17]{0:T(128)} %pad_add_fusion.meta, bf16[8,256,640]{2,1,0:T(8,128)(2,1)} %get-tuple-element.48.q_ref, bf16[8,256,256]{2,1,0:T(8,128)(2,1)} %all-to-all-done.do_ref, f32[8,192,256]{2,1,0:T(8,128)} %get-tuple-element.58.ot_ref, ...), custom_call_target="tpu_custom_call" | custom-call | flops 32212254720 | bytes 20000000 | tf_op jit(solution)/shard_map/attend_backward/pallas_call | solution.py:475
  296.3 1.6 collective-permute-start.17
  299.1 4.4 all-to-all-start.1
  304.0 1.8 convert_reduce_fusion.1
  309.9 2.2 slice_add_fusion
  312.7 2.7 slice_add_fusion.1
  315.5 16.1 %all-to-all-done.1 = bf16[8,256,256]{2,1,0:T(8,128)(2,1)} async-done(((bf16[8,256,256]{2,1,0:T(8,128)(2,1)}), bf16[8,256,256]{2,1,0:T(8,128)(2,1)}, u32[]{:S(2)}, u32[]{:S(2)}) %all-to-all-start.1) | async-done | bytes 1048608 | tf_op jit(solution)/shard_map/all_to_all | solution.py:775
  331.6 9.8 %unturn.1 = (bf16[8,256,640]{2,1,0:T(8,128)(2,1)}, bf16[8,128,768]{2,1,0:T(8,128)(2,1)}, bf16[8,128,768]{2,1,0:T(8,128)(2,1)}) custom-call(s32[1]{0:T(128)} %bitcast.18.place_ref, bf16[8,256,640]{2,1,0:T(8,128)(2,1)} %get-tuple-element.65.own_ref, bf16[8,256,512]{2,1,0:T(8,128)(2,1)} %collective-permute-done.17.refs_0_, bf16[768,768]{1,0:T(8,128)(2,1)} %bitcast.286, ...), custom_call_target="tpu_custom_call" | custom-call | tf_op jit(solution)/shard_map/unturn/pallas_call | solution.py:187
  341.4 2.1 copy.95
  343.7 1.5 copy-done.19
  346.7 2.5 fusion.34
  350.1 1.5 copy.106
  354.2 11.2 %trio_gradient.1 = (bf16[768,768]{1,0:T(8,128)(2,1)}, f32[1,640]{1,0:T(1,128)}) custom-call(bf16[8,256,768]{2,1,0:T(8,128)(2,1)} %get-tuple-element.73.norm_ref, bf16[8,256,768]{2,1,0:T(8,128)(2,1)} %get-tuple-element.74.hat_ref, bf16[8,256,640]{2,1,0:T(8,128)(2,1)} %get-tuple-element.75.grad_ref, bf16[768,768]{1,0:T(8,128)(2,1)} %bitcast.287, ...), custom_call_target="tpu_custom_call" | custom-call | tf_op jit(solution)/shard_map/trio_gradient/pallas_call | solution.py:678
  368.8 1.3 fusion.2
  372.3 17.1 %collective-permute-done.18 = bf16[2,2,128,768]{3,2,1,0:T(8,128)(2,1)} collective-permute-done((bf16[2,2,128,768]{3,2,1,0:T(8,128)(2,1)}, bf16[2,2,128,768]{3,2,1,0:T(8,128)(2,1)}, u32[]{:S(2)}, u32[]{:S(2)}) %collective-permute-start.18) | collective-permute-done | bytes 786464 | tf_op jit(solution)/shard_map/ppermute | solution.py:784
  389.4 1.6 fusion.7
  391.1 2.9 collective-permute-start.19
  394.0 1.4 fusion.6
  395.6 1.9 fusion
  397.6 3.6 collective-permute-start.24
  401.2 1.5 collective-permute-done.19
  402.8 5.3 %collective-permute-done.21 = bf16[2,128,768]{2,1,0:T(8,128)(2,1)S(1)} collective-permute-done((bf16[2,128,768]{2,1,0:T(8,128)(2,1)S(1)}, bf16[2,128,768]{2,1,0:T(8,128)(2,1)S(1)}, u32[]{:S(2)}, u32[]{:S(2)}) %collective-permute-start.21) | collective-permute-done | bytes 393248 | tf_op jit(solution)/shard_map/ppermute | solution.py:784
  408.3 3.0 collective-permute-start.22
  411.3 7.5 %collective-permute-done.24 = bf16[8,32,1536]{2,1,0:T(8,128)(2,1)S(1)} collective-permute-done((bf16[8,32,1536]{2,1,0:T(8,128)(2,1)S(1)}, bf16[8,32,1536]{2,1,0:T(8,128)(2,1)S(1)}, u32[]{:S(2)}, u32[]{:S(2)}) %collective-permute-start.24) | collective-permute-done | bytes 786464 | tf_op jit(solution)/shard_map/ppermute | solution.py:781
  419.0 2.8 collective-permute-start.25
  421.9 1.7 copy.127
  423.6 26.1 %collective-permute-done.22 = bf16[256,768]{1,0:T(8,128)(2,1)S(1)} collective-permute-done((bf16[256,768]{1,0:T(8,128)(2,1)S(1)}, bf16[256,768]{1,0:T(8,128)(2,1)S(1)}, u32[]{:S(2)}, u32[]{:S(2)}) %collective-permute-start.22) | collective-permute-done | bytes 393248 | tf_op jit(solution)/shard_map/ppermute | solution.py:784
  450.4 7.3 %collective-permute-done.25 = bf16[2,2,32,1536]{3,2,1,0:T(8,128)(2,1)S(1)} collective-permute-done((bf16[2,2,32,1536]{3,2,1,0:T(8,128)(2,1)S(1)}, bf16[2,2,32,1536]{3,2,1,0:T(8,128)(2,1)S(1)}, u32[]{:S(2)}, u32[]{:S(2)}) %collective-permute-start.25) | collective-permute-done | bytes 393248 | tf_op jit(solution)/shard_map/ppermute | solution.py:784
  457.8 2.2 collective-permute-start.26
  460.1 12.7 %collective-permute-done.26 = bf16[2,2,32,1536]{3,2,1,0:T(8,128)(2,1)S(1)} collective-permute-done((bf16[2,2,32,1536]{3,2,1,0:T(8,128)(2,1)S(1)}, bf16[2,2,32,1536]{3,2,1,0:T(8,128)(2,1)S(1)}, u32[]{:S(2)}, u32[]{:S(2)}) %collective-permute-start.26) | collective-permute-done | bytes 393248 | tf_op jit(solution)/shard_map/ppermute | solution.py:784
  473.7 1.9 fusion.15
  475.6 1.7 copy.126
  477.3 5.4 %collective-permute-done.27 = bf16[2,2,32,1536]{3,2,1,0:T(8,128)(2,1)S(1)} collective-permute-done((bf16[2,2,32,1536]{3,2,1,0:T(8,128)(2,1)S(1)}, bf16[2,2,32,1536]{3,2,1,0:T(8,128)(2,1)S(1)}, u32[]{:S(2)}, u32[]{:S(2)}) %collective-permute-start.27) | collective-permute-done | bytes 393248 | tf_op jit(solution)/shard_map/ppermute | solution.py:784
  491.5 2.6 reshape.430
  (305 shorter events, 60.0 us)
Async XLA Ops:
  7.2 125.7 %all-gather.2.cloned.1.call-start = ((), (), s32[]{:S(2)}) async-start(), calls=%async_computation.3 | async-start | bytes 5640192 | tf_op jit(solution)/shard_map/all_gather | solution.py:921
  11.6 2.8 copy-start.36
  11.6 2.9 copy-start.39
  11.7 3.0 copy-start.40
  11.7 3.1 copy-start.41
  11.7 3.2 copy-start.42
  11.7 3.3 copy-start.43
  11.7 3.4 copy-start.44
  11.7 3.5 copy-start.45
  11.7 3.6 copy-start.46
  11.8 11.3 %copy-start = (bf16[256,2,768]{2,1,0:T(2,128)(2,1)S(1)}, bf16[256,2,768]{2,1,0:T(2,128)(2,1)}, u32[]{:S(2)}) copy-start(bf16[256,2,768]{2,1,0:T(2,128)(2,1)} %param.15) | copy-start | bytes 2359300
  12.0 1.5 collective-permute-start.13
  19.1 24.9 %collective-permute-start = (bf16[2,2,24,768]{3,2,1,0:T(8,128)(2,1)S(1)}, bf16[2,2,24,768]{3,2,1,0:T(8,128)(2,1)S(1)}, u32[]{:S(2)}, u32[]{:S(2)}) collective-permute-start(bf16[2,2,24,768]{3,2,1,0:T(8,128)(2,1)S(1)} %get-tuple-element.142), channel_id=1, source_target_pairs={{0,8},{2,10},{4,12},{6,14},{8,0},{10,2},{12,4},{14,6},{1,9},{3,11}... | collective-permute-start | bytes 442376 | tf_op jit(solution)/shard_map/ppermute | solution.py:784
  23.3 35.2 %collective-permute-start.3 = (bf16[256,768]{1,0:T(8,128)(2,1)S(1)}, bf16[256,768]{1,0:T(8,128)(2,1)S(1)}, u32[]{:S(2)}, u32[]{:S(2)}) collective-permute-start(bf16[256,768]{1,0:T(8,128)(2,1)S(1)} %get-tuple-element.124), channel_id=1, source_target_pairs={{0,8},{2,10},{4,12},{6,14},{8,0},{10,2},{12,4},{14,6},{1,9},{3,11}... | collective-permute-start | bytes 1179656 | tf_op jit(solution)/shard_map/ppermute | solution.py:784
  44.0 12.8 %collective-permute-start.1 = (bf16[2,2,24,768]{3,2,1,0:T(8,128)(2,1)S(1)}, bf16[2,2,24,768]{3,2,1,0:T(8,128)(2,1)S(1)}, u32[]{:S(2)}, u32[]{:S(2)}) collective-permute-start(bf16[2,2,24,768]{3,2,1,0:T(8,128)(2,1)S(1)} %get-tuple-element.140), channel_id=1, source_target_pairs={{0,4},{2,6},{4,0},{6,2},{8,12},{10,14},{12,8},{14,10},{1,5},{3,7},... | collective-permute-start | bytes 442376 | tf_op jit(solution)/shard_map/ppermute | solution.py:784
  56.8 9.4 %collective-permute-start.2 = (bf16[2,2,24,768]{3,2,1,0:T(8,128)(2,1)S(1)}, bf16[2,2,24,768]{3,2,1,0:T(8,128)(2,1)S(1)}, u32[]{:S(2)}, u32[]{:S(2)}) collective-permute-start(bf16[2,2,24,768]{3,2,1,0:T(8,128)(2,1)S(1)} %get-tuple-element.139), channel_id=1, source_target_pairs={{0,2},{2,0},{4,6},{6,4},{8,10},{10,8},{12,14},{14,12},{1,3},{3,1},... | collective-permute-start | bytes 442376 | tf_op jit(solution)/shard_map/ppermute | solution.py:784
  58.5 19.7 %collective-permute-start.6 = (bf16[2,128,768]{2,1,0:T(8,128)(2,1)S(1)}, bf16[2,128,768]{2,1,0:T(8,128)(2,1)S(1)}, u32[]{:S(2)}, u32[]{:S(2)}) collective-permute-start(bf16[2,128,768]{2,1,0:T(8,128)(2,1)S(1)} %get-tuple-element.120), channel_id=1, source_target_pairs={{0,2},{2,0},{4,6},{6,4},{8,10},{10,8},{12,14},{14,12},{1,3},{3,1},... | collective-permute-start | bytes 1179656 | tf_op jit(solution)/shard_map/ppermute | solution.py:784
  59.1 21.5 %collective-permute-start.4 = (bf16[2,128,768]{2,1,0:T(8,128)(2,1)S(1)}, bf16[2,128,768]{2,1,0:T(8,128)(2,1)S(1)}, u32[]{:S(2)}, u32[]{:S(2)}) collective-permute-start(bf16[2,128,768]{2,1,0:T(8,128)(2,1)S(1)} %get-tuple-element.121), channel_id=1, source_target_pairs={{0,4},{2,6},{4,0},{6,2},{8,12},{10,14},{12,8},{14,10},{1,5},{3,7},... | collective-permute-start | bytes 1179656 | tf_op jit(solution)/shard_map/ppermute | solution.py:784
  66.4 10.6 %collective-permute-start.8 = (bf16[8,24,768]{2,1,0:T(8,128)(2,1)S(1)}, bf16[8,24,768]{2,1,0:T(8,128)(2,1)S(1)}, u32[]{:S(2)}, u32[]{:S(2)}) collective-permute-start(bf16[8,24,768]{2,1,0:T(8,128)(2,1)S(1)} %bitcast.304), channel_id=1, source_target_pairs={{0,16},{16,0},{1,17},{17,1},{2,18},{18,2},{3,19},{19,3},{4,20},{20... | collective-permute-start | bytes 884744 | tf_op jit(solution)/shard_map/ppermute | solution.py:781
  77.1 6.2 %collective-permute-start.9 = (bf16[2,8,24,768]{3,2,1,0:T(8,128)(2,1)S(1)}, bf16[2,8,24,768]{3,2,1,0:T(8,128)(2,1)S(1)}, u32[]{:S(2)}, u32[]{:S(2)}) collective-permute-start(bf16[2,8,24,768]{3,2,1,0:T(8,128)(2,1)S(1)} %maximum_select_fusion.4), channel_id=1, source_target_pairs={{0,1},{1,0},{2,3},{3,2},{4,5},{5,4},{6,7},{7,6},{8,9},{9,8},{10,11... | collective-permute-start | bytes 1769480 | tf_op jit(solution)/shard_map/ppermute | solution.py:781
  79.2 34.3 %collective-permute-start.7 = (bf16[2,2,128,768]{3,2,1,0:T(8,128)(2,1)}, bf16[2,2,128,768]{3,2,1,0:T(8,128)(2,1)}, u32[]{:S(2)}, u32[]{:S(2)}) collective-permute-start(bf16[2,2,128,768]{3,2,1,0:T(8,128)(2,1)} %get-tuple-element.119), channel_id=1, source_target_pairs={{0,4},{2,6},{4,0},{6,2},{8,12},{10,14},{12,8},{14,10},{1,5},{3,7},... | collective-permute-start | bytes 2359304 | tf_op jit(solution)/shard_map/ppermute | solution.py:784
  81.8 34.3 %collective-permute-start.5 = (bf16[2,2,128,768]{3,2,1,0:T(8,128)(2,1)}, bf16[2,2,128,768]{3,2,1,0:T(8,128)(2,1)}, u32[]{:S(2)}, u32[]{:S(2)}) collective-permute-start(bf16[2,2,128,768]{3,2,1,0:T(8,128)(2,1)} %get-tuple-element.123), channel_id=1, source_target_pairs={{0,2},{2,0},{4,6},{6,4},{8,10},{10,8},{12,14},{14,12},{1,3},{3,1},... | collective-permute-start | bytes 2359304 | tf_op jit(solution)/shard_map/ppermute | solution.py:784
  83.5 7.4 %copy-start.3 = (bf16[2,8,2,24,768]{4,3,2,1,0:T(8,128)(2,1)}, bf16[2,8,2,24,768]{4,3,2,1,0:T(8,128)(2,1)S(1)}, u32[]{:S(2)}) copy-start(bf16[2,8,2,24,768]{4,3,2,1,0:T(8,128)(2,1)S(1)} %copy.86) | copy-start | bytes 3538948
  118.6 11.4 %copy-start.11 = (bf16[256,2,768]{2,1,0:T(2,128)(2,1)S(1)}, bf16[256,2,768]{2,1,0:T(2,128)(2,1)}, u32[]{:S(2)}) copy-start(bf16[256,2,768]{2,1,0:T(2,128)(2,1)} %param.29) | copy-start | bytes 2359300
  129.9 26.3 %collective-permute-start.10 = (bf16[8,256,512]{2,1,0:T(8,128)(2,1)}, bf16[8,256,512]{2,1,0:T(8,128)(2,1)}, u32[]{:S(2)}, u32[]{:S(2)}) collective-permute-start(bf16[8,256,512]{2,1,0:T(8,128)(2,1)} %get-tuple-element.49.refs_0_), channel_id=1, source_target_pairs={{0,1},{1,0},{2,3},{3,2},{4,5},{5,4},{6,7},{7,6},{8,9},{9,8},{10,11... | collective-permute-start | bytes 6291464 | tf_op jit(solution)/shard_map/ppermute | solution.py:781
  130.1 221.5 %copy-start.6 = (bf16[2,256,768]{2,1,0:T(8,128)(2,1)}, bf16[2,256,768]{2,1,0:T(8,128)(2,1)S(1)}, u32[]{:S(2)}) copy-start(bf16[2,256,768]{2,1,0:T(8,128)(2,1)S(1)} %copy.89) | copy-start | bytes 2359300
  130.1 6.0 %copy-start.29 = (f32[768]{0:T(1024)S(1)}, f32[768]{0:T(1024)}, u32[]{:S(2)}) copy-start(f32[768]{0:T(1024)} %get-tuple-element.89) | copy-start | bytes 9220
  130.1 68.4 %collective-permute-start.12 = (bf16[512,768]{1,0:T(8,128)(2,1)S(1)}, bf16[512,768]{1,0:T(8,128)(2,1)}, u32[]{:S(2)}, u32[]{:S(2)}) collective-permute-start(bf16[512,768]{1,0:T(8,128)(2,1)S(1)} %bitcast.288), channel_id=1, source_target_pairs={{0,1},{1,0},{2,3},{3,2},{4,5},{5,4},{6,7},{7,6},{8,9},{9,8},{10,11... | collective-permute-start | bytes 2359304 | tf_op jit(solution)/shard_map/ppermute | solution.py:781
  130.8 3.8 copy-start.27
  134.0 3.3 collective-permute-start.14
  134.7 2.8 copy-start.23
  134.7 2.8 copy-start.25
  148.3 81.7 %all-to-all-start = ((bf16[8,256,256]{2,1,0:T(8,128)(2,1)}), bf16[8,256,256]{2,1,0:T(8,128)(2,1)}, u32[]{:S(2)}, u32[]{:S(2)}) async-start(bf16[8,256,256]{2,1,0:T(8,128)(2,1)} %bitcast.292), calls=%async_computation | async-start | bytes 2097152 | tf_op jit(solution)/shard_map/all_to_all | solution.py:775
  197.0 6.2 %collective-permute-start.11 = (bf16[512,768]{1,0:T(8,128)(2,1)}, bf16[512,768]{1,0:T(8,128)(2,1)}, u32[]{:S(2)}, u32[]{:S(2)}) collective-permute-start(bf16[512,768]{1,0:T(8,128)(2,1)} %fusion.30), channel_id=1, source_target_pairs={{0,1},{1,0},{2,3},{3,2},{4,5},{5,4},{6,7},{7,6},{8,9},{9,8},{10,11... | collective-permute-start | bytes 2359304 | tf_op jit(solution)/shard_map/ppermute | solution.py:781
  230.0 79.8 %collective-permute-start.16 = (f32[512,768]{1,0:T(8,128)}, f32[512,768]{1,0:T(8,128)}, u32[]{:S(2)}, u32[]{:S(2)}) collective-permute-start(f32[512,768]{1,0:T(8,128)} %slice.276), channel_id=1, source_target_pairs={{0,1},{1,0},{2,3},{3,2},{4,5},{5,4},{6,7},{7,6},{8,9},{9,8},{10,11... | collective-permute-start | bytes 4718600 | tf_op jit(solution)/shard_map/ppermute | solution.py:781
  242.9 55.0 %copy-start.12 = (f32[1024,768]{1,0:T(8,128)S(1)}, f32[1024,768]{1,0:T(8,128)}, u32[]{:S(2)}) copy-start(f32[1024,768]{1,0:T(8,128)} %get-tuple-element.63) | copy-start | bytes 9437188
  296.3 35.4 %collective-permute-start.17 = (bf16[8,256,512]{2,1,0:T(8,128)(2,1)}, bf16[8,256,512]{2,1,0:T(8,128)(2,1)}, u32[]{:S(2)}, u32[]{:S(2)}) collective-permute-start(bf16[8,256,512]{2,1,0:T(8,128)(2,1)} %bitcast.356), channel_id=1, source_target_pairs={{0,1},{1,0},{2,3},{3,2},{4,5},{5,4},{6,7},{7,6},{8,9},{9,8},{10,11... | collective-permute-start | bytes 6291464 | tf_op jit(solution)/shard_map/ppermute | solution.py:781
  299.1 7.9 %copy-start.35 = (f32[1,1536]{1,0:T(1,128)S(1)}, f32[1,1536]{1,0:T(1,128)}, u32[]{:S(2)}) copy-start(f32[1,1536]{1,0:T(1,128)} %get-tuple-element.76) | copy-start | bytes 18436
  299.1 13.0 %collective-permute-start.15 = (f32[512,768]{1,0:T(8,128)}, f32[512,768]{1,0:T(8,128)}, u32[]{:S(2)}, u32[]{:S(2)}) collective-permute-start(f32[512,768]{1,0:T(8,128)} %slice.274), channel_id=1, source_target_pairs={{0,1},{1,0},{2,3},{3,2},{4,5},{5,4},{6,7},{7,6},{8,9},{9,8},{10,11... | collective-permute-start | bytes 4718600 | tf_op jit(solution)/shard_map/ppermute | solution.py:781
  299.1 32.5 %all-to-all-start.1 = ((bf16[8,256,256]{2,1,0:T(8,128)(2,1)}), bf16[8,256,256]{2,1,0:T(8,128)(2,1)}, u32[]{:S(2)}, u32[]{:S(2)}) async-start(bf16[8,256,256]{2,1,0:T(8,128)(2,1)} %get-tuple-element.61), calls=%async_computation.1 | async-start | bytes 2097152 | tf_op jit(solution)/shard_map/all_to_all | solution.py:775
  303.5 181.2 %reduce-scatter.2.cloned.1.call-start = ((), (), s32[]{:S(2)}) async-start(), calls=%async_computation.4 | async-start | bytes 5013504 | tf_op jit(solution)/shard_map/reduce_scatter | solution.py:977
  309.9 2.8 copy-start.13
  312.1 34.2 %copy-start.1 = (f32[512,768]{1,0:T(8,128)}, f32[512,768]{1,0:T(8,128)S(1)}, u32[]{:S(2)}) copy-start(f32[512,768]{1,0:T(8,128)S(1)} %slice_add_fusion) | copy-start | bytes 4718596
  354.2 11.9 %copy-start.18 = (bf16[8,128,768]{2,1,0:T(8,128)(2,1)S(1)}, bf16[8,128,768]{2,1,0:T(8,128)(2,1)}, u32[]{:S(2)}) copy-start(bf16[8,128,768]{2,1,0:T(8,128)(2,1)} %get-tuple-element.70) | copy-start | bytes 4718596
  367.4 22.0 %collective-permute-start.18 = (bf16[2,2,128,768]{3,2,1,0:T(8,128)(2,1)}, bf16[2,2,128,768]{3,2,1,0:T(8,128)(2,1)}, u32[]{:S(2)}, u32[]{:S(2)}) collective-permute-start(bf16[2,2,128,768]{3,2,1,0:T(8,128)(2,1)} %bitcast.66), channel_id=1, source_target_pairs={{0,2},{2,0},{4,6},{6,4},{8,10},{10,8},{12,14},{14,12},{1,3},{3,1},... | collective-permute-start | bytes 2359304 | tf_op jit(solution)/shard_map/ppermute | solution.py:784
  370.2 25.3 %collective-permute-start.23 = (bf16[2,8,32,1536]{3,2,1,0:T(8,128)(2,1)}, bf16[2,8,32,1536]{3,2,1,0:T(8,128)(2,1)}, u32[]{:S(2)}, u32[]{:S(2)}) collective-permute-start(bf16[2,8,32,1536]{3,2,1,0:T(8,128)(2,1)} %fusion.2), channel_id=1, source_target_pairs={{0,1},{1,0},{2,3},{3,2},{4,5},{5,4},{6,7},{7,6},{8,9},{9,8},{10,11... | collective-permute-start | bytes 4718600 | tf_op jit(solution)/shard_map/ppermute | solution.py:781
  372.3 21.7 %collective-permute-start.20 = (bf16[2,2,128,768]{3,2,1,0:T(8,128)(2,1)}, bf16[2,2,128,768]{3,2,1,0:T(8,128)(2,1)}, u32[]{:S(2)}, u32[]{:S(2)}) collective-permute-start(bf16[2,2,128,768]{3,2,1,0:T(8,128)(2,1)} %bitcast.70), channel_id=1, source_target_pairs={{0,4},{2,6},{4,0},{6,2},{8,12},{10,14},{12,8},{14,10},{1,5},{3,7},... | collective-permute-start | bytes 2359304 | tf_op jit(solution)/shard_map/ppermute | solution.py:784
  389.4 4.6 copy-start.14
  391.1 11.6 %collective-permute-start.19 = (bf16[2,128,768]{2,1,0:T(8,128)(2,1)S(1)}, bf16[2,128,768]{2,1,0:T(8,128)(2,1)S(1)}, u32[]{:S(2)}, u32[]{:S(2)}) collective-permute-start(bf16[2,128,768]{2,1,0:T(8,128)(2,1)S(1)} %slice_bitcast_fusion.2), channel_id=1, source_target_pairs={{0,4},{2,6},{4,0},{6,2},{8,12},{10,14},{12,8},{14,10},{1,5},{3,7},... | collective-permute-start | bytes 1179656 | tf_op jit(solution)/shard_map/ppermute | solution.py:784
  395.5 12.6 %collective-permute-start.21 = (bf16[2,128,768]{2,1,0:T(8,128)(2,1)S(1)}, bf16[2,128,768]{2,1,0:T(8,128)(2,1)S(1)}, u32[]{:S(2)}, u32[]{:S(2)}) collective-permute-start(bf16[2,128,768]{2,1,0:T(8,128)(2,1)S(1)} %slice_bitcast_fusion), channel_id=1, source_target_pairs={{0,2},{2,0},{4,6},{6,4},{8,10},{10,8},{12,14},{14,12},{1,3},{3,1},... | collective-permute-start | bytes 1179656 | tf_op jit(solution)/shard_map/ppermute | solution.py:784
  397.5 3.6 copy-start.34
  397.6 21.1 %collective-permute-start.24 = (bf16[8,32,1536]{2,1,0:T(8,128)(2,1)S(1)}, bf16[8,32,1536]{2,1,0:T(8,128)(2,1)S(1)}, u32[]{:S(2)}, u32[]{:S(2)}) collective-permute-start(bf16[8,32,1536]{2,1,0:T(8,128)(2,1)S(1)} %dynamic-slice_bitcast_fusion), channel_id=1, source_target_pairs={{0,16},{16,0},{1,17},{17,1},{2,18},{18,2},{3,19},{19,3},{4,20},{20... | collective-permute-start | bytes 2359304 | tf_op jit(solution)/shard_map/ppermute | solution.py:781
  408.3 13.6 %copy-start.33 = (f32[512]{0:T(512)S(1)}, f32[512]{0:T(512)}, u32[]{:S(2)}) copy-start(f32[512]{0:T(512)} %get-tuple-element.82) | copy-start | bytes 6148
  408.3 13.6 %copy-start.16 = (bf16[512,768]{1,0:T(8,128)(2,1)S(1)}, bf16[512,768]{1,0:T(8,128)(2,1)}, u32[]{:S(2)}) copy-start(bf16[512,768]{1,0:T(8,128)(2,1)} %get-tuple-element.117) | copy-start | bytes 2359300
  408.3 41.4 %collective-permute-start.22 = (bf16[256,768]{1,0:T(8,128)(2,1)S(1)}, bf16[256,768]{1,0:T(8,128)(2,1)S(1)}, u32[]{:S(2)}, u32[]{:S(2)}) collective-permute-start(bf16[256,768]{1,0:T(8,128)(2,1)S(1)} %get-tuple-element.115), channel_id=1, source_target_pairs={{0,8},{2,10},{4,12},{6,14},{8,0},{10,2},{12,4},{14,6},{1,9},{3,11}... | collective-permute-start | bytes 1179656 | tf_op jit(solution)/shard_map/ppermute | solution.py:784
  419.0 30.8 %copy-start.28 = (f32[2,256]{1,0:T(2,128)S(1)}, f32[2,256]{1,0:T(2,128)}, u32[]{:S(2)}) copy-start(f32[2,256]{1,0:T(2,128)} %copy-done.27) | copy-start | bytes 6148
  419.0 30.7 %copy-start.32 = (f32[2,256]{1,0:T(2,128)S(1)}, f32[2,256]{1,0:T(2,128)}, u32[]{:S(2)}) copy-start(f32[2,256]{1,0:T(2,128)} %get-tuple-element.166) | copy-start | bytes 6148
  419.0 38.7 %collective-permute-start.25 = (bf16[2,2,32,1536]{3,2,1,0:T(8,128)(2,1)S(1)}, bf16[2,2,32,1536]{3,2,1,0:T(8,128)(2,1)S(1)}, u32[]{:S(2)}, u32[]{:S(2)}) collective-permute-start(bf16[2,2,32,1536]{3,2,1,0:T(8,128)(2,1)S(1)} %get-tuple-element.113), channel_id=1, source_target_pairs={{0,8},{2,10},{4,12},{6,14},{8,0},{10,2},{12,4},{14,6},{1,9},{3,11}... | collective-permute-start | bytes 1179656 | tf_op jit(solution)/shard_map/ppermute | solution.py:784
  457.7 15.9 %copy-start.2 = (f32[512,768]{1,0:T(8,128)S(1)}, f32[512,768]{1,0:T(8,128)}, u32[]{:S(2)}) copy-start(f32[512,768]{1,0:T(8,128)} %copy-done.1) | copy-start | bytes 4718596
  457.7 15.9 %copy-start.7 = (bf16[2,256,768]{2,1,0:T(8,128)(2,1)S(1)}, bf16[2,256,768]{2,1,0:T(8,128)(2,1)}, u32[]{:S(2)}) copy-start(bf16[2,256,768]{2,1,0:T(8,128)(2,1)} %copy-done.6) | copy-start | bytes 2359300
  457.8 14.9 %collective-permute-start.26 = (bf16[2,2,32,1536]{3,2,1,0:T(8,128)(2,1)S(1)}, bf16[2,2,32,1536]{3,2,1,0:T(8,128)(2,1)S(1)}, u32[]{:S(2)}, u32[]{:S(2)}) collective-permute-start(bf16[2,2,32,1536]{3,2,1,0:T(8,128)(2,1)S(1)} %get-tuple-element.111), channel_id=1, source_target_pairs={{0,4},{2,6},{4,0},{6,2},{8,12},{10,14},{12,8},{14,10},{1,5},{3,7},... | collective-permute-start | bytes 1179656 | tf_op jit(solution)/shard_map/ppermute | solution.py:784
  472.8 9.9 %collective-permute-start.27 = (bf16[2,2,32,1536]{3,2,1,0:T(8,128)(2,1)S(1)}, bf16[2,2,32,1536]{3,2,1,0:T(8,128)(2,1)S(1)}, u32[]{:S(2)}, u32[]{:S(2)}) collective-permute-start(bf16[2,2,32,1536]{3,2,1,0:T(8,128)(2,1)S(1)} %get-tuple-element.110), channel_id=1, source_target_pairs={{0,2},{2,0},{4,6},{6,4},{8,10},{10,8},{12,14},{14,12},{1,3},{3,1},... | collective-permute-start | bytes 1179656 | tf_op jit(solution)/shard_map/ppermute | solution.py:784
  485.7 3.1 collective-permute-start.28
  486.6 8.2 %copy-start.38 = (f32[24]{0:T(128)}, f32[24]{0:T(128)S(1)}, u32[]{:S(2)}) copy-start(f32[24]{0:T(128)S(1)} %get-tuple-element.201) | copy-start | bytes 292
  (17 other events, 29.0 us)
Sparse Core Ops, SparseCore 0:
  14.5 118.2 all-gather.1
  315.6 154.9 reduce-scatter.1

commit v6 on v5

--- a/solution.py
+++ b/solution.py
@@ -196,6 +196,7 @@
         ),
         out_shape=[jax.ShapeDtypeStruct(own.shape, BF), half, half],
         compiler_params=params_of("arbitrary"),
+        cost_estimate=pl.CostEstimate(flops=0, bytes_accessed=0, transcendentals=0),
         name="unturn",
     )(place, own, *others, weight, cos, sin)
 
@@ -415,13 +416,6 @@
                         own_ref[unit, :, (t + 1) * TILE : (t + 2) * TILE] = tile
                     else:
                         oth_ref[i - 1, unit, :, t * TILE : (t + 1) * TILE] = tile
-
-
-def attention_cost(products, units, rows, part):
-    pairs = TRIO * rows * rows * units * units * part // 2
-    return pl.CostEstimate(
-        flops=2 * 64 * products * pairs, bytes_accessed=20_000_000, transcendentals=pairs
-    )
 
 
 def whole_spec(shape):
@@ -462,7 +456,7 @@
             jax.ShapeDtypeStruct((units, 8, rows), F32),
         ],
         compiler_params=params_of("arbitrary"),
-        cost_estimate=attention_cost(8, units, rows, part),
+        cost_estimate=pl.CostEstimate(flops=0, bytes_accessed=0, transcendentals=0),
         name="attend_forward",
     )(meta, packed, *kv, seg)
 
@@ -506,7 +500,7 @@
             jax.ShapeDtypeStruct(others, BF),
         ],
         compiler_params=params_of("arbitrary"),
-        cost_estimate=attention_cost(20, units, rows, part),
+        cost_estimate=pl.CostEstimate(flops=0, bytes_accessed=0, transcendentals=0),
         name="attend_backward",
     )(meta, packed, dout, out_t, lse, *kv, seg)
 
@@ -695,7 +689,9 @@
             jax.ShapeDtypeStruct((1, PACK), F32),
         ],
         compiler_params=params_of("arbitrary"),
-        cost_estimate=pl.CostEstimate(flops=0, bytes_accessed=0, transcendentals=0),
+        cost_estimate=pl.CostEstimate(
+            flops=12 * units * rows * d * PACK, bytes_accessed=0, transcendentals=0
+        ),
         name="trio_gradient",
     )(normed, hat, grad, weight, vec)
 
@@ -811,19 +807,6 @@
     def add(a, b):
         return (a.astype(F32) + b.astype(F32)).astype(BF)
 
-    def collect_tokens(one, two):
-        one = one.reshape(2, 2, 2, rows // 2, d)
-        two = two.reshape(2, 2, 2, rows // 2, d)
-        one = add(one[0], flip_unit(one[1], 1))
-        two = add(two[0], flip_unit(two[1], 2))
-        one = add(one[0], flip_unit(one[1], 2))
-        two = add(two[0], flip_unit(two[1], 1))
-        both = jnp.concatenate([one, two], 1)
-        other = flip_unit(both[1], trios)
-        return jnp.where(
-            bits[0] == 0, jnp.stack([both[0], other]), jnp.stack([other, both[0]])
-        )
-
     def natural_order(got, me):
         n = len(got)
         if n == 2:
@@ -846,12 +829,11 @@
     def all_parts(value):
         return jnp.concatenate([value] + [shift(value, "part", i) for i in range(1, part)], 0)
 
-    def sum_parts(value):
+    def part_pieces(value):
         n = value.shape[0] // part
-        total = value[:n]
-        for i in range(1, part):
-            total = total + shift(value[i * n : (i + 1) * n], "part", part - i)
-        return total
+        return [value[:n]] + [
+            shift(value[i * n : (i + 1) * n], "part", part - i) for i in range(1, part)
+        ]
 
     def scatter_small(value, axis):
         n = lax.axis_size(axis)
@@ -904,14 +886,13 @@
 
     feed_blocks = output_feed_weight.reshape(blocks, r, d)
     half = blocks // part
-    dense_cols = d // part
     up_local = split_hidden(fc1_weight, count, r)
     second_pack = jnp.stack(
         [
             jnp.concatenate(
                 [up_local[:, p * half * d : (p + 1) * half * d]]
                 + [feed_blocks[b] for b in range(p * half, (p + 1) * half)]
-                + [dense_weight[:, p * dense_cols : (p + 1) * dense_cols]],
+                + [dense_weight],
                 1,
             )
             for p in range(part)
@@ -919,9 +900,9 @@
     )
     second_pack = swap_parts(second_pack).reshape(part * r, -1)
     second = lax.all_gather(second_pack, ("seq", "unit"), axis=0, tiled=True)
-    dense_full = gather_small(second[:, 2 * half * d :], "part").transpose(1, 0, 2)
     dense_pad = jnp.pad(
-        dense_full.reshape(trios, d // trios, d), ((0, 0), (0, OPACK - d // trios), (0, 0))
+        second[:, 2 * half * d :].reshape(trios, d // trios, d),
+        ((0, 0), (0, OPACK - d // trios), (0, 0)),
     )
 
     block_start = (jnp.arange(units, dtype=jnp.int32) * part + c) * rows
@@ -940,7 +921,6 @@
 
     x = token_rows.reshape(all_rows, d).astype(F32)
     cot = cotangent.transpose(1, 0, 2).reshape(all_rows, d)
-    cot_float = cot.astype(F32)
     centre = x - jnp.mean(x, -1, keepdims=True)
     spread = lax.rsqrt(jnp.mean(centre * centre, -1, keepdims=True) + EPSILON)
     xhat = centre * spread
@@ -949,10 +929,6 @@
         "sld,gkd->sglk", cot.reshape(groups, rows, d), dense_pad, preferred_element_type=F32
     ).astype(BF)
     dout = exchange(attended_grad.reshape(units, rows, OPACK))
-    out_low, out_t, lse = attend_forward(meta, packed, kv, seg_mine)
-    normed_two, out_low = lax.optimization_barrier((normed_two, out_low))
-    attended = exchange(out_low)
-
     normed_all = all_parts(normed_two)
     cot_all = all_parts(cot)
     up_shift = lax.dynamic_slice_in_dim(up_shift, c * half * d, half * d, 1)
@@ -960,12 +936,8 @@
         normed_all, cot_all, second, up_shift, half
     )
     hidden_low, pre_grad, dout = lax.optimization_barrier((hidden_low, pre_grad, dout))
-    second_branch = sum_parts(second_branch)
-    normed_two_grad = sum_parts(normed_two_grad)
-    up_shift_grad = lax.dynamic_update_slice_in_dim(
-        jnp.zeros((1, ff), F32), up_shift_grad, c * half * d, 1
-    )
-
+    second_branch = part_pieces(second_branch)
+    normed_two_grad = part_pieces(normed_two_grad)
     def norm_back(grad, gain):
         gy = grad * gain
         return spread * (
@@ -973,18 +945,31 @@
         )
 
     mlp_grads = gradients(normed_all, pre_grad, hidden_low, cot_all)
-    mlp_grads, dout = lax.optimization_barrier((mlp_grads, dout))
+    mlp_grads, meta = lax.optimization_barrier((mlp_grads, meta))
     mlp_sum = lax.psum_scatter(mlp_grads, ("seq", "unit"), scatter_dimension=0, tiled=True)
+
+    out_low, out_t, lse = attend_forward(meta, packed, kv, seg_mine)
+    attended = exchange(out_low)
 
     own, others = attend_backward(meta, packed, dout, out_t, lse, kv, seg_mine)
     others = [shift(others[i - 1], "part", part - i) for i in range(1, part)]
     own, attended = lax.optimization_barrier((own, attended))
     qkv_grad, back_one, back_two = unturn(place_unit, own, others, trio_full, cos, sin)
-    back = collect_tokens(back_one, back_two)
-
-    attended, second_branch, normed_two_grad, qkv_grad = lax.optimization_barrier(
-        (attended, second_branch, normed_two_grad, qkv_grad)
-    )
+    back_one = back_one.reshape(2, 2, 2, rows // 2, d)
+    back_two = back_two.reshape(2, 2, 2, rows // 2, d)
+    swapped = flip_unit(back_one[1], 1), flip_unit(back_two[1], 2)
+
+    attended, second_branch, normed_two_grad, qkv_grad, cot, up_shift_grad = (
+        lax.optimization_barrier(
+            (attended, second_branch, normed_two_grad, qkv_grad, cot, up_shift_grad)
+        )
+    )
+    cot_float = cot.astype(F32)
+    up_shift_grad = lax.dynamic_update_slice_in_dim(
+        jnp.zeros((1, ff), F32), up_shift_grad, c * half * d, 1
+    )
+    second_branch = sum(second_branch)
+    normed_two_grad = sum(normed_two_grad)
     attended = attended.reshape(groups, trios, rows, OPACK).transpose(0, 2, 1, 3)
     attended = attended.reshape(all_rows, trios * OPACK)
     dense_grad = outer_sum(attended, cot).reshape(trios, OPACK, d)[:, : d // trios].reshape(d, d)
@@ -1008,6 +993,10 @@
     )
     late, shift_grad = trio_gradient(normed_one, hat_one, qkv_grad, trio_full, vec_grads)
     late = jnp.concatenate([late, dense_grad.astype(BF)], 1)
+    swapped, late = lax.optimization_barrier((swapped, late))
+    back_one = add(back_one[0], swapped[0])
+    back_two = add(back_two[0], swapped[1])
+    swapped = flip_unit(back_one[1], 2), flip_unit(back_two[1], 1)
     late = late.reshape(seqs, units, part, r, -1)
     width = late.shape[-1]
     shift_rows = jnp.pad(shift_grad.astype(BF), ((0, 7), (0, width - PACK)))
@@ -1015,7 +1004,17 @@
         [late, jnp.broadcast_to(shift_rows, (seqs, units, part) + shift_rows.shape)], 3
     )
     late = scatter_small(late.transpose(2, 0, 1, 3, 4), "part")
-    late = exchange_small(scatter_small(late, "seq")).astype(F32)
+    swapped, late = lax.optimization_barrier((swapped, late))
+    both = jnp.concatenate(
+        [add(back_one[0], swapped[0]), add(back_two[0], swapped[1])], 1
+    )
+    swapped = flip_unit(both[1], trios)
+    late = scatter_small(late, "seq")
+    swapped, late, mlp_sum = lax.optimization_barrier((swapped, late, mlp_sum))
+    back = jnp.where(
+        bits[0] == 0, jnp.stack([both[0], swapped]), jnp.stack([swapped, both[0]])
+    )
+    late = exchange_small(late).astype(F32)
     late = jnp.sum(late.reshape(groups, trios, r + 8, width), 0)
     qkv_weight_grad = unpack_columns(
         late[:, :r, :PACK].transpose(1, 0, 2).reshape(r, trios * PACK), trios

time: 509 us -> 498 us (0.978)
  Pallas kernels: 163 us -> 145 us
  starting transfers between devices: 46.3 us -> 52.7 us
    ppermute x16, waiting for transfers between devices: 133 us -> 92.9 us  [flip_unit(): return lax.ppermute(value, 'unit', [(u, u ^ bit) for u in range(units)])]
    all_to_all x2, starting transfers between devices: 12.2 us -> 30.1 us  [exchange(): lax.all_to_all(blocks_out.reshape(-1, width), 'unit', 0, 0, tiled=True)]
    all_gather x1, waiting for transfers between devices: 1.64 us -> 17.7 us  [on_device(): second = lax.all_gather(second_pack, ('seq', 'unit'), axis=0, tiled=True)]
    all_to_all x2, waiting for transfers between devices: 16.1 us -> 29.8 us  [exchange(): lax.all_to_all(blocks_out.reshape(-1, width), 'unit', 0, 0, tiled=True)]
    pallas_call x1, Pallas kernels: 53.4 us -> 43.4 us  [attend_backward(): pl.pallas_call(functools.partial(backward_kernel, part, units), grid_spec...]
    ppermute x13 -> x12, waiting for transfers between devices: 17.2 us -> 26.3 us  [shift(): return lax.ppermute(value, axis, [(p, (p + i) % n) for p in range(n)])]
    pallas_call x1, Pallas kernels: 40.8 us -> 33.2 us  [attend_forward(): pl.pallas_call(functools.partial(forward_kernel, part, units), grid_spec=...]
    ppermute x16, starting transfers between devices: 23.7 us -> 17.3 us  [flip_unit(): return lax.ppermute(value, 'unit', [(u, u ^ bit) for u in range(units)])]
  transfers between devices with their start and end apart: 33 -> 32, of which waited for: 16 -> 17; matrix products, arithmetic and copies ran while one was open for 18% -> 18% of each run, Pallas kernels for 32% -> 30%
where the time goes in v6:
time: 498 us; the launch traced here: 488 us
  waiting for transfers between devices  167 us (34%)
  Pallas kernels  145 us (29%)
  local copies, waits for them, and re-layouts  61.2 us (12%)
  starting transfers between devices  52.7 us (11%)
  other arithmetic  42.4 us (9%)
  between operations  15.8 us (3%)
    ppermute x16, waiting for transfers between devices, flip_unit(): return lax.ppermute(value, 'unit', [(u, u ^ bit) for u in range(units)])  92.9 us
    pallas_call x1, Pallas kernels, attend_backward(): pl.pallas_call(functools.partial(backward_kernel, part, units), grid_spec...  43.4 us
    pallas_call x1, Pallas kernels, attend_forward(): pl.pallas_call(functools.partial(forward_kernel, part, units), grid_spec=...  33.2 us
    all_to_all x2, starting transfers between devices, exchange(): lax.all_to_all(blocks_out.reshape(-1, width), 'unit', 0, 0, tiled=True)  30.1 us
    all_to_all x2, waiting for transfers between devices, exchange(): lax.all_to_all(blocks_out.reshape(-1, width), 'unit', 0, 0, tiled=True)  29.8 us
    ppermute x12, waiting for transfers between devices, shift(): return lax.ppermute(value, axis, [(p, (p + i) % n) for p in range(n)])  26.3 us
    pallas_call x1, Pallas kernels, feed_forward(): pl.pallas_call(feed_kernel, grid=(2 * blocks,), in_specs=[wide, wide, pl....  21.9 us
    all_gather x1, waiting for transfers between devices, on_device(): second = lax.all_gather(second_pack, ('seq', 'unit'), axis=0, tiled=True)  17.7 us
  transfers between devices with their start and end apart: 32, of which 17 were waited for; matrix products, arithmetic and copies ran while one was open for 18% of the time, Pallas kernels for 30%

profile of v6, /device:TPU:0, one launch (start us, length us, event | category | flops | bytes accessed | tf_op | source)
XLA Modules:
  0.0 488.4 jit_solution(3966558425988677435)
XLA Ops:
  8.1 2.1 reshape.403
  16.3 1.8 pack_early.1
  18.0 1.7 dynamic-slice_bitcast_fusion.5
  19.7 4.0 collective-permute-start
  25.3 19.6 %collective-permute-done = bf16[2,2,24,768]{3,2,1,0:T(8,128)(2,1)S(1)} collective-permute-done((bf16[2,2,24,768]{3,2,1,0:T(8,128)(2,1)}, bf16[2,2,24,768]{3,2,1,0:T(8,128)(2,1)S(1)}, u32[]{:S(2)}, u32[]{:S(2)}) %collective-permute-start) | collective-permute-done | bytes 147488 | tf_op jit(solution)/shard_map/ppermute | solution.py:780
  45.0 1.6 collective-permute-start.1
  47.2 10.9 %collective-permute-done.1 = bf16[2,2,24,768]{3,2,1,0:T(8,128)(2,1)S(1)} collective-permute-done((bf16[2,2,24,768]{3,2,1,0:T(8,128)(2,1)S(1)}, bf16[2,2,24,768]{3,2,1,0:T(8,128)(2,1)S(1)}, u32[]{:S(2)}, u32[]{:S(2)}) %collective-permute-start.1) | collective-permute-done | bytes 147488 | tf_op jit(solution)/shard_map/ppermute | solution.py:780
  58.1 1.6 collective-permute-start.2
  61.4 5.4 %collective-permute-done.2 = bf16[2,2,24,768]{3,2,1,0:T(8,128)(2,1)} collective-permute-done((bf16[2,2,24,768]{3,2,1,0:T(8,128)(2,1)S(1)}, bf16[2,2,24,768]{3,2,1,0:T(8,128)(2,1)}, u32[]{:S(2)}, u32[]{:S(2)}) %collective-permute-start.2) | collective-permute-done | bytes 147488 | tf_op jit(solution)/shard_map/ppermute | solution.py:780
  68.0 1.8 collective-permute-start.3
  70.7 8.9 %collective-permute-done.3 = bf16[8,24,768]{2,1,0:T(8,128)(2,1)S(1)} collective-permute-done((bf16[8,24,768]{2,1,0:T(8,128)(2,1)S(1)}, bf16[8,24,768]{2,1,0:T(8,128)(2,1)S(1)}, u32[]{:S(2)}, u32[]{:S(2)}) %collective-permute-start.3) | collective-permute-done | bytes 294944 | tf_op jit(solution)/shard_map/ppermute | solution.py:777
  80.8 2.3 fusion.84
  86.0 1.4 collective-permute-start.10
  88.8 1.9 reshape.411
  90.7 1.3 slice_reduce_fusion.12
  92.9 1.3 reshape.412
  94.2 2.3 fusion.91
  96.6 1.8 copy.92.bias_ref
  98.4 1.7 copy.91.gain_ref
  100.1 1.9 fusion.29
  102.8 16.3 %collective-permute-done.12 = bf16[2,2,128,768]{3,2,1,0:T(8,128)(2,1)} collective-permute-done((bf16[2,2,128,768]{3,2,1,0:T(8,128)(2,1)}, bf16[2,2,128,768]{3,2,1,0:T(8,128)(2,1)}, u32[]{:S(2)}, u32[]{:S(2)}) %collective-permute-start.12) | collective-permute-done | bytes 786464 | tf_op jit(solution)/shard_map/ppermute | solution.py:780
  119.1 2.5 pad_maximum_fusion.4
  121.6 2.4 pad_maximum_fusion.3
  124.1 17.7 %all-gather.2.cloned.1.call-done.up_ref.down_ref = bf16[768,3840]{1,0:T(8,128)(2,1)} async-done(((bf16[48,3840]{1,0:T(8,128)(2,1)}), bf16[768,3840]{1,0:T(8,128)(2,1)}) %all-gather.2.cloned.1.call-update) | async-done | bytes 5898256 | tf_op jit(solution)/shard_map/all_gather | solution.py:902
  141.7 1.4 slice.317
  146.6 3.9 all-to-all-start
  150.7 11.1 %project.1 = (bf16[8,256,640]{2,1,0:T(8,128)(2,1)}, bf16[8,256,512]{2,1,0:T(8,128)(2,1)}, bf16[8,256,768]{2,1,0:T(8,128)(2,1)}, bf16[8,256,768]{2,1,0:T(8,128)(2,1)}) custom-call(s32[1]{0:T(128)} %bitcast.42.place_ref, bf16[8,128,768]{2,1,0:T(8,128)(2,1)} %bitcast.304, bf16[8,128,768]{2,1,0:T(8,128)(2,1)} %bitcast.303, bf16[768,768]{1,0:T(8,128)(2,1)} %bitcast.280, ...), custom_call_target="tpu_custom_call" | custom-call | flops 2013265920 | bytes 12058624 | tf_op jit(solution)/shard_map/project/pallas_call | solution.py:125
  162.7 2.4 pad_maximum_fusion.2.cot_ref
  166.1 2.6 pad_maximum_fusion.1.x_ref.norm_ref
  168.8 21.9 %feed_forward.1 = (bf16[1024,1536]{1,0:T(8,128)(2,1)}, bf16[1024,1536]{1,0:T(8,128)(2,1)}, f32[1,1536]{1,0:T(1,128)}, f32[1024,768]{1,0:T(8,128)}, f32[1024,768]{1,0:T(8,128)}) custom-call(bf16[1024,768]{1,0:T(8,128)(2,1)} %pad_maximum_fusion.1.x_ref.norm_ref, bf16[1024,768]{1,0:T(8,128)(2,1)} %pad_maximum_fusion.2.cot_ref, ...), custom_call_target="tpu_custom_call" | custom-call | flops 9663676416 | bytes 4718592 | tf_op jit(solution)/shard_map/feed_forward/pallas_call | solution.py:573
  190.7 13.2 %gradients.1 = bf16[768,3072]{1,0:T(8,128)(2,1)} custom-call(bf16[1024,768]{1,0:T(8,128)(2,1)} %pad_maximum_fusion.1.x_ref.norm_ref, bf16[1024,1536]{1,0:T(8,128)(2,1)} %get-tuple-element.61.pre_ref, bf16[1024,1536]{1,0:T(8,128)(2,1)} %get-tuple-element.62.hidden_ref, bf16[1024,768]{1,0:T(8,128)(2,1)} %pad_maximum_fusion.2.cot_ref), custom_call_target="tpu_custom_call" | custom-call | flops 4831838208 | tf_op jit(solution)/shard_map/gradients/pallas_call | solution.py:619
  203.9 33.2 %attend_forward.1 = (bf16[8,256,256]{2,1,0:T(8,128)(2,1)}, f32[8,192,256]{2,1,0:T(8,128)}, f32[8,8,256]{2,1,0:T(8,128)}) custom-call(s32[17]{0:T(128)} %pad_add_fusion.meta, bf16[8,256,640]{2,1,0:T(8,128)(2,1)} %get-tuple-element.64.q_ref, bf16[8,256,512]{2,1,0:T(8,128)(2,1)} %get-tuple-element.66.refs_0_, ...), custom_call_target="tpu_custom_call" | custom-call | tf_op jit(solution)/shard_map/attend_forward/pallas_call | solution.py:429
  237.1 43.4 %attend_backward.1 = (bf16[8,256,640]{2,1,0:T(8,128)(2,1)}, bf16[1,8,256,512]{3,2,1,0:T(8,128)(2,1)}) custom-call(s32[17]{0:T(128)} %pad_add_fusion.meta, bf16[8,256,640]{2,1,0:T(8,128)(2,1)} %get-tuple-element.64.q_ref, bf16[8,256,256]{2,1,0:T(8,128)(2,1)} %copy-done.12, f32[8,192,256]{2,1,0:T(8,128)} %get-tuple-element.67.ot_ref, ...), custom_call_target="tpu_custom_call" | custom-call | tf_op jit(solution)/shard_map/attend_backward/pallas_call | solution.py:469
  280.5 1.4 fusion.87
  282.4 26.2 %all-to-all-start.1 = ((bf16[8,256,256]{2,1,0:T(8,128)(2,1)}), bf16[8,256,256]{2,1,0:T(8,128)(2,1)}, u32[]{:S(2)}, u32[]{:S(2)}) async-start(bf16[8,256,256]{2,1,0:T(8,128)(2,1)} %get-tuple-element.70), calls=%async_computation.1 | async-start | bytes 2097152 | tf_op jit(solution)/shard_map/all_to_all | solution.py:771
  308.6 3.9 fusion.86
  314.1 29.8 %all-to-all-done.1 = bf16[8,256,256]{2,1,0:T(8,128)(2,1)} async-done(((bf16[8,256,256]{2,1,0:T(8,128)(2,1)}), bf16[8,256,256]{2,1,0:T(8,128)(2,1)}, u32[]{:S(2)}, u32[]{:S(2)}) %all-to-all-start.1) | async-done | bytes 1048608 | tf_op jit(solution)/shard_map/all_to_all | solution.py:771
  343.9 9.7 %unturn.1 = (bf16[8,256,640]{2,1,0:T(8,128)(2,1)}, bf16[8,128,768]{2,1,0:T(8,128)(2,1)}, bf16[8,128,768]{2,1,0:T(8,128)(2,1)}) custom-call(s32[1]{0:T(128)} %bitcast.42.place_ref, bf16[8,256,640]{2,1,0:T(8,128)(2,1)} %get-tuple-element.74.own_ref, bf16[8,256,512]{2,1,0:T(8,128)(2,1)} %collective-permute-done.16.refs_0_, bf16[768,768]{1,0:T(8,128)(2,1)} %bitcast.281, ...), custom_call_target="tpu_custom_call" | custom-call | tf_op jit(solution)/shard_map/unturn/pallas_call | solution.py:187
  353.6 2.1 copy.93
  355.9 1.6 copy-done.18
  358.9 4.4 fusion.30
  365.2 3.6 fusion.88
  368.8 1.5 collective-permute-start.17
  371.2 11.1 %trio_gradient.1 = (bf16[768,768]{1,0:T(8,128)(2,1)}, f32[1,640]{1,0:T(1,128)}) custom-call(bf16[8,256,768]{2,1,0:T(8,128)(2,1)} %get-tuple-element.84.norm_ref, bf16[8,256,768]{2,1,0:T(8,128)(2,1)} %get-tuple-element.85.hat_ref, bf16[8,256,640]{2,1,0:T(8,128)(2,1)} %get-tuple-element.86.grad_ref, bf16[768,768]{1,0:T(8,128)(2,1)} %bitcast.282, ...), custom_call_target="tpu_custom_call" | custom-call | flops 12079595520 | tf_op jit(solution)/shard_map/trio_gradient/pallas_call | solution.py:672
  382.9 1.6 copy.104
  384.5 2.2 fusion.46
  388.4 1.4 fusion.4
  389.8 2.9 copy.125
  392.7 1.4 fusion.9
  394.1 2.0 collective-permute-start.19
  396.1 1.4 fusion.8
  397.6 1.5 collective-permute-start.20
  399.1 1.9 fusion
  401.0 4.9 collective-permute-done.19
  405.9 3.0 collective-permute-done.20
  408.9 1.7 collective-permute-start.23
  411.6 16.3 %collective-permute-done.23 = bf16[8,32,1536]{2,1,0:T(8,128)(2,1)S(1)} collective-permute-done((bf16[8,32,1536]{2,1,0:T(8,128)(2,1)S(1)}, bf16[8,32,1536]{2,1,0:T(8,128)(2,1)S(1)}, u32[]{:S(2)}, u32[]{:S(2)}) %collective-permute-start.23) | collective-permute-done | bytes 786464 | tf_op jit(solution)/shard_map/ppermute | solution.py:777
  428.1 2.4 collective-permute-done.22
  432.3 1.9 fusion.2
  434.2 1.7 copy.124
  435.9 15.3 %collective-permute-done.24 = bf16[2,2,32,1536]{3,2,1,0:T(8,128)(2,1)S(1)} collective-permute-done((bf16[2,2,32,1536]{3,2,1,0:T(8,128)(2,1)S(1)}, bf16[2,2,32,1536]{3,2,1,0:T(8,128)(2,1)S(1)}, u32[]{:S(2)}, u32[]{:S(2)}) %collective-permute-start.24) | collective-permute-done | bytes 393248 | tf_op jit(solution)/shard_map/ppermute | solution.py:780
  453.2 10.2 %collective-permute-done.25 = bf16[2,2,32,1536]{3,2,1,0:T(8,128)(2,1)S(1)} collective-permute-done((bf16[2,2,32,1536]{3,2,1,0:T(8,128)(2,1)}, bf16[2,2,32,1536]{3,2,1,0:T(8,128)(2,1)S(1)}, u32[]{:S(2)}, u32[]{:S(2)}) %collective-permute-start.25) | collective-permute-done | bytes 393248 | tf_op jit(solution)/shard_map/ppermute | solution.py:780
  467.8 2.6 reshape.430
  471.1 4.3 collective-permute-done.26
  (295 shorter events, 49.2 us)
Async XLA Ops:
  7.2 134.6 %all-gather.2.cloned.1.call-start = ((), (), s32[]{:S(2)}) async-start(), calls=%async_computation.3 | async-start | bytes 6266880 | tf_op jit(solution)/shard_map/all_gather | solution.py:902
  11.6 2.8 copy-start.37
  11.6 2.9 copy-start.38
  11.7 3.0 copy-start.39
  11.7 3.0 copy-start.40
  11.7 3.1 copy-start.41
  11.7 3.2 copy-start.42
  11.7 3.3 copy-start.43
  11.7 3.4 copy-start.44
  11.7 3.5 copy-start.35
  11.8 11.8 %copy-start = (bf16[256,2,768]{2,1,0:T(2,128)(2,1)S(1)}, bf16[256,2,768]{2,1,0:T(2,128)(2,1)}, u32[]{:S(2)}) copy-start(bf16[256,2,768]{2,1,0:T(2,128)(2,1)} %param.15) | copy-start | bytes 2359300
  12.0 1.6 collective-permute-start.7
  19.7 4.9 copy-start.20
  19.7 25.3 %collective-permute-start = (bf16[2,2,24,768]{3,2,1,0:T(8,128)(2,1)}, bf16[2,2,24,768]{3,2,1,0:T(8,128)(2,1)S(1)}, u32[]{:S(2)}, u32[]{:S(2)}) collective-permute-start(bf16[2,2,24,768]{3,2,1,0:T(8,128)(2,1)} %get-tuple-element.172), channel_id=1, source_target_pairs={{0,8},{2,10},{4,12},{6,14},{8,0},{10,2},{12,4},{14,6},{1,9},{3,11}... | collective-permute-start | bytes 442376 | tf_op jit(solution)/shard_map/ppermute | solution.py:780
  24.6 36.3 %collective-permute-start.8 = (bf16[256,768]{1,0:T(8,128)(2,1)}, bf16[256,768]{1,0:T(8,128)(2,1)S(1)}, u32[]{:S(2)}, u32[]{:S(2)}) collective-permute-start(bf16[256,768]{1,0:T(8,128)(2,1)} %get-tuple-element.149), channel_id=1, source_target_pairs={{0,8},{2,10},{4,12},{6,14},{8,0},{10,2},{12,4},{14,6},{1,9},{3,11}... | collective-permute-start | bytes 1179656 | tf_op jit(solution)/shard_map/ppermute | solution.py:780
  24.7 359.8 %copy-start.1 = (bf16[2,256,768]{2,1,0:T(8,128)(2,1)}, bf16[2,256,768]{2,1,0:T(8,128)(2,1)S(1)}, u32[]{:S(2)}) copy-start(bf16[2,256,768]{2,1,0:T(8,128)(2,1)S(1)} %copy.84) | copy-start | bytes 2359300
  24.7 138.0 %collective-permute-start.6 = (bf16[512,768]{1,0:T(8,128)(2,1)S(1)}, bf16[512,768]{1,0:T(8,128)(2,1)}, u32[]{:S(2)}, u32[]{:S(2)}) collective-permute-start(bf16[512,768]{1,0:T(8,128)(2,1)S(1)} %bitcast.274), channel_id=1, source_target_pairs={{0,1},{1,0},{2,3},{3,2},{4,5},{5,4},{6,7},{7,6},{8,9},{9,8},{10,11... | collective-permute-start | bytes 2359304 | tf_op jit(solution)/shard_map/ppermute | solution.py:777
  25.0 20.0 %copy-start.27 = (f32[2,256]{1,0:T(2,128)}, f32[2,256]{1,0:T(2,128)S(1)}, u32[]{:S(2)}) copy-start(f32[2,256]{1,0:T(2,128)S(1)} %get-tuple-element.199) | copy-start | bytes 6148
  45.0 13.1 %collective-permute-start.1 = (bf16[2,2,24,768]{3,2,1,0:T(8,128)(2,1)S(1)}, bf16[2,2,24,768]{3,2,1,0:T(8,128)(2,1)S(1)}, u32[]{:S(2)}, u32[]{:S(2)}) collective-permute-start(bf16[2,2,24,768]{3,2,1,0:T(8,128)(2,1)S(1)} %get-tuple-element.170), channel_id=1, source_target_pairs={{0,4},{2,6},{4,0},{6,2},{8,12},{10,14},{12,8},{14,10},{1,5},{3,7},... | collective-permute-start | bytes 442376 | tf_op jit(solution)/shard_map/ppermute | solution.py:780
  58.1 8.7 %collective-permute-start.2 = (bf16[2,2,24,768]{3,2,1,0:T(8,128)(2,1)S(1)}, bf16[2,2,24,768]{3,2,1,0:T(8,128)(2,1)}, u32[]{:S(2)}, u32[]{:S(2)}) collective-permute-start(bf16[2,2,24,768]{3,2,1,0:T(8,128)(2,1)S(1)} %get-tuple-element.169), channel_id=1, source_target_pairs={{0,2},{2,0},{4,6},{6,4},{8,10},{10,8},{12,14},{14,12},{1,3},{3,1},... | collective-permute-start | bytes 442376 | tf_op jit(solution)/shard_map/ppermute | solution.py:780
  60.9 19.9 %collective-permute-start.11 = (bf16[2,128,768]{2,1,0:T(8,128)(2,1)S(1)}, bf16[2,128,768]{2,1,0:T(8,128)(2,1)}, u32[]{:S(2)}, u32[]{:S(2)}) collective-permute-start(bf16[2,128,768]{2,1,0:T(8,128)(2,1)S(1)} %get-tuple-element.145), channel_id=1, source_target_pairs={{0,2},{2,0},{4,6},{6,4},{8,10},{10,8},{12,14},{14,12},{1,3},{3,1},... | collective-permute-start | bytes 1179656 | tf_op jit(solution)/shard_map/ppermute | solution.py:780
  61.4 23.3 %collective-permute-start.9 = (bf16[2,128,768]{2,1,0:T(8,128)(2,1)S(1)}, bf16[2,128,768]{2,1,0:T(8,128)(2,1)S(1)}, u32[]{:S(2)}, u32[]{:S(2)}) collective-permute-start(bf16[2,128,768]{2,1,0:T(8,128)(2,1)S(1)} %get-tuple-element.146), channel_id=1, source_target_pairs={{0,4},{2,6},{4,0},{6,2},{8,12},{10,14},{12,8},{14,10},{1,5},{3,7},... | collective-permute-start | bytes 1179656 | tf_op jit(solution)/shard_map/ppermute | solution.py:780
  68.0 11.6 %collective-permute-start.3 = (bf16[8,24,768]{2,1,0:T(8,128)(2,1)S(1)}, bf16[8,24,768]{2,1,0:T(8,128)(2,1)S(1)}, u32[]{:S(2)}, u32[]{:S(2)}) collective-permute-start(bf16[8,24,768]{2,1,0:T(8,128)(2,1)S(1)} %bitcast.295), channel_id=1, source_target_pairs={{0,16},{16,0},{1,17},{17,1},{2,18},{18,2},{3,19},{19,3},{4,20},{20... | collective-permute-start | bytes 884744 | tf_op jit(solution)/shard_map/ppermute | solution.py:777
  79.7 7.7 %collective-permute-start.4 = (bf16[2,8,24,768]{3,2,1,0:T(8,128)(2,1)S(1)}, bf16[2,8,24,768]{3,2,1,0:T(8,128)(2,1)S(1)}, u32[]{:S(2)}, u32[]{:S(2)}) collective-permute-start(bf16[2,8,24,768]{3,2,1,0:T(8,128)(2,1)S(1)} %maximum_select_fusion.3), channel_id=1, source_target_pairs={{0,1},{1,0},{2,3},{3,2},{4,5},{5,4},{6,7},{7,6},{8,9},{9,8},{10,11... | collective-permute-start | bytes 1769480 | tf_op jit(solution)/shard_map/ppermute | solution.py:777
  83.1 36.0 %collective-permute-start.12 = (bf16[2,2,128,768]{3,2,1,0:T(8,128)(2,1)}, bf16[2,2,128,768]{3,2,1,0:T(8,128)(2,1)}, u32[]{:S(2)}, u32[]{:S(2)}) collective-permute-start(bf16[2,2,128,768]{3,2,1,0:T(8,128)(2,1)} %get-tuple-element.144), channel_id=1, source_target_pairs={{0,4},{2,6},{4,0},{6,2},{8,12},{10,14},{12,8},{14,10},{1,5},{3,7},... | collective-permute-start | bytes 2359304 | tf_op jit(solution)/shard_map/ppermute | solution.py:780
  86.0 35.7 %collective-permute-start.10 = (bf16[2,2,128,768]{3,2,1,0:T(8,128)(2,1)}, bf16[2,2,128,768]{3,2,1,0:T(8,128)(2,1)}, u32[]{:S(2)}, u32[]{:S(2)}) collective-permute-start(bf16[2,2,128,768]{3,2,1,0:T(8,128)(2,1)} %get-tuple-element.148), channel_id=1, source_target_pairs={{0,2},{2,0},{4,6},{6,4},{8,10},{10,8},{12,14},{14,12},{1,3},{3,1},... | collective-permute-start | bytes 2359304 | tf_op jit(solution)/shard_map/ppermute | solution.py:780
  87.7 8.8 %copy-start.7 = (bf16[2,8,2,24,768]{4,3,2,1,0:T(8,128)(2,1)}, bf16[2,8,2,24,768]{4,3,2,1,0:T(8,128)(2,1)S(1)}, u32[]{:S(2)}) copy-start(bf16[2,8,2,24,768]{4,3,2,1,0:T(8,128)(2,1)S(1)} %copy.83) | copy-start | bytes 3538948
  96.5 5.5 %slice-start = ((f32[1,4,192]{2,1,0:T(4,128)}), f32[1,4,64]{2,1,0:T(4,128)S(1)}, s32[]{:S(2)}) async-start(f32[1,4,192]{2,1,0:T(4,128)} %copy-done.31), calls=%async_computation.5 | async-start | bytes 4096 | tf_op jit(solution)/shard_map/slice | solution.py:706
  96.5 5.5 %slice-start.1 = ((f32[1,4,192]{2,1,0:T(4,128)}), f32[1,4,128]{2,1,0:T(4,128)S(1)}, s32[]{:S(2)}) async-start(f32[1,4,192]{2,1,0:T(4,128)} %copy-done.31), calls=%async_computation.6 | async-start | bytes 4096 | tf_op jit(solution)/shard_map/slice | solution.py:705
  96.5 5.5 %slice-start.2 = ((f32[1,4,192]{2,1,0:T(4,128)}), f32[1,4,64]{2,1,0:T(4,128)S(1)}, s32[]{:S(2)}) async-start(f32[1,4,192]{2,1,0:T(4,128)} %copy-done.32), calls=%async_computation.7 | async-start | bytes 4096 | tf_op jit(solution)/shard_map/slice | solution.py:705
  96.5 5.5 %slice-start.3 = ((f32[1,4,192]{2,1,0:T(4,128)}), f32[1,4,128]{2,1,0:T(4,128)S(1)}, s32[]{:S(2)}) async-start(f32[1,4,192]{2,1,0:T(4,128)} %copy-done.32), calls=%async_computation.8 | async-start | bytes 4096 | tf_op jit(solution)/shard_map/slice | solution.py:705
  96.5 5.5 %slice-start.4 = ((f32[1,4,192]{2,1,0:T(4,128)}), f32[1,4,64]{2,1,0:T(4,128)S(1)}, s32[]{:S(2)}) async-start(f32[1,4,192]{2,1,0:T(4,128)} %reshape.412), calls=%async_computation.9 | async-start | bytes 4096 | tf_op jit(solution)/shard_map/slice | solution.py:705
  96.6 5.5 %slice-start.5 = ((f32[1,4,192]{2,1,0:T(4,128)}), f32[1,4,128]{2,1,0:T(4,128)S(1)}, s32[]{:S(2)}) async-start(f32[1,4,192]{2,1,0:T(4,128)} %reshape.412), calls=%async_computation.10 | async-start | bytes 4096 | tf_op jit(solution)/shard_map/slice | solution.py:705
  96.6 22.5 %copy-start.16 = (bf16[1,2,2,128,768]{4,3,2,1,0:T(8,128)(2,1)S(1)}, bf16[1,2,2,128,768]{4,3,2,1,0:T(8,128)(2,1)}, u32[]{:S(2)}) copy-start(bf16[1,2,2,128,768]{4,3,2,1,0:T(8,128)(2,1)} %get-tuple-element.143) | copy-start | bytes 2359300
  102.0 64.1 %collective-permute-start.5 = (bf16[512,768]{1,0:T(8,128)(2,1)}, bf16[512,768]{1,0:T(8,128)(2,1)}, u32[]{:S(2)}, u32[]{:S(2)}) collective-permute-start(bf16[512,768]{1,0:T(8,128)(2,1)} %fusion.29), channel_id=1, source_target_pairs={{0,1},{1,0},{2,3},{3,2},{4,5},{5,4},{6,7},{7,6},{8,9},{9,8},{10,11... | collective-permute-start | bytes 2359304 | tf_op jit(solution)/shard_map/ppermute | solution.py:777
  146.6 44.1 %all-to-all-start = ((bf16[8,256,256]{2,1,0:T(8,128)(2,1)}), bf16[8,256,256]{2,1,0:T(8,128)(2,1)S(1)}, u32[]{:S(2)}, u32[]{:S(2)}) async-start(bf16[8,256,256]{2,1,0:T(8,128)(2,1)} %bitcast.40), calls=%async_computation | async-start | bytes 2097152 | tf_op jit(solution)/shard_map/all_to_all | solution.py:771
  150.5 280.0 %reduce-scatter.2.cloned.1.call-start = ((), (), s32[]{:S(2)}) async-start(), calls=%async_computation.4 | async-start | bytes 5013504 | tf_op jit(solution)/shard_map/reduce_scatter | solution.py:949
  161.8 42.1 %collective-permute-start.13 = (bf16[8,256,512]{2,1,0:T(8,128)(2,1)}, bf16[8,256,512]{2,1,0:T(8,128)(2,1)}, u32[]{:S(2)}, u32[]{:S(2)}) collective-permute-start(bf16[8,256,512]{2,1,0:T(8,128)(2,1)} %get-tuple-element.66.refs_0_), channel_id=1, source_target_pairs={{0,1},{1,0},{2,3},{3,2},{4,5},{5,4},{6,7},{7,6},{8,9},{9,8},{10,11... | collective-permute-start | bytes 6291464 | tf_op jit(solution)/shard_map/ppermute | solution.py:777
  190.7 13.2 %copy-start.12 = (bf16[8,256,256]{2,1,0:T(8,128)(2,1)}, bf16[8,256,256]{2,1,0:T(8,128)(2,1)S(1)}, u32[]{:S(2)}) copy-start(bf16[8,256,256]{2,1,0:T(8,128)(2,1)S(1)} %all-to-all-done.do_ref) | copy-start | bytes 3145732
  237.1 43.4 %copy-start.13 = (f32[1024,768]{1,0:T(8,128)S(1)}, f32[1024,768]{1,0:T(8,128)}, u32[]{:S(2)}) copy-start(f32[1024,768]{1,0:T(8,128)} %get-tuple-element.72) | copy-start | bytes 9437188
  280.5 63.4 %collective-permute-start.16 = (bf16[8,256,512]{2,1,0:T(8,128)(2,1)}, bf16[8,256,512]{2,1,0:T(8,128)(2,1)}, u32[]{:S(2)}, u32[]{:S(2)}) collective-permute-start(bf16[8,256,512]{2,1,0:T(8,128)(2,1)} %bitcast.346), channel_id=1, source_target_pairs={{0,1},{1,0},{2,3},{3,2},{4,5},{5,4},{6,7},{7,6},{8,9},{9,8},{10,11... | collective-permute-start | bytes 6291464 | tf_op jit(solution)/shard_map/ppermute | solution.py:777
  281.9 71.8 %collective-permute-start.14 = (f32[512,768]{1,0:T(8,128)}, f32[512,768]{1,0:T(8,128)}, u32[]{:S(2)}, u32[]{:S(2)}) collective-permute-start(f32[512,768]{1,0:T(8,128)} %get-tuple-element.128), channel_id=1, source_target_pairs={{0,1},{1,0},{2,3},{3,2},{4,5},{5,4},{6,7},{7,6},{8,9},{9,8},{10,11... | collective-permute-start | bytes 4718600 | tf_op jit(solution)/shard_map/ppermute | solution.py:777
  282.4 61.5 %all-to-all-start.1 = ((bf16[8,256,256]{2,1,0:T(8,128)(2,1)}), bf16[8,256,256]{2,1,0:T(8,128)(2,1)}, u32[]{:S(2)}, u32[]{:S(2)}) async-start(bf16[8,256,256]{2,1,0:T(8,128)(2,1)} %get-tuple-element.70), calls=%async_computation.1 | async-start | bytes 2097152 | tf_op jit(solution)/shard_map/all_to_all | solution.py:771
  308.6 4.2 copy-start.9
  312.5 41.1 %collective-permute-start.15 = (f32[512,768]{1,0:T(8,128)}, f32[512,768]{1,0:T(8,128)}, u32[]{:S(2)}, u32[]{:S(2)}) collective-permute-start(f32[512,768]{1,0:T(8,128)} %get-tuple-element.126), channel_id=1, source_target_pairs={{0,1},{1,0},{2,3},{3,2},{4,5},{5,4},{6,7},{7,6},{8,9},{9,8},{10,11... | collective-permute-start | bytes 4718600 | tf_op jit(solution)/shard_map/ppermute | solution.py:777
  358.9 4.5 copy-start.34
  368.8 19.5 %collective-permute-start.18 = (bf16[2,2,128,768]{3,2,1,0:T(8,128)(2,1)}, bf16[2,2,128,768]{3,2,1,0:T(8,128)(2,1)}, u32[]{:S(2)}, u32[]{:S(2)}) collective-permute-start(bf16[2,2,128,768]{3,2,1,0:T(8,128)(2,1)} %bitcast.65), channel_id=1, source_target_pairs={{0,4},{2,6},{4,0},{6,2},{8,12},{10,14},{12,8},{14,10},{1,5},{3,7},... | collective-permute-start | bytes 2359304 | tf_op jit(solution)/shard_map/ppermute | solution.py:780
  368.8 19.5 %collective-permute-start.17 = (bf16[2,2,128,768]{3,2,1,0:T(8,128)(2,1)}, bf16[2,2,128,768]{3,2,1,0:T(8,128)(2,1)}, u32[]{:S(2)}, u32[]{:S(2)}) collective-permute-start(bf16[2,2,128,768]{3,2,1,0:T(8,128)(2,1)} %bitcast.64), channel_id=1, source_target_pairs={{0,2},{2,0},{4,6},{6,4},{8,10},{10,8},{12,14},{14,12},{1,3},{3,1},... | collective-permute-start | bytes 2359304 | tf_op jit(solution)/shard_map/ppermute | solution.py:780
  371.1 11.8 %copy-start.11 = (bf16[64,8,4,256]{3,1,2,0:T(8,128)(2,1)S(1)}, bf16[64,8,4,256]{3,1,2,0:T(8,128)(2,1)}, u32[]{:S(2)}) copy-start(bf16[64,8,4,256]{3,1,2,0:T(8,128)(2,1)} %copy-done.10) | copy-start | bytes 3145732
  389.8 9.3 %collective-permute-start.21 = (bf16[2,8,32,1536]{3,2,1,0:T(8,128)(2,1)}, bf16[2,8,32,1536]{3,2,1,0:T(8,128)(2,1)}, u32[]{:S(2)}, u32[]{:S(2)}) collective-permute-start(bf16[2,8,32,1536]{3,2,1,0:T(8,128)(2,1)} %fusion.4), channel_id=1, source_target_pairs={{0,1},{1,0},{2,3},{3,2},{4,5},{5,4},{6,7},{7,6},{8,9},{9,8},{10,11... | collective-permute-start | bytes 4718600 | tf_op jit(solution)/shard_map/ppermute | solution.py:777
  389.8 2.9 copy-start.15
  392.7 3.4 copy-start.14
  394.1 11.8 %collective-permute-start.19 = (bf16[2,128,768]{2,1,0:T(8,128)(2,1)S(1)}, bf16[2,128,768]{2,1,0:T(8,128)(2,1)S(1)}, u32[]{:S(2)}, u32[]{:S(2)}) collective-permute-start(bf16[2,128,768]{2,1,0:T(8,128)(2,1)S(1)} %slice_bitcast_fusion.2), channel_id=1, source_target_pairs={{0,4},{2,6},{4,0},{6,2},{8,12},{10,14},{12,8},{14,10},{1,5},{3,7},... | collective-permute-start | bytes 1179656 | tf_op jit(solution)/shard_map/ppermute | solution.py:780
  396.1 3.0 copy-start.4
  397.6 11.3 %collective-permute-start.20 = (bf16[2,128,768]{2,1,0:T(8,128)(2,1)S(1)}, bf16[2,128,768]{2,1,0:T(8,128)(2,1)S(1)}, u32[]{:S(2)}, u32[]{:S(2)}) collective-permute-start(bf16[2,128,768]{2,1,0:T(8,128)(2,1)S(1)} %slice_bitcast_fusion.1), channel_id=1, source_target_pairs={{0,2},{2,0},{4,6},{6,4},{8,10},{10,8},{12,14},{14,12},{1,3},{3,1},... | collective-permute-start | bytes 1179656 | tf_op jit(solution)/shard_map/ppermute | solution.py:780
  408.9 18.9 %collective-permute-start.23 = (bf16[8,32,1536]{2,1,0:T(8,128)(2,1)S(1)}, bf16[8,32,1536]{2,1,0:T(8,128)(2,1)S(1)}, u32[]{:S(2)}, u32[]{:S(2)}) collective-permute-start(bf16[8,32,1536]{2,1,0:T(8,128)(2,1)S(1)} %dynamic-slice_bitcast_fusion), channel_id=1, source_target_pairs={{0,16},{16,0},{1,17},{17,1},{2,18},{18,2},{3,19},{19,3},{4,20},{20... | collective-permute-start | bytes 2359304 | tf_op jit(solution)/shard_map/ppermute | solution.py:777
  411.0 19.6 %copy-start.28 = (f32[2,256]{1,0:T(2,128)S(1)}, f32[2,256]{1,0:T(2,128)}, u32[]{:S(2)}) copy-start(f32[2,256]{1,0:T(2,128)} %copy-done.27) | copy-start | bytes 6148
  411.0 19.6 %copy-start.33 = (f32[2,256]{1,0:T(2,128)S(1)}, f32[2,256]{1,0:T(2,128)}, u32[]{:S(2)}) copy-start(f32[2,256]{1,0:T(2,128)} %get-tuple-element.196) | copy-start | bytes 6148
  411.0 19.5 %collective-permute-start.22 = (bf16[256,768]{1,0:T(8,128)(2,1)S(1)}, bf16[256,768]{1,0:T(8,128)(2,1)S(1)}, u32[]{:S(2)}, u32[]{:S(2)}) collective-permute-start(bf16[256,768]{1,0:T(8,128)(2,1)S(1)} %get-tuple-element.140), channel_id=1, source_target_pairs={{0,8},{2,10},{4,12},{6,14},{8,0},{10,2},{12,4},{14,6},{1,9},{3,11}... | collective-permute-start | bytes 1179656 | tf_op jit(solution)/shard_map/ppermute | solution.py:780
  431.5 4.4 collective-permute-start.27
  431.6 19.6 %collective-permute-start.24 = (bf16[2,2,32,1536]{3,2,1,0:T(8,128)(2,1)S(1)}, bf16[2,2,32,1536]{3,2,1,0:T(8,128)(2,1)S(1)}, u32[]{:S(2)}, u32[]{:S(2)}) collective-permute-start(bf16[2,2,32,1536]{3,2,1,0:T(8,128)(2,1)S(1)} %get-tuple-element.138), channel_id=1, source_target_pairs={{0,8},{2,10},{4,12},{6,14},{8,0},{10,2},{12,4},{14,6},{1,9},{3,11}... | collective-permute-start | bytes 1179656 | tf_op jit(solution)/shard_map/ppermute | solution.py:780
  452.0 11.3 %collective-permute-start.25 = (bf16[2,2,32,1536]{3,2,1,0:T(8,128)(2,1)}, bf16[2,2,32,1536]{3,2,1,0:T(8,128)(2,1)S(1)}, u32[]{:S(2)}, u32[]{:S(2)}) collective-permute-start(bf16[2,2,32,1536]{3,2,1,0:T(8,128)(2,1)} %get-tuple-element.136), channel_id=1, source_target_pairs={{0,4},{2,6},{4,0},{6,2},{8,12},{10,14},{12,8},{14,10},{1,5},{3,7},... | collective-permute-start | bytes 1179656 | tf_op jit(solution)/shard_map/ppermute | solution.py:780
  465.2 10.3 %collective-permute-start.26 = (bf16[2,2,32,1536]{3,2,1,0:T(8,128)(2,1)S(1)}, bf16[2,2,32,1536]{3,2,1,0:T(8,128)(2,1)S(1)}, u32[]{:S(2)}, u32[]{:S(2)}) collective-permute-start(bf16[2,2,32,1536]{3,2,1,0:T(8,128)(2,1)S(1)} %get-tuple-element.135), channel_id=1, source_target_pairs={{0,2},{2,0},{4,6},{6,4},{8,10},{10,8},{12,14},{14,12},{1,3},{3,1},... | collective-permute-start | bytes 1179656 | tf_op jit(solution)/shard_map/ppermute | solution.py:780
  477.0 4.1 copy-start.36
  (19 other events, 29.9 us)
Sparse Core Ops, SparseCore 0:
  14.5 127.1 all-gather.1
  204.0 155.9 reduce-scatter.1
